TPU v7x, 512 devices: a whole 4x8x8 slice. The times are simulated.
512 devices in a mesh: dst: 32 (over z, y_lo), src: 16 (over x, y_hi, core).
Axes of the slice: x: 4, y: 8 (y_hi: 2, y_lo: 4; y = y_hi * 4 + y_lo), z: 8, core: 2. Of those that a mesh axis runs over, the one named last changes fastest.
Arguments:
- node_features: bfloat16 [64, 196608], P(None, ('dst', 'src')), may hold values from -6 to 6
- edge_values: bfloat16 [32, 16, 8, 128, 128], P('dst', 'src'), may hold values from 0 to 2, as said below
- tile_rows: int32 [32, 16, 8], P('dst', 'src'), may hold values from 0 to 47, as said below
- tile_cols: int32 [32, 16, 8], P('dst', 'src'), may hold values from 0 to 95
- a_weight: bfloat16 [64, 64], replicated, may hold values from -0.75 to 0.75
- b_weight: bfloat16 [64, 64], replicated, may hold values from -1.5 to 1.5
- d_weight: bfloat16 [64, 64], replicated, may hold values from -0.75 to 0.75
- e_weight: bfloat16 [64, 64], replicated, may hold values from -0.75 to 0.75
- edge_gain: float32 [64], replicated, may hold values from -4 to 4
- ln_gain: float32 [64], replicated, may hold values from 0.1 to 1.9
Outputs:
- new_features: bfloat16 [64, 196608], P(None, ('dst', 'src'))
Inputs may be any that keep to these rules, and one draw needn't show every extreme that they name: Within one device the pairs (tile_rows, tile_cols) are all different. All tiles of one device whose tile_rows have the same value of tile_rows // 3 have the same tile_rows. Each device has a number of live tiles, from 8 / 2 (rounded down) up to 8, at least one device having 8; its slots past that number hold only zeros in edge_values. `edge_values`: live tiles have about one entry in 20 nonzero; nonzero entries lie between 0.5 and 2.
All inputs are finite; a program needn't handle non-finite values.
Results may differ from a plain program's by a relative error of at most 0.007.
Values may be sent and summed in bfloat16 or wider, within the bound.
No kernel may reach another device: no remote copies, remote signals or barrier semaphores. Data moves between devices by JAX's collectives and lax.ppermute only.
A program may use at most 64 MiB of HBM per device.

v0:
```python
import jax
import jax.numpy as jnp
from jax import lax
from jax.sharding import PartitionSpec as P


def tile_terms(row_gate, col_gate, col_value, values, edge_gain):
    values_f = values.astype(jnp.float32)
    preact = (
        row_gate.astype(jnp.float32)[:, :, None]
        + col_gate.astype(jnp.float32)[:, None, :]
        + edge_gain[:, None, None] * values_f[None]
    )
    gate_vals = jax.nn.sigmoid(preact) * (values != 0).astype(jnp.float32)[None]
    numerator = jnp.einsum("fij,fj->fi", gate_vals, col_value.astype(jnp.float32))
    denominator = jnp.sum(gate_vals, axis=2)
    return (numerator, denominator)


def finish(features, a_proj, numerator, denominator, ln_gain):
    mixed = a_proj + numerator / (denominator + 1e-06)
    center = mixed - jnp.mean(mixed, axis=0, keepdims=True)
    spread = jnp.mean(center * center, axis=0, keepdims=True)
    normed = center * lax.rsqrt(spread + 1e-05) * ln_gain[:, None]
    return (features.astype(jnp.float32) + jax.nn.relu(normed)).astype(jnp.bfloat16)


def project(weight, features):
    return jnp.dot(weight, features, preferred_element_type=jnp.float32).astype(jnp.bfloat16)


def local(
    node_features,
    edge_values,
    tile_rows,
    tile_cols,
    a_weight,
    b_weight,
    d_weight,
    e_weight,
    edge_gain,
    ln_gain,
):
    feat_width = node_features.shape[0]
    block_len = edge_values.shape[-1]
    d_proj = project(d_weight, node_features)
    row_panel = lax.all_gather(d_proj, "src", axis=1, tiled=True)
    b_proj = project(b_weight, node_features)
    e_proj = project(e_weight, node_features)
    b_panel, e_panel = (
        lax.all_gather(b_proj, "dst", axis=1, tiled=True),
        lax.all_gather(e_proj, "dst", axis=1, tiled=True),
    )
    panel_len = row_panel.shape[1]
    values_all = edge_values.reshape(-1, block_len, block_len)
    rows_flat = tile_rows.reshape(-1)
    row_starts = rows_flat * block_len
    col_starts = tile_cols.reshape(-1) * block_len
    zero_index = jnp.zeros((), jnp.int32)

    def tile_pair(values, row_start, col_start):
        row_gate = lax.dynamic_slice(row_panel, (zero_index, row_start), (feat_width, block_len))
        col_gate = lax.dynamic_slice(e_panel, (zero_index, col_start), (feat_width, block_len))
        col_value = lax.dynamic_slice(b_panel, (zero_index, col_start), (feat_width, block_len))
        return tile_terms(row_gate, col_gate, col_value, values, edge_gain)

    def add_tile(totals, tile_item):
        numerator, denominator = totals
        values, row_start, col_start = tile_item
        part_num, part_den = tile_pair(values, row_start, col_start)
        old_num = lax.dynamic_slice(numerator, (zero_index, row_start), (feat_width, block_len))
        old_den = lax.dynamic_slice(denominator, (zero_index, row_start), (feat_width, block_len))
        numerator = lax.dynamic_update_slice(numerator, old_num + part_num, (zero_index, row_start))
        denominator = lax.dynamic_update_slice(
            denominator, old_den + part_den, (zero_index, row_start)
        )
        return ((numerator, denominator), None)

    start_sums = (
        jnp.zeros((feat_width, panel_len), jnp.float32),
        jnp.zeros((feat_width, panel_len), jnp.float32),
    )
    (numerator, denominator), _ = lax.scan(
        add_tile, start_sums, (values_all, row_starts, col_starts)
    )
    numerator, denominator = (
        lax.psum_scatter(
            numerator.astype(jnp.bfloat16), "src", scatter_dimension=1, tiled=True
        ).astype(jnp.float32),
        lax.psum_scatter(
            denominator.astype(jnp.bfloat16), "src", scatter_dimension=1, tiled=True
        ).astype(jnp.float32),
    )
    a_proj = jnp.dot(a_weight, node_features, preferred_element_type=jnp.float32)
    return finish(node_features, a_proj, numerator, denominator, ln_gain)


def solution(mesh):
    in_specs = (
        P(None, ("dst", "src")),
        P("dst", "src", None, None, None),
        P("dst", "src", None),
        P("dst", "src", None),
        P(),
        P(),
        P(),
        P(),
        P(),
        P(),
    )
    out_specs = P(None, ("dst", "src"))
    return jax.shard_map(local, mesh=mesh, in_specs=in_specs, out_specs=out_specs, check_vma=False)
```

profile of v0, /device:TPU:2, one launch (start us, length us, event | category | flops | bytes accessed | tf_op | source)
XLA Modules:
  0.0 641.4 jit_solution(15654343737141036641)
XLA Ops:
  6.5 1.6 convolution_convert_fusion
  8.2 1.6 convolution_convert_fusion.1
  10.5 1.0 convolution_convert_fusion.2
  11.5 39.3 %all_gather.9 = bf16[64,6144]{1,0:T(8,128)(2,1)} all-gather(bf16[64,384]{1,0:T(8,128)(2,1)S(1)} %convolution_convert_fusion.2), channel_id=1, replica_groups=mesh['dst'=32,'src'=16] {'src'}, dimensions={1}, use_global_device_ids=true | all-gather | bytes 835584 | tf_op jit(solution)/shard_map/all_gather | solution.py:47
  50.8 120.8 %all-gather.5.cloned.1.call-done = bf16[64,12288]{1,0:T(8,128)(2,1)} async-done(((bf16[64,384]{1,0:T(8,128)(2,1)}), bf16[64,12288]{1,0:T(8,128)(2,1)}) %all-gather.5.cloned.1.call-update) | async-done | bytes 1572880 | tf_op jit(solution)/shard_map/all_gather | solution.py:51
  171.6 157.9 %all-gather.3.cloned.1.call-done = bf16[64,12288]{1,0:T(8,128)(2,1)} async-done(((bf16[64,384]{1,0:T(8,128)(2,1)}), bf16[64,12288]{1,0:T(8,128)(2,1)}) %all-gather.3.cloned.1.call-update) | async-done | bytes 1572880 | tf_op jit(solution)/shard_map/all_gather | solution.py:52
  330.1 116.4 %while.12 = (s32[]{:T(128)}, f32[64,6144]{1,0:T(8,128)S(1)}, f32[64,6144]{1,0:T(8,128)S(1)}, s32[8]{0:T(128)S(1)}, bf16[64,6144]{1,0:T(8,128)(2,1)}, /*index=5*/...) while((s32[]{:T(128)}, f32[64,6144]{1,0:T(8,128)S(1)}, ...), condition=%wide.region_2.3_spmd, body=%wide.region_0.2_spmd.sunk | while | flops 17899528 | bytes 1131273 | solution.py:83
  335.2 0.8 dynamic-slice_bitcast_fusion.2
  336.0 0.8 dynamic-slice_convert_fusion.4
  336.9 0.8 dynamic-slice_convert_fusion.5
  337.7 0.8 convert_bitcast_fusion.2
  338.5 0.8 bitcast_convert_fusion.2
  339.3 1.6 fusion.18
  340.8 2.8 fusion.17
  349.8 0.8 dynamic-slice_bitcast_fusion.2
  350.6 0.8 dynamic-slice_convert_fusion.4
  351.4 0.8 dynamic-slice_convert_fusion.5
  352.3 0.8 convert_bitcast_fusion.2
  353.0 0.8 bitcast_convert_fusion.2
  353.8 1.6 fusion.18
  355.4 2.8 fusion.17
  364.3 0.8 dynamic-slice_bitcast_fusion.2
  365.2 0.8 dynamic-slice_convert_fusion.4
  366.0 0.8 dynamic-slice_convert_fusion.5
  367.6 0.8 bitcast_convert_fusion.2
  368.4 1.6 fusion.18
  370.0 2.8 fusion.17
  378.9 0.8 dynamic-slice_bitcast_fusion.2
  379.7 0.8 dynamic-slice_convert_fusion.4
  380.5 0.8 dynamic-slice_convert_fusion.5
  382.2 0.8 bitcast_convert_fusion.2
  382.9 1.6 fusion.18
  384.5 2.8 fusion.17
  393.4 0.8 dynamic-slice_bitcast_fusion.2
  394.3 0.8 dynamic-slice_convert_fusion.4
  395.1 0.8 dynamic-slice_convert_fusion.5
  396.7 0.8 bitcast_convert_fusion.2
  397.5 1.6 fusion.18
  399.1 2.8 fusion.17
  408.0 0.8 dynamic-slice_bitcast_fusion.2
  408.8 0.8 dynamic-slice_convert_fusion.4
  409.7 0.8 dynamic-slice_convert_fusion.5
  411.3 0.8 bitcast_convert_fusion.2
  412.0 1.6 fusion.18
  413.6 2.8 fusion.17
  422.5 0.8 dynamic-slice_bitcast_fusion.2
  423.4 0.8 dynamic-slice_convert_fusion.4
  424.2 0.8 dynamic-slice_convert_fusion.5
  425.8 0.8 bitcast_convert_fusion.2
  426.6 1.6 fusion.18
  428.2 2.8 fusion.17
  437.1 0.8 dynamic-slice_bitcast_fusion.2
  437.9 0.8 dynamic-slice_convert_fusion.4
  438.8 0.8 dynamic-slice_convert_fusion.5
  440.4 0.8 bitcast_convert_fusion.2
  441.1 1.6 fusion.18
  442.7 2.8 fusion.17
  446.6 1.0 convert_element_type.44
  447.6 2.5 copy.15
  450.2 1.5 copy.13
  451.7 88.8 %reduce-scatter.9.cloned.1.call-done = bf16[384,64]{1,0:T(8,128)(2,1)} async-done(((bf16[6144,64]{1,0:T(8,128)(2,1)}), bf16[384,64]{1,0:T(8,128)(2,1)}) %reduce-scatter.9.cloned.1.call-update) | async-done | bytes 49168
  540.5 1.0 copy.16
  541.5 91.4 %reduce-scatter.7.cloned.1.call-done = bf16[384,64]{1,0:T(8,128)(2,1)} async-done(((bf16[6144,64]{1,0:T(8,128)(2,1)}), bf16[384,64]{1,0:T(8,128)(2,1)}) %reduce-scatter.7.cloned.1.call-update) | async-done | bytes 49168
  632.9 1.0 copy.14
  (71 shorter events, 24.4 us)
Async XLA Ops:
  6.5 627.4 %copy-start = (bf16[64,64]{1,0:T(8,128)(2,1)S(1)}, bf16[64,64]{1,0:T(8,128)(2,1)}, u32[]{:S(2)}) copy-start(bf16[64,64]{1,0:T(8,128)(2,1)} %param.16) | copy-start | bytes 24580
  6.5 165.1 %all-gather.5.cloned.1.call-start = ((), (), s32[]{:S(2)}) async-start(), calls=%async_computation.3 | async-start | bytes 1622016 | tf_op jit(solution)/shard_map/all_gather | solution.py:51
  8.1 321.3 %all-gather.3.cloned.1.call-start = ((), (), s32[]{:S(2)}) async-start(), calls=%async_computation.2 | async-start | bytes 1622016 | tf_op jit(solution)/shard_map/all_gather | solution.py:52
  9.8 530.7 %reduce-scatter.9.cloned.1.call-start = ((), (), s32[]{:S(2)}) async-start(), calls=%async_computation.5 | async-start | bytes 1671168
  329.5 0.7 copy-start.3
  450.0 182.9 %reduce-scatter.7.cloned.1.call-start = ((), (), s32[]{:S(2)}) async-start(), calls=%async_computation.4 | async-start | bytes 1671168
  450.2 183.7 %copy-start.1 = (bf16[64,384]{1,0:T(8,128)(2,1)S(1)}, bf16[64,384]{1,0:T(8,128)(2,1)}, u32[]{:S(2)}) copy-start(bf16[64,384]{1,0:T(8,128)(2,1)} %param.12) | copy-start | bytes 147460
  451.7 182.4 %copy-start.2 = (f32[64]{0:T(128)S(1)}, f32[64]{0:T(128)}, u32[]{:S(2)}) copy-start(f32[64]{0:T(128)} %param.21) | copy-start | bytes 772
Sparse Core Ops, SparseCore 0:
  9.5 162.1 all-gather.4
  173.7 155.7 all-gather.2
  450.2 90.3 reduce-scatter.8
  545.1 87.7 reduce-scatter.6
where the time goes:
time: 645 us; the launch traced here: 641 us
  waiting for transfers between devices  459 us (71%)
  other arithmetic  51.4 us (8%)
  blocking collectives  39.3 us (6%)
  loops' own time  31.5 us (5%)
  local copies, waits for them, and re-layouts  29.9 us (5%)
  matrix products  17 us (3%)
  between operations  13.2 us (2%)
    unnamed x6, waiting for transfers between devices  180 us
    all_gather x1, waiting for transfers between devices, local(): lax.all_gather(e_proj, 'dst', axis=1, tiled=True)  158 us
    all_gather x1, waiting for transfers between devices, local(): lax.all_gather(b_proj, 'dst', axis=1, tiled=True)  121 us
    all_gather x1, blocking collectives, local(): row_panel = lax.all_gather(d_proj, 'src', axis=1, tiled=True)  39.3 us
    another operation x1, loops' own time, local(): lax.scan(add_tile, start_sums, (values_all, row_starts, col_starts))  31.5 us
    reduce_sum x8, other arithmetic, tile_terms(): denominator = jnp.sum(gate_vals, axis=2)  22.5 us
  transfers between devices with their start and end apart: 4, of which 4 were waited for; matrix products, arithmetic and copies ran while one was open for 1% of the time, Pallas kernels for 0%

commit v1 on v0

v1 whole, which is shorter than its diff:
```python
import jax, jax.numpy as jnp
from jax import lax
from jax.sharding import Mesh, PartitionSpec as P
from jax.experimental import pallas as pl
from jax.experimental.pallas import tpu as pltpu

GROUP = 8

def tiles_kernel(owner_ref, row_ref, block_ref, col_ref, gain_ref, rows_ref, cols_ref, w_ref, wd_ref, we_ref, wb_ref,
                 out_ref, acc, gates, d_scr, b_scr, wt_scr, mask_scr):
    n_tiles, block_len, _ = w_ref.shape
    width = wd_ref.shape[0]
    n_groups = width // GROUP
    acc[...] = jnp.zeros_like(acc)
    out_ref[:, 2 * width:, :] = jnp.zeros((out_ref.shape[0], 16, block_len), out_ref.dtype)
    row_id = lax.broadcasted_iota(jnp.int32, (2 * GROUP, block_len), 0)

    def tile(t, _):
        owner = owner_ref[t]
        xr = rows_ref[row_ref[t]]
        xc = cols_ref[col_ref[t]]
        half = jnp.float32(0.5)
        d_scr[...] = half * jnp.dot(wd_ref[...], xr, preferred_element_type=jnp.float32).astype(jnp.bfloat16).astype(jnp.float32)
        b_scr[...] = jnp.dot(wb_ref[...], xc, preferred_element_type=jnp.float32).astype(jnp.bfloat16).astype(jnp.float32)
        wt = w_ref[t].astype(jnp.float32).T
        wt_scr[...] = half * wt
        mask_scr[...] = (wt != 0).astype(jnp.float32)

        def group(g, _):
            we_g = we_ref[pl.ds(pl.multiple_of(g * GROUP, GROUP), GROUP), :]
            e_t = lax.dot_general(xc, we_g, (((0,), (1,)), ((), ())), preferred_element_type=jnp.float32)
            e_t = half * e_t.astype(jnp.bfloat16).astype(jnp.float32)
            d_g = d_scr[pl.ds(pl.multiple_of(g * GROUP, GROUP), GROUP), :]
            b_g = b_scr[pl.ds(pl.multiple_of(g * GROUP, GROUP), GROUP), :]
            lhs = []
            for k in range(GROUP):
                p = gain_ref[g * GROUP + k] * wt_scr[...] + d_g[k:k + 1, :] + e_t[:, k:k + 1]
                s = (jnp.tanh(p) + 1.0) * mask_scr[...]
                gates[k * block_len:(k + 1) * block_len, :] = s.astype(jnp.bfloat16)
                lhs.append(jnp.where(row_id == k, b_g[k:k + 1, :], jnp.where(row_id == GROUP + k, 1.0, 0.0)).astype(jnp.bfloat16))
            lhs = jnp.concatenate(lhs, axis=1)
            sums = jnp.dot(lhs, gates[...], preferred_element_type=jnp.float32)
            at = pl.ds(pl.multiple_of(g * GROUP, GROUP), GROUP)
            acc[owner, at, :] += half * sums[:GROUP]
            at2 = pl.ds(pl.multiple_of(width + g * GROUP, GROUP), GROUP)
            acc[owner, at2, :] += half * sums[GROUP:]
            return 0
        lax.fori_loop(0, n_groups, group, 0)
        out_ref[owner, 2 * width:, :] = jnp.full((16, block_len), block_ref[t], jnp.int32).astype(jnp.float32).astype(out_ref.dtype)
        return 0
    lax.fori_loop(0, n_tiles, tile, 0)
    out_ref[:, :2 * width, :] = acc[...].astype(out_ref.dtype)


def tile_sums(owner, row, block, col, gain, rows, cols, w, wd, we, wb, n_owners):
    n_tiles, block_len, _ = w.shape
    width = wd.shape[0]
    smem = pl.BlockSpec(memory_space=pltpu.SMEM)
    vmem = pl.BlockSpec(memory_space=pltpu.VMEM)
    return pl.pallas_call(
        tiles_kernel,
        out_shape=jax.ShapeDtypeStruct((n_owners, 2 * width + 16, block_len), jnp.bfloat16),
        in_specs=[smem] * 5 + [vmem] * 6,
        out_specs=vmem,
        scratch_shapes=[
            pltpu.VMEM((n_owners, 2 * width, block_len), jnp.float32),
            pltpu.VMEM((GROUP * block_len, block_len), jnp.bfloat16),
            pltpu.VMEM((width, block_len), jnp.float32),
            pltpu.VMEM((width, block_len), jnp.float32),
            pltpu.VMEM((block_len, block_len), jnp.float32),
            pltpu.VMEM((block_len, block_len), jnp.float32),
        ],
        compiler_params=pltpu.CompilerParams(vmem_limit_bytes=32 * 1024 * 1024),
        name="tile_sums",
    )(owner, row, block, col, gain, rows, cols, w, wd, we, wb)


def finish_kernel(parts_ref, x_ref, wa_ref, gain_ref, out_ref):
    width = wa_ref.shape[0]
    n_src, _, block_len = parts_ref.shape
    n_blocks = x_ref.shape[1] // block_len
    for k in range(n_blocks):
        num = jnp.zeros((width, block_len), jnp.float32)
        den = jnp.zeros((width, block_len), jnp.float32)
        for s in range(n_src):
            hit = (parts_ref[s, 2 * width:, :].astype(jnp.float32)[:1] == float(k)).astype(jnp.float32)
            num += parts_ref[s, :width, :].astype(jnp.float32) * hit
            den += parts_ref[s, width:2 * width, :].astype(jnp.float32) * hit
        x = x_ref[:, k * block_len:(k + 1) * block_len]
        a = jnp.dot(wa_ref[...], x, preferred_element_type=jnp.float32)
        mixed = a + num / (den + 1e-6)
        center = mixed - jnp.mean(mixed, axis=0, keepdims=True)
        spread = jnp.mean(center * center, axis=0, keepdims=True)
        normed = center * lax.rsqrt(spread + 1e-5) * gain_ref[...]
        out_ref[:, k * block_len:(k + 1) * block_len] = (x.astype(jnp.float32) + jnp.maximum(normed, 0.0)).astype(jnp.bfloat16)


def finish(parts, x, wa, gain):
    vmem = pl.BlockSpec(memory_space=pltpu.VMEM)
    return pl.pallas_call(
        finish_kernel,
        out_shape=jax.ShapeDtypeStruct(x.shape, jnp.bfloat16),
        in_specs=[vmem] * 4, out_specs=vmem,
        name="finish",
    )(parts, x, wa, gain[:, None])


def spread(x, axes, n):
    return lax.all_to_all(jnp.broadcast_to(x[None], (n,) + x.shape), axes, 0, 0)


def local(x, edge_values, tile_rows, tile_cols, wa, wb, wd, we, edge_gain, ln_gain):
    width, shard = x.shape
    n_tiles, block_len = edge_values.shape[-3], edge_values.shape[-1]
    n_blocks = shard // block_len
    n_z, n_y, n_x, n_h, n_c = (lax.axis_size(a) for a in AXES)
    n_src = n_x * n_h * n_c
    rows, cols = tile_rows.reshape(-1), tile_cols.reshape(-1)
    tiles = edge_values.reshape(n_tiles, block_len, block_len)
    blocks = x.reshape(width, n_blocks, block_len).transpose(1, 0, 2)

    partner = lax.ppermute(blocks, "yhi", [(i, (i + 1) % n_h) for i in range(n_h)])
    by_z = spread(blocks, "z", n_z).reshape(n_z * n_blocks, width, block_len)
    wanted = spread(cols, "ylo", n_y)
    both = jnp.stack([blocks, partner])
    row_panel = spread(both, ("x", "core"), n_x * n_c)
    owner, block = wanted // n_blocks, wanted % n_blocks
    picked = jnp.take(by_z, ((owner // n_y) * n_blocks + block).reshape(-1), axis=0)
    col_blocks = lax.all_to_all(picked.reshape(n_y, n_tiles, width, block_len), "ylo", 0, 0)

    row_owner, row_block = rows // n_blocks, rows % n_blocks
    h = row_owner // n_c % n_h
    other = (h != lax.axis_index("yhi")).astype(jnp.int32)
    row_at = (((row_owner // (n_h * n_c)) * n_c + row_owner % n_c) * n_h + other) * n_blocks + row_block
    col_at = (cols // n_blocks % n_y) * n_tiles + jnp.arange(n_tiles, dtype=jnp.int32)
    parts = tile_sums(
        row_owner, row_at, row_block, col_at, edge_gain,
        row_panel.reshape(-1, width, block_len), col_blocks.reshape(-1, width, block_len),
        tiles, wd, we, wb, n_src,
    )
    parts = lax.all_to_all(parts, SRC, 0, 0)
    return finish(parts, x, wa, ln_gain)


AXES = ("z", "ylo", "x", "yhi", "core")
DST, SRC = AXES[:2], AXES[2:]


def solution(mesh):
    n_dst, n_src = mesh.devices.shape
    fine = Mesh(mesh.devices.reshape(n_dst // 4, 4, n_src // 4, 2, 2), AXES)
    in_specs = (
        P(None, AXES), P(DST, SRC, None, None, None), P(DST, SRC, None), P(DST, SRC, None),
        P(), P(), P(), P(), P(), P(),
    )
    return jax.shard_map(local, mesh=fine, in_specs=in_specs, out_specs=P(None, AXES), check_vma=False)
```

time: 645 us -> 145 us (0.22)
  the two profiles are of different devices: /device:TPU:2 before, /device:TPU:1 now
where the time goes in v1:
time: 145 us; the launch traced here: 144 us
  waiting for transfers between devices  49.5 us (34%)
  Pallas kernels  43.6 us (30%)
  starting transfers between devices  40.8 us (28%)
  local copies, waits for them, and re-layouts  8.24 us (6%)
  other arithmetic  1.82 us (1%)
    pallas_call x1, Pallas kernels, tile_sums(): pl.pallas_call(tiles_kernel, out_shape=jax.ShapeDtypeStruct((n_owners, 2...  41.5 us
    all_to_all x3, starting transfers between devices, spread(): return lax.all_to_all(jnp.broadcast_to(x[None], (n,) + x.shape), axes, 0, 0)  23.3 us
    all_to_all x3, waiting for transfers between devices, spread(): return lax.all_to_all(jnp.broadcast_to(x[None], (n,) + x.shape), axes, 0, 0)  17.2 us
    all_to_all x1, waiting for transfers between devices, local(): parts = lax.all_to_all(parts, SRC, 0, 0)  17 us
    all_to_all x1, waiting for transfers between devices, local(): lax.all_to_all(picked.reshape(n_y, n_tiles, width, block_len), 'ylo', 0, 0)  13.9 us
    all_to_all x1, starting transfers between devices, local(): parts = lax.all_to_all(parts, SRC, 0, 0)  7.76 us
    ppermute x1, starting transfers between devices, local(): lax.ppermute(blocks, 'yhi', [(i, (i + 1) % n_h) for i in range(n_h)])  6.05 us
    all_to_all x1, starting transfers between devices, local(): lax.all_to_all(picked.reshape(n_y, n_tiles, width, block_len), 'ylo', 0, 0)  3.6 us
  transfers between devices with their start and end apart: 6, of which 6 were waited for; matrix products, arithmetic and copies ran while one was open for 3% of the time, Pallas kernels for 0%

profile of v1, /device:TPU:1, one launch (start us, length us, event | category | flops | bytes accessed | tf_op | source)
XLA Modules:
  0.0 144.0 jit_solution(18041271187724305021)
XLA Ops:
  0.0 0.0 copy-start.7
  0.0 0.7 copy-done.7
  0.7 0.6 broadcast_in_dim.31
  1.2 5.4 %all-to-all-start.1 = ((s32[4,1,8]{2,1,0:T(1,128)}), s32[4,1,8]{2,1,0:T(1,128)S(1)}, u32[]{:S(2)}, u32[]{:S(2)}) async-start(s32[4,1,8]{2,1,0:T(1,128)} %broadcast_in_dim.31), calls=%async_computation.1 | async-start | bytes 4096 | tf_op jit(solution)/shard_map/all_to_all | solution.py:109
  6.7 0.8 reshape.177
  7.5 3.5 %all-to-all-done.1 = s32[4,1,8]{2,1,0:T(1,128)S(1)} async-done(((s32[4,1,8]{2,1,0:T(1,128)}), s32[4,1,8]{2,1,0:T(1,128)S(1)}, u32[]{:S(2)}, u32[]{:S(2)}) %all-to-all-start.1) | async-done | bytes 160 | tf_op jit(solution)/shard_map/all_to_all | solution.py:109
  11.0 0.8 broadcast_in_dim.33
  11.8 10.0 %all-to-all-start.2 = ((bf16[8,3,64,128]{3,2,1,0:T(8,128)(2,1)}), bf16[8,3,64,128]{3,2,1,0:T(8,128)(2,1)S(1)}, u32[]{:S(2)}, u32[]{:S(2)}) async-start(bf16[8,3,64,128]{3,2,1,0:T(8,128)(2,1)} %broadcast_in_dim.33), calls=%async_computation.2 | async-start | bytes 786432 | tf_op jit(solution)/shard_map/all_to_all | solution.py:109
  21.8 6.0 %collective-permute-start = (bf16[3,64,128]{2,0,1:T(4,128)(2,1)S(1)}, bf16[3,64,128]{2,0,1:T(4,128)(2,1)S(1)}, u32[]{:S(2)}, u32[]{:S(2)}) collective-permute-start(bf16[3,64,128]{2,0,1:T(4,128)(2,1)S(1)} %bitcast.43), channel_id=1, source_target_pairs={{0,2},{2,0},{1,3},{3,1},{4,6},{6,4},{5,7},{7,5},{8,10},{10,8},{9,1... | collective-permute-start | bytes 147464 | tf_op jit(solution)/shard_map/ppermute | solution.py:122
  27.9 0.5 broadcast.276
  28.4 0.7 broadcast_remainder_fusion
  29.1 0.1 rem.175
  29.2 0.1 div.88
  29.3 0.1 ne.190
  29.4 1.4 collective-permute-done
  30.7 0.1 pad_maximum_fusion
  30.9 3.0 %all-to-all-done.2 = bf16[8,3,64,128]{3,2,1,0:T(8,128)(2,1)S(1)} async-done(((bf16[8,3,64,128]{3,2,1,0:T(8,128)(2,1)}), bf16[8,3,64,128]{3,2,1,0:T(8,128)(2,1)S(1)}, u32[]{:S(2)}, u32[]{:S(2)}) %all-to-all-start.2) | async-done | bytes 393248 | tf_op jit(solution)/shard_map/all_to_all | solution.py:109
  33.9 1.1 broadcast_in_dim.30
  35.0 7.9 %all-to-all-start = ((bf16[8,2,3,64,128]{4,3,2,1,0:T(8,128)(2,1)}), bf16[8,2,3,64,128]{4,3,2,1,0:T(8,128)(2,1)S(1)}, u32[]{:S(2)}, u32[]{:S(2)}) async-start(bf16[8,2,3,64,128]{4,3,2,1,0:T(8,128)(2,1)} %broadcast_in_dim.30), calls=%async_computation | async-start | bytes 1572864 | tf_op jit(solution)/shard_map/all_to_all | solution.py:109
  42.9 0.6 gather_fusion
  43.6 0.9 broadcast_select_fusion
  44.5 0.0 copy-start
  44.5 10.7 %all-to-all-done = bf16[8,2,3,64,128]{4,3,2,1,0:T(8,128)(2,1)S(1)} async-done(((bf16[8,2,3,64,128]{4,3,2,1,0:T(8,128)(2,1)}), bf16[8,2,3,64,128]{4,3,2,1,0:T(8,128)(2,1)S(1)}, u32[]{:S(2)}, u32[]{:S(2)}) %all-to-all-start) | async-done | bytes 786464 | tf_op jit(solution)/shard_map/all_to_all | solution.py:109
  55.2 0.0 copy-start.8
  55.2 0.0 copy-start.2
  55.2 0.0 copy-start.3
  55.2 3.6 %all-to-all-start.3 = ((bf16[4,8,64,128]{3,2,1,0:T(8,128)(2,1)}), bf16[4,8,64,128]{3,2,1,0:T(8,128)(2,1)S(1)}, u32[]{:S(2)}, u32[]{:S(2)}) async-start(bf16[4,8,64,128]{3,2,1,0:T(8,128)(2,1)} %broadcast_select_fusion), calls=%async_computation.3 | async-start | bytes 1048576 | tf_op jit(solution)/shard_map/all_to_all | solution.py:129
  58.8 0.0 copy-start.1
  58.8 0.0 copy-done.8
  58.9 13.9 %all-to-all-done.3 = bf16[4,8,64,128]{3,2,1,0:T(8,128)(2,1)S(1)} async-done(((bf16[4,8,64,128]{3,2,1,0:T(8,128)(2,1)}), bf16[4,8,64,128]{3,2,1,0:T(8,128)(2,1)S(1)}, u32[]{:S(2)}, u32[]{:S(2)}) %all-to-all-start.3) | async-done | bytes 524320 | tf_op jit(solution)/shard_map/all_to_all | solution.py:129
  72.7 0.0 copy-start.4
  72.8 0.0 copy-done
  72.8 0.0 copy-done.2
  72.8 0.0 copy-done.3
  72.8 0.0 copy-done.1
  72.8 0.6 copy-done.4
  73.4 41.5 %tile_sums.1 = bf16[16,144,128]{2,1,0:T(8,128)(2,1)} custom-call(s32[8]{0:T(128)S(1)} %get-tuple-element.11.owner_ref, s32[8]{0:T(128)S(1)} %get-tuple-element.9.row_ref, s32[8]{0:T(128)S(1)} %get-tuple-element.10.block_ref, s32[8]{0:T(128)S(1)} %fusion.9.col_ref, f32[64]{0:T(128)S(1)} %copy-done.4, bf16[48,64,128]{2,1,0:T(8,128)(2,1)S(1)} %bitcast.37, ...), custom_call_target="tpu_custom_call" | custom-call | tf_op jit(solution)/shard_map/tile_sums/pallas_call | solution.py:60
  114.9 7.8 %all-to-all-start.4 = ((bf16[16,144,128]{2,1,0:T(8,128)(2,1)}), bf16[16,144,128]{2,1,0:T(8,128)(2,1)S(1)}, u32[]{:S(2)}, u32[]{:S(2)}) async-start(bf16[16,144,128]{2,1,0:T(8,128)(2,1)} %tile_sums.1), calls=%async_computation.4 | async-start | bytes 1179648 | tf_op jit(solution)/shard_map/all_to_all | solution.py:141
  122.7 0.0 copy-start.6
  122.7 0.6 copy-done.6
  123.3 0.7 copy.22.gain_ref
  124.0 17.0 %all-to-all-done.4.parts_ref = bf16[16,144,128]{2,1,0:T(8,128)(2,1)S(1)} async-done(((bf16[16,144,128]{2,1,0:T(8,128)(2,1)}), bf16[16,144,128]{2,1,0:T(8,128)(2,1)S(1)}, u32[]{:S(2)}, u32[]{:S(2)}) %all-to-all-start.4) | async-done | bytes 589856 | tf_op jit(solution)/shard_map/all_to_all | solution.py:141
  141.1 0.0 copy-start.5
  141.1 0.8 copy-done.5
  141.9 2.1 %finish.1 = bf16[64,384]{1,0:T(8,128)(2,1)} custom-call(bf16[16,144,128]{2,1,0:T(8,128)(2,1)} %copy-done.5, bf16[64,384]{1,0:T(8,128)(2,1)} %x_ref.1, bf16[64,64]{1,0:T(8,128)(2,1)} %wa_ref.1, f32[64,1]{1,0:T(8,128)} %copy.22.gain_ref), custom_call_target="tpu_custom_call" | custom-call | tf_op jit(solution)/shard_map/finish/pallas_call | solution.py:100
  (8 shorter events, 0.2 us)
Async XLA Ops:
  0.0 0.7 copy-start.7
  1.2 9.7 %all-to-all-start.1 = ((s32[4,1,8]{2,1,0:T(1,128)}), s32[4,1,8]{2,1,0:T(1,128)S(1)}, u32[]{:S(2)}, u32[]{:S(2)}) async-start(s32[4,1,8]{2,1,0:T(1,128)} %broadcast_in_dim.31), calls=%async_computation.1 | async-start | bytes 4096 | tf_op jit(solution)/shard_map/all_to_all | solution.py:109
  11.8 22.1 %all-to-all-start.2 = ((bf16[8,3,64,128]{3,2,1,0:T(8,128)(2,1)}), bf16[8,3,64,128]{3,2,1,0:T(8,128)(2,1)S(1)}, u32[]{:S(2)}, u32[]{:S(2)}) async-start(bf16[8,3,64,128]{3,2,1,0:T(8,128)(2,1)} %broadcast_in_dim.33), calls=%async_computation.2 | async-start | bytes 786432 | tf_op jit(solution)/shard_map/all_to_all | solution.py:109
  21.8 8.9 %collective-permute-start = (bf16[3,64,128]{2,0,1:T(4,128)(2,1)S(1)}, bf16[3,64,128]{2,0,1:T(4,128)(2,1)S(1)}, u32[]{:S(2)}, u32[]{:S(2)}) collective-permute-start(bf16[3,64,128]{2,0,1:T(4,128)(2,1)S(1)} %bitcast.43), channel_id=1, source_target_pairs={{0,2},{2,0},{1,3},{3,1},{4,6},{6,4},{5,7},{7,5},{8,10},{10,8},{9,1... | collective-permute-start | bytes 147464 | tf_op jit(solution)/shard_map/ppermute | solution.py:122
  35.0 20.2 %all-to-all-start = ((bf16[8,2,3,64,128]{4,3,2,1,0:T(8,128)(2,1)}), bf16[8,2,3,64,128]{4,3,2,1,0:T(8,128)(2,1)S(1)}, u32[]{:S(2)}, u32[]{:S(2)}) async-start(bf16[8,2,3,64,128]{4,3,2,1,0:T(8,128)(2,1)} %broadcast_in_dim.30), calls=%async_computation | async-start | bytes 1572864 | tf_op jit(solution)/shard_map/all_to_all | solution.py:109
  44.5 28.2 %copy-start = (bf16[1,1,8,128,128]{4,3,2,1,0:T(8,128)(2,1)S(1)}, bf16[1,1,8,128,128]{4,3,2,1,0:T(8,128)(2,1)}, u32[]{:S(2)}) copy-start(bf16[1,1,8,128,128]{4,3,2,1,0:T(8,128)(2,1)} %param.11) | copy-start | bytes 786436
  55.2 3.7 %copy-start.8 = (s32[1,1,8]{2,1,0:T(1,128)S(1)}, s32[1,1,8]{2,1,0:T(1,128)}, u32[]{:S(2)}) copy-start(s32[1,1,8]{2,1,0:T(1,128)} %param.12) | copy-start | bytes 100
  55.2 17.6 %copy-start.2 = (bf16[64,64]{1,0:T(8,128)(2,1)S(1)}, bf16[64,64]{1,0:T(8,128)(2,1)}, u32[]{:S(2)}) copy-start(bf16[64,64]{1,0:T(8,128)(2,1)} %we_ref.1) | copy-start | bytes 24580
  55.2 17.6 %copy-start.3 = (bf16[64,64]{1,0:T(8,128)(2,1)S(1)}, bf16[64,64]{1,0:T(8,128)(2,1)}, u32[]{:S(2)}) copy-start(bf16[64,64]{1,0:T(8,128)(2,1)} %wb_ref.1) | copy-start | bytes 24580
  55.2 17.6 %all-to-all-start.3 = ((bf16[4,8,64,128]{3,2,1,0:T(8,128)(2,1)}), bf16[4,8,64,128]{3,2,1,0:T(8,128)(2,1)S(1)}, u32[]{:S(2)}, u32[]{:S(2)}) async-start(bf16[4,8,64,128]{3,2,1,0:T(8,128)(2,1)} %broadcast_select_fusion), calls=%async_computation.3 | async-start | bytes 1048576 | tf_op jit(solution)/shard_map/all_to_all | solution.py:129
  58.8 14.0 %copy-start.1 = (bf16[64,64]{1,0:T(8,128)(2,1)S(1)}, bf16[64,64]{1,0:T(8,128)(2,1)}, u32[]{:S(2)}) copy-start(bf16[64,64]{1,0:T(8,128)(2,1)} %wd_ref.1) | copy-start | bytes 24580
  72.7 0.7 copy-start.4
  114.9 26.2 %all-to-all-start.4 = ((bf16[16,144,128]{2,1,0:T(8,128)(2,1)}), bf16[16,144,128]{2,1,0:T(8,128)(2,1)S(1)}, u32[]{:S(2)}, u32[]{:S(2)}) async-start(bf16[16,144,128]{2,1,0:T(8,128)(2,1)} %tile_sums.1), calls=%async_computation.4 | async-start | bytes 1179648 | tf_op jit(solution)/shard_map/all_to_all | solution.py:141
  122.7 0.7 copy-start.6
  141.1 0.8 copy-start.5

commit v2 on v1

v2 whole, which is shorter than its diff:
```python
import jax, jax.numpy as jnp
from jax import lax
from jax.sharding import Mesh, PartitionSpec as P
from jax.experimental import pallas as pl
from jax.experimental.pallas import tpu as pltpu

AXES = ("za", "zb", "ya", "yb", "x", "yhi", "core")
DST, SRC = AXES[:4], AXES[4:]
GROUP = 8
CHUNK = 128
BAND = 16


def pack_kernel(rows_ref, x_ref, shard_ref, spread_ref):
    width, shard = x_ref.shape
    block_len = spread_ref.shape[3]
    n_tiles = rows_ref.shape[0]
    for k in range(shard // block_len):
        block = x_ref[:, k * block_len:(k + 1) * block_len]
        shard_ref[k * width:(k + 1) * width, :] = block
        for n in range(spread_ref.shape[0]):
            spread_ref[n, k] = block
    sub = lax.broadcasted_iota(jnp.int32, (BAND, block_len), 0)
    band = jnp.full((BAND, block_len), -1, jnp.int32)
    for t in range(n_tiles):
        band = jnp.where(sub == t, rows_ref[t], band)
    shard_ref[shard // block_len * width:, :] = band.astype(jnp.float32).astype(shard_ref.dtype)


def pack(rows, x, block_len, copies):
    width, shard = x.shape
    n_blocks = shard // block_len
    vmem = pl.BlockSpec(memory_space=pltpu.VMEM)
    return pl.pallas_call(
        pack_kernel,
        out_shape=(
            jax.ShapeDtypeStruct((n_blocks * width + BAND, block_len), x.dtype),
            jax.ShapeDtypeStruct((copies, n_blocks, width, block_len), x.dtype),
        ),
        in_specs=[pl.BlockSpec(memory_space=pltpu.SMEM), vmem],
        out_specs=(vmem, vmem),
        name="pack",
    )(rows, x)


def pair_kernel(own_ref, partner_ref, out_ref):
    for n in range(out_ref.shape[0]):
        out_ref[n, 0] = own_ref[...]
        out_ref[n, 1] = partner_ref[...]


def pair(own, partner, copies):
    vmem = pl.BlockSpec(memory_space=pltpu.VMEM)
    return pl.pallas_call(
        pair_kernel,
        out_shape=jax.ShapeDtypeStruct((copies, 2) + own.shape, own.dtype),
        in_specs=[vmem, vmem],
        out_specs=vmem,
        name="pair",
    )(own, partner)


def tiles_kernel(here_ref, tile_rows_ref, tile_cols_ref, gain_ref, rows_ref, own_ref, got_z_ref, got_y_ref, got_zy_ref, w_ref, wd_ref, we_ref, wb_ref,
                 out_ref, acc, x_scr, d_scr, e_scr, w_scr, m_scr, lhs_scr, rep_scr, gain_scr):
    n_tiles, block_len, _ = w_ref.shape
    width = wd_ref.shape[0]
    n_blocks = rows_ref.shape[1] // width
    n_groups = width // GROUP
    n_chunks = block_len // CHUNK
    span = GROUP * CHUNK
    f32, bf16 = jnp.float32, jnp.bfloat16
    half = f32(0.5)
    acc[...] = jnp.zeros_like(acc)
    lane = lax.broadcasted_iota(jnp.int32, (block_len, n_chunks * span), 1)
    sub = lax.broadcasted_iota(jnp.int32, (block_len, n_chunks * span), 0)
    rep_scr[...] = (sub == lane // span * CHUNK + lane % CHUNK).astype(f32).astype(bf16)
    lane = lax.broadcasted_iota(jnp.int32, (GROUP, span), 1)
    sub = lax.broadcasted_iota(jnp.int32, (GROUP, span), 0)
    own = (lane // CHUNK == sub).astype(f32)

    lane = lax.broadcasted_iota(jnp.int32, (width, width), 1)
    sub = lax.broadcasted_iota(jnp.int32, (width, width), 0)
    column = jnp.sum(jnp.where(lane == sub, gain_ref[...], 0.0), axis=1, keepdims=True)
    gain_scr[...] = jnp.broadcast_to(column, gain_scr.shape)

    for t in range(n_tiles):
        at = slice(t * block_len, (t + 1) * block_len)
        owner, block = tile_rows_ref[t] // n_blocks, tile_rows_ref[t] % n_blocks
        panel = (owner // 4 * 2 + owner % 2) * 2 + ((owner // 2 % 2) ^ here_ref[2])
        x_scr[0, :, at] = rows_ref[panel, pl.ds(pl.multiple_of(block * width, width), width), :]
        owner = tile_cols_ref[t] // n_blocks
        source = ((owner // 4 % 2) ^ here_ref[0]) * 2 + ((owner % 2) ^ here_ref[1])
        place = (owner // 8 * 2 + owner // 2 % 2) * n_blocks + tile_cols_ref[t] % n_blocks
        for k, ref in enumerate((own_ref, got_y_ref, got_z_ref, got_zy_ref)):
            @pl.when(source == k)
            def _(ref=ref, at=at, t=t, k=k):
                x_scr[1, :, at] = ref[place if k == 0 else t]
    d_all = half * jnp.dot(wd_ref[...], x_scr[0], preferred_element_type=f32).astype(bf16).astype(f32)
    b_all = jnp.dot(wb_ref[...], x_scr[1], preferred_element_type=f32).astype(bf16)
    e_all = lax.dot_general(x_scr[1], we_ref[...], (((0,), (1,)), ((), ())), preferred_element_type=f32)
    e_all = (half * e_all.astype(bf16).astype(f32)).astype(bf16)
    for t in range(n_tiles):
        at = slice(t * block_len, (t + 1) * block_len)
        d_scr[t] = d_all[:, at]
        e_scr[t] = e_all[at, :]
        wt = w_ref[t].astype(f32).T
        m_scr[t] = (wt != 0).astype(f32).astype(bf16)
        w_scr[t] = half * wt
        for c in range(n_chunks):
            b_rep = jnp.dot(b_all[:, at], rep_scr[:, c * span:(c + 1) * span], preferred_element_type=f32)
            for g in range(n_groups):
                lhs_scr[t, c, g] = jnp.concatenate([b_rep[g * GROUP:(g + 1) * GROUP] * own, own], axis=0).astype(bf16)

    def tile(t, _):
        owner = tile_rows_ref[t] // n_blocks
        for c in range(n_chunks):
            at = slice(c * CHUNK, (c + 1) * CHUNK)
            w_c, m_c, e_c = w_scr[t, at, :], m_scr[t, at, :], e_scr[t, at, :]
            for g in range(n_groups):
                gates = []
                for k in range(GROUP):
                    f = g * GROUP + k
                    e_f = e_c[:, f:f + 1].astype(f32)
                    p = gain_scr[f:f + 1, :] * w_c + d_scr[t, f:f + 1, :] + e_f
                    gates.append((jnp.tanh(p) + 1.0).astype(bf16) * m_c)
                sums = jnp.dot(lhs_scr[t, c, g], jnp.concatenate(gates, axis=0), preferred_element_type=f32)
                acc[owner, g * GROUP:(g + 1) * GROUP, :] += sums[:GROUP]
                acc[owner, width + g * GROUP:width + (g + 1) * GROUP, :] += sums[GROUP:]
        return 0
    lax.fori_loop(0, n_tiles, tile, 0)
    out_ref[...] = (half * acc[...]).astype(out_ref.dtype)


def tile_sums(here, tile_rows, tile_cols, gain, rows, own, got_z, got_y, got_zy, w, wd, we, wb, n_owners):
    n_tiles, block_len, _ = w.shape
    width = wd.shape[0]
    smem = pl.BlockSpec(memory_space=pltpu.SMEM)
    vmem = pl.BlockSpec(memory_space=pltpu.VMEM)
    n_chunks, n_groups = block_len // CHUNK, width // GROUP
    return pl.pallas_call(
        tiles_kernel,
        out_shape=jax.ShapeDtypeStruct((n_owners, 2 * width, block_len), jnp.bfloat16),
        in_specs=[smem] * 3 + [vmem] * 10,
        out_specs=vmem,
        scratch_shapes=[
            pltpu.VMEM((n_owners, 2 * width, block_len), jnp.float32),
            pltpu.VMEM((2, width, n_tiles * block_len), jnp.bfloat16),
            pltpu.VMEM((n_tiles, width, block_len), jnp.float32),
            pltpu.VMEM((n_tiles, block_len, width), jnp.bfloat16),
            pltpu.VMEM((n_tiles, block_len, block_len), jnp.float32),
            pltpu.VMEM((n_tiles, block_len, block_len), jnp.bfloat16),
            pltpu.VMEM((n_tiles, n_chunks, n_groups, 2 * GROUP, GROUP * CHUNK), jnp.bfloat16),
            pltpu.VMEM((block_len, n_chunks * GROUP * CHUNK), jnp.bfloat16),
            pltpu.VMEM((width, block_len), jnp.float32),
        ],
        compiler_params=pltpu.CompilerParams(vmem_limit_bytes=32 * 1024 * 1024),
        name="tile_sums",
    )(here, tile_rows, tile_cols, gain, rows, own, got_z, got_y, got_zy, w, wd, we, wb)


def finish_kernel(here_ref, parts_ref, band_ref, x_ref, wa_ref, gain_ref, out_ref):
    width = wa_ref.shape[0]
    n_src, _, block_len = parts_ref.shape
    n_blocks = x_ref.shape[1] // block_len
    f32 = jnp.float32
    lane = lax.broadcasted_iota(jnp.int32, (width, width), 1)
    sub = lax.broadcasted_iota(jnp.int32, (width, width), 0)
    gain = jnp.sum(jnp.where(lane == sub, gain_ref[...], 0.0), axis=1, keepdims=True)
    first = (here_ref[3] * n_blocks).astype(f32)
    named = [band_ref[(s // 4 * 2 + s % 2) * 2 + ((s // 2 % 2) ^ here_ref[2])].astype(f32) for s in range(n_src)]
    for k in range(n_blocks):
        num = jnp.zeros((width, block_len), f32)
        den = jnp.zeros((width, block_len), f32)
        for s in range(n_src):
            hit = jnp.max((named[s] == first + float(k)).astype(f32), axis=0, keepdims=True)
            num += parts_ref[s, :width, :].astype(f32) * hit
            den += parts_ref[s, width:, :].astype(f32) * hit
        x = x_ref[:, k * block_len:(k + 1) * block_len]
        a = jnp.dot(wa_ref[...], x, preferred_element_type=f32)
        mixed = a + num / (den + 1e-6)
        center = mixed - jnp.mean(mixed, axis=0, keepdims=True)
        spread = jnp.mean(center * center, axis=0, keepdims=True)
        normed = center * lax.rsqrt(spread + 1e-5) * gain
        out_ref[:, k * block_len:(k + 1) * block_len] = (x.astype(f32) + jnp.maximum(normed, 0.0)).astype(jnp.bfloat16)


def finish(here, parts, rows, x, wa, gain):
    whole = lambda a: pl.BlockSpec(a.shape, lambda i: (0,) * a.ndim)
    n, depth, block_len = rows.shape
    return pl.pallas_call(
        finish_kernel,
        grid=(1,),
        out_shape=jax.ShapeDtypeStruct(x.shape, jnp.bfloat16),
        in_specs=[
            pl.BlockSpec(memory_space=pltpu.SMEM),
            whole(parts),
            pl.BlockSpec((n, BAND, block_len), lambda i: (0, depth // BAND - 1, 0)),
            whole(x), whole(wa), whole(gain),
        ],
        out_specs=whole(x),
        name="finish",
    )(here, parts, rows, x, wa, gain)


def flip(x, axes):
    last = 2 ** len(axes) - 1
    return lax.ppermute(x, axes, [(i, i ^ last) for i in range(last + 1)])


def local(x, edge_values, tile_rows, tile_cols, wa, wb, wd, we, edge_gain, ln_gain):
    width, shard = x.shape
    n_tiles, block_len = edge_values.shape[-3], edge_values.shape[-1]
    n_blocks = shard // block_len
    n_za, n_x = lax.axis_size("za"), lax.axis_size("x")
    rows, cols = tile_rows.reshape(-1), tile_cols.reshape(-1)
    tiles = edge_values.reshape(n_tiles, block_len, block_len)
    here = jnp.stack([lax.axis_index(a) for a in ("zb", "yb", "yhi", SRC)]).astype(jnp.int32)

    shard_rows, copies = pack(rows, x, block_len, n_za * 2)
    partner = flip(shard_rows, ("yhi",))
    held = lax.all_to_all(copies, ("za", "ya"), 0, 0).reshape(-1, width, block_len)
    cols_z = flip(cols, ("zb",))
    cols_y, cols_zy = flip(jnp.stack([cols, cols_z]), ("yb",))
    row_panel = lax.all_to_all(pair(shard_rows, partner, n_x * 2), ("x", "core"), 0, 0)
    row_panel = row_panel.reshape(n_x * 4, -1, block_len)

    def pick(names):
        owner = names // n_blocks
        place = (owner // 8 * 2 + owner // 2 % 2) * n_blocks + names % n_blocks
        return held.at[place].get(mode="promise_in_bounds")

    got_z = flip(pick(cols_z), ("zb",))
    got_y = flip(pick(cols_y), ("yb",))
    got_zy = flip(pick(cols_zy), ("zb", "yb"))

    parts = tile_sums(
        here, rows, cols, edge_gain[None], row_panel, held, got_z, got_y, got_zy, tiles, wd, we, wb, n_x * 4
    )
    parts = lax.all_to_all(parts, SRC, 0, 0)
    return finish(here, parts, row_panel, x, wa, ln_gain[None])


def solution(mesh):
    n_dst, n_src = mesh.devices.shape
    fine = Mesh(mesh.devices.reshape(n_dst // 8, 2, 2, 2, n_src // 4, 2, 2), AXES)
    in_specs = (
        P(None, AXES), P(DST, SRC, None, None, None), P(DST, SRC, None), P(DST, SRC, None),
        P(), P(), P(), P(), P(), P(),
    )
    return jax.shard_map(local, mesh=fine, in_specs=in_specs, out_specs=P(None, AXES), check_vma=False)
```

time: 145 us -> 95 us (0.66)
  the two profiles are of different devices: /device:TPU:1 before, /device:TPU:8 now
where the time goes in v2:
time: 95 us; the launch traced here: 94.1 us
  starting transfers between devices  38.1 us (40%)
  blocking collectives  28.1 us (30%)
  Pallas kernels  16.6 us (17%)
  waiting for transfers between devices  7.95 us (8%)
  local copies, waits for them, and re-layouts  2.99 us (3%)
    all_to_all x1, blocking collectives, local(): parts = lax.all_to_all(parts, SRC, 0, 0)  28.1 us
    ppermute x6, starting transfers between devices, flip(): return lax.ppermute(x, axes, [(i, i ^ last) for i in range(last + 1)])  21.4 us
    all_to_all x1, starting transfers between devices, local(): lax.all_to_all(copies, ('za', 'ya'), 0, 0).reshape(-1, width, block_len)  12.5 us
    pallas_call x1, Pallas kernels, tile_sums(): pl.pallas_call(tiles_kernel, out_shape=jax.ShapeDtypeStruct((n_owners, 2...  10.9 us
    ppermute x6, waiting for transfers between devices, flip(): return lax.ppermute(x, axes, [(i, i ^ last) for i in range(last + 1)])  5.81 us
    all_to_all x1, starting transfers between devices, local(): lax.all_to_all(pair(shard_rows, partner, n_x * 2), ('x', 'core'), 0, 0)  4.3 us
    pallas_call x1, Pallas kernels, finish(): pl.pallas_call(finish_kernel, grid=(1,), out_shape=jax.ShapeDtypeStruct(x...  2.16 us
    all_to_all x1, waiting for transfers between devices, local(): lax.all_to_all(pair(shard_rows, partner, n_x * 2), ('x', 'core'), 0, 0)  2.14 us
  transfers between devices with their start and end apart: 8, of which 3 were waited for; matrix products, arithmetic and copies ran while one was open for 2% of the time, Pallas kernels for 2%

profile of v2, /device:TPU:8, one launch (start us, length us, event | category | flops | bytes accessed | tf_op | source)
XLA Modules:
  0.0 94.1 jit_solution(17838495143956721024)
XLA Ops:
  0.0 1.7 %pack.1 = (bf16[208,128]{1,0:T(8,128)(2,1)}, bf16[8,3,64,128]{3,2,1,0:T(8,128)(2,1)}) custom-call(s32[8]{0:T(128)} %bitcast.66, bf16[64,384]{1,0:T(8,128)(2,1)} %x_ref.3), custom_call_target="tpu_custom_call" | custom-call | tf_op jit(solution)/shard_map/pack/pallas_call | solution.py:34
  1.7 0.0 copy-start.9
  1.7 12.5 %all-to-all-start.1 = ((bf16[8,3,64,128]{3,2,1,0:T(8,128)(2,1)}), bf16[8,3,64,128]{3,2,1,0:T(8,128)(2,1)S(1)}, u32[]{:S(2)}, u32[]{:S(2)}) async-start(bf16[8,3,64,128]{3,2,1,0:T(8,128)(2,1)} %get-tuple-element.8), calls=%async_computation.1 | async-start | bytes 786432 | tf_op jit(solution)/shard_map/all_to_all | solution.py:221
  14.1 0.0 copy-done.9
  14.1 0.0 copy-start.7
  14.1 5.0 %collective-permute-start = (bf16[208,128]{1,0:T(8,128)(2,1)S(1)}, bf16[208,128]{1,0:T(8,128)(2,1)S(1)}, u32[]{:S(2)}, u32[]{:S(2)}) collective-permute-start(bf16[208,128]{1,0:T(8,128)(2,1)S(1)} %copy-done.9), channel_id=1, source_target_pairs={{0,2},{2,0},{1,3},{3,1},{4,6},{6,4},{5,7},{7,5},{8,10},{10,8},{9,1... | collective-permute-start | bytes 159752 | tf_op jit(solution)/shard_map/ppermute | solution.py:207
  19.2 0.0 copy-done.7
  19.2 3.4 %collective-permute-start.1 = (s32[8]{0:T(128)S(1)}, s32[8]{0:T(128)S(1)}, u32[]{:S(2)}, u32[]{:S(2)}) collective-permute-start(s32[8]{0:T(128)S(1)} %bitcast.68), channel_id=1, source_target_pairs={{0,64},{64,0},{1,65},{65,1},{2,66},{66,2},{3,67},{67,3},{4,68},{68... | collective-permute-start | bytes 104 | tf_op jit(solution)/shard_map/ppermute | solution.py:207
  22.6 2.0 %collective-permute-done.1 = s32[8]{0:T(128)S(1)} collective-permute-done((s32[8]{0:T(128)S(1)}, s32[8]{0:T(128)S(1)}, u32[]{:S(2)}, u32[]{:S(2)}) %collective-permute-start.1) | collective-permute-done | bytes 64 | tf_op jit(solution)/shard_map/ppermute | solution.py:207
  24.6 3.3 %collective-permute-start.3 = (s32[2,8]{1,0:T(2,128)S(1)}, s32[2,8]{1,0:T(2,128)S(1)}, u32[]{:S(2)}, u32[]{:S(2)}) collective-permute-start(s32[2,8]{1,0:T(2,128)S(1)} %pad_add_fusion), channel_id=1, source_target_pairs={{0,16},{16,0},{1,17},{17,1},{2,18},{18,2},{3,19},{19,3},{4,20},{20... | collective-permute-start | bytes 200 | tf_op jit(solution)/shard_map/ppermute | solution.py:207
  27.9 0.0 collective-permute-done.partner_ref
  27.9 0.0 copy-start.10
  27.9 0.6 copy-done.10
  28.5 1.9 %pair.1 = bf16[8,2,208,128]{3,2,1,0:T(8,128)(2,1)} custom-call(bf16[208,128]{1,0:T(8,128)(2,1)} %get-tuple-element.7.own_ref, bf16[208,128]{1,0:T(8,128)(2,1)} %copy-done.10), custom_call_target="tpu_custom_call" | custom-call | tf_op jit(solution)/shard_map/pair/pallas_call | solution.py:54
  30.4 0.0 all-to-all-done.1
  30.4 4.3 %all-to-all-start = ((bf16[8,2,208,128]{3,2,1,0:T(8,128)(2,1)}), bf16[8,2,208,128]{3,2,1,0:T(8,128)(2,1)S(1)}, u32[]{:S(2)}, u32[]{:S(2)}) async-start(bf16[8,2,208,128]{3,2,1,0:T(8,128)(2,1)} %pair.1), calls=%async_computation | async-start | bytes 1703936 | tf_op jit(solution)/shard_map/all_to_all | solution.py:224
  34.7 0.0 collective-permute-done.3
  34.8 0.6 gather_fusion
  35.4 0.0 copy-start.1
  35.4 3.5 %collective-permute-start.2 = (bf16[8,64,128]{2,1,0:T(8,128)(2,1)S(1)}, bf16[8,64,128]{2,1,0:T(8,128)(2,1)S(1)}, u32[]{:S(2)}, u32[]{:S(2)}) collective-permute-start(bf16[8,64,128]{2,1,0:T(8,128)(2,1)S(1)} %gather_fusion), channel_id=1, source_target_pairs={{0,64},{64,0},{1,65},{65,1},{2,66},{66,2},{3,67},{67,3},{4,68},{68... | collective-permute-start | bytes 393224 | tf_op jit(solution)/shard_map/ppermute | solution.py:207
  38.9 0.6 gather_fusion.1
  39.5 4.1 %collective-permute-start.4 = (bf16[8,64,128]{2,1,0:T(8,128)(2,1)S(1)}, bf16[8,64,128]{2,1,0:T(8,128)(2,1)S(1)}, u32[]{:S(2)}, u32[]{:S(2)}) collective-permute-start(bf16[8,64,128]{2,1,0:T(8,128)(2,1)S(1)} %gather_fusion.1), channel_id=1, source_target_pairs={{0,16},{16,0},{1,17},{17,1},{2,18},{18,2},{3,19},{19,3},{4,20},{20... | collective-permute-start | bytes 393224 | tf_op jit(solution)/shard_map/ppermute | solution.py:207
  43.6 0.6 gather_fusion.2
  44.2 2.1 %collective-permute-start.5 = (bf16[8,64,128]{2,1,0:T(8,128)(2,1)S(1)}, bf16[8,64,128]{2,1,0:T(8,128)(2,1)S(1)}, u32[]{:S(2)}, u32[]{:S(2)}) collective-permute-start(bf16[8,64,128]{2,1,0:T(8,128)(2,1)S(1)} %gather_fusion.2), channel_id=1, source_target_pairs={{0,80},{16,64},{64,16},{80,0},{1,81},{17,65},{65,17},{81,1},{2,82}... | collective-permute-start | bytes 393224 | tf_op jit(solution)/shard_map/ppermute | solution.py:207
  46.3 0.0 copy-start.4
  46.3 0.0 copy-start.8
  46.3 0.0 copy-start.2
  46.3 0.0 copy-start.3
  46.3 0.1 pad_add_fusion.1.here_ref
  46.4 0.0 copy-start.5
  46.4 2.1 %all-to-all-done = bf16[8,2,208,128]{3,2,1,0:T(8,128)(2,1)S(1)} async-done(((bf16[8,2,208,128]{3,2,1,0:T(8,128)(2,1)}), bf16[8,2,208,128]{3,2,1,0:T(8,128)(2,1)S(1)}, u32[]{:S(2)}, u32[]{:S(2)}) %all-to-all-start) | async-done | bytes 852000 | tf_op jit(solution)/shard_map/all_to_all | solution.py:224
  48.5 0.0 copy-start
  48.5 0.0 collective-permute-done.2.got_z_ref
  48.5 0.0 collective-permute-done.4.got_y_ref
  48.6 3.8 %collective-permute-done.5.got_zy_ref = bf16[8,64,128]{2,1,0:T(8,128)(2,1)S(1)} collective-permute-done((bf16[8,64,128]{2,1,0:T(8,128)(2,1)S(1)}, bf16[8,64,128]{2,1,0:T(8,128)(2,1)S(1)}, u32[]{:S(2)}, u32[]{:S(2)}) %collective-permute-start.5) | collective-permute-done | bytes 131104 | tf_op jit(solution)/shard_map/ppermute | solution.py:207
  52.3 0.0 copy-start.6
  52.3 0.0 copy-done.5
  52.3 0.0 copy-done.1
  52.3 0.0 copy-done.4
  52.3 0.0 copy-done.8
  52.3 0.0 copy-done.2
  52.3 0.0 copy-done.3
  52.4 0.6 copy-done.6
  53.0 10.9 %tile_sums.1 = bf16[16,128,128]{2,1,0:T(8,128)(2,1)S(1)} custom-call(s32[4]{0:T(128)S(1)} %pad_add_fusion.1.here_ref, s32[8]{0:T(128)S(1)} %bitcast.67, s32[8]{0:T(128)S(1)} %bitcast.70, f32[1,64]{1,0:T(1,128)S(1)} %bitcast.71, bf16[16,208,128]{2,1,0:T(8,128)(2,1)S(1)} %bitcast.59, bf16[24,64,128]{2,1,0:T(8,128)(2,1)S(1)} %bitcast.64, ...), custom_call_target="tpu_custom_call" | custom-call | tf_op jit(solution)/shard_map/tile_sums/pallas_call | solution.py:140
  63.9 0.0 copy-done
  63.9 28.1 %all_to_all.15.parts_ref = bf16[16,128,128]{2,1,0:T(8,128)(2,1)} all-to-all(bf16[16,128,128]{2,1,0:T(8,128)(2,1)S(1)} %tile_sums.1), channel_id=1, replica_groups=mesh['za'=4,'zb'=2,'ya'=2,'yb'=2,'x'=4,'yhi'=2,'core'=2] {'x','yhi','core'}, dimensions={0} | all-to-all | bytes 1048576 | tf_op jit(solution)/shard_map/all_to_all | solution.py:239
  92.0 2.2 %finish.1 = bf16[64,384]{1,0:T(8,128)(2,1)} custom-call(s32[4]{0:T(128)} %copy-done.5, bf16[16,128,128]{2,1,0:T(8,128)(2,1)} %all_to_all.15.parts_ref, bf16[16,208,128]{2,1,0:T(8,128)(2,1)} %bitcast.60, bf16[64,384]{1,0:T(8,128)(2,1)} %x_ref.3, bf16[64,64]{1,0:T(8,128)(2,1)} %wa_ref.1, f32[1,64]{1,0:T(1,128)} %bitcast.72), custom_call_target="tpu_custom_call" | custom-call | tf_op jit(solution)/shard_map/finish/pallas_call | solution.py:190
  (6 shorter events, 0.1 us)
Async XLA Ops:
  1.7 12.5 %copy-start.9 = (bf16[208,128]{1,0:T(8,128)(2,1)S(1)}, bf16[208,128]{1,0:T(8,128)(2,1)}, u32[]{:S(2)}) copy-start(bf16[208,128]{1,0:T(8,128)(2,1)} %get-tuple-element.7.own_ref) | copy-start | bytes 159748
  1.7 28.7 %all-to-all-start.1 = ((bf16[8,3,64,128]{3,2,1,0:T(8,128)(2,1)}), bf16[8,3,64,128]{3,2,1,0:T(8,128)(2,1)S(1)}, u32[]{:S(2)}, u32[]{:S(2)}) async-start(bf16[8,3,64,128]{3,2,1,0:T(8,128)(2,1)} %get-tuple-element.8), calls=%async_computation.1 | async-start | bytes 786432 | tf_op jit(solution)/shard_map/all_to_all | solution.py:221
  14.1 5.1 %copy-start.7 = (s32[1,1,8]{2,1,0:T(1,128)S(1)}, s32[1,1,8]{2,1,0:T(1,128)}, u32[]{:S(2)}) copy-start(s32[1,1,8]{2,1,0:T(1,128)} %param.13) | copy-start | bytes 100
  14.1 13.8 %collective-permute-start = (bf16[208,128]{1,0:T(8,128)(2,1)S(1)}, bf16[208,128]{1,0:T(8,128)(2,1)S(1)}, u32[]{:S(2)}, u32[]{:S(2)}) collective-permute-start(bf16[208,128]{1,0:T(8,128)(2,1)S(1)} %copy-done.9), channel_id=1, source_target_pairs={{0,2},{2,0},{1,3},{3,1},{4,6},{6,4},{5,7},{7,5},{8,10},{10,8},{9,1... | collective-permute-start | bytes 159752 | tf_op jit(solution)/shard_map/ppermute | solution.py:207
  19.2 5.4 %collective-permute-start.1 = (s32[8]{0:T(128)S(1)}, s32[8]{0:T(128)S(1)}, u32[]{:S(2)}, u32[]{:S(2)}) collective-permute-start(s32[8]{0:T(128)S(1)} %bitcast.68), channel_id=1, source_target_pairs={{0,64},{64,0},{1,65},{65,1},{2,66},{66,2},{3,67},{67,3},{4,68},{68... | collective-permute-start | bytes 104 | tf_op jit(solution)/shard_map/ppermute | solution.py:207
  24.6 10.1 %collective-permute-start.3 = (s32[2,8]{1,0:T(2,128)S(1)}, s32[2,8]{1,0:T(2,128)S(1)}, u32[]{:S(2)}, u32[]{:S(2)}) collective-permute-start(s32[2,8]{1,0:T(2,128)S(1)} %pad_add_fusion), channel_id=1, source_target_pairs={{0,16},{16,0},{1,17},{17,1},{2,18},{18,2},{3,19},{19,3},{4,20},{20... | collective-permute-start | bytes 200 | tf_op jit(solution)/shard_map/ppermute | solution.py:207
  27.9 0.6 copy-start.10
  30.4 18.2 %all-to-all-start = ((bf16[8,2,208,128]{3,2,1,0:T(8,128)(2,1)}), bf16[8,2,208,128]{3,2,1,0:T(8,128)(2,1)S(1)}, u32[]{:S(2)}, u32[]{:S(2)}) async-start(bf16[8,2,208,128]{3,2,1,0:T(8,128)(2,1)} %pair.1), calls=%async_computation | async-start | bytes 1703936 | tf_op jit(solution)/shard_map/all_to_all | solution.py:224
  35.4 16.9 %copy-start.1 = (bf16[1,1,8,128,128]{4,3,2,1,0:T(8,128)(2,1)S(1)}, bf16[1,1,8,128,128]{4,3,2,1,0:T(8,128)(2,1)}, u32[]{:S(2)}) copy-start(bf16[1,1,8,128,128]{4,3,2,1,0:T(8,128)(2,1)} %param.11) | copy-start | bytes 786436
  35.4 13.1 %collective-permute-start.2 = (bf16[8,64,128]{2,1,0:T(8,128)(2,1)S(1)}, bf16[8,64,128]{2,1,0:T(8,128)(2,1)S(1)}, u32[]{:S(2)}, u32[]{:S(2)}) collective-permute-start(bf16[8,64,128]{2,1,0:T(8,128)(2,1)S(1)} %gather_fusion), channel_id=1, source_target_pairs={{0,64},{64,0},{1,65},{65,1},{2,66},{66,2},{3,67},{67,3},{4,68},{68... | collective-permute-start | bytes 393224 | tf_op jit(solution)/shard_map/ppermute | solution.py:207
  39.5 9.0 %collective-permute-start.4 = (bf16[8,64,128]{2,1,0:T(8,128)(2,1)S(1)}, bf16[8,64,128]{2,1,0:T(8,128)(2,1)S(1)}, u32[]{:S(2)}, u32[]{:S(2)}) collective-permute-start(bf16[8,64,128]{2,1,0:T(8,128)(2,1)S(1)} %gather_fusion.1), channel_id=1, source_target_pairs={{0,16},{16,0},{1,17},{17,1},{2,18},{18,2},{3,19},{19,3},{4,20},{20... | collective-permute-start | bytes 393224 | tf_op jit(solution)/shard_map/ppermute | solution.py:207
  44.2 8.1 %collective-permute-start.5 = (bf16[8,64,128]{2,1,0:T(8,128)(2,1)S(1)}, bf16[8,64,128]{2,1,0:T(8,128)(2,1)S(1)}, u32[]{:S(2)}, u32[]{:S(2)}) collective-permute-start(bf16[8,64,128]{2,1,0:T(8,128)(2,1)S(1)} %gather_fusion.2), channel_id=1, source_target_pairs={{0,80},{16,64},{64,16},{80,0},{1,81},{17,65},{65,17},{81,1},{2,82}... | collective-permute-start | bytes 393224 | tf_op jit(solution)/shard_map/ppermute | solution.py:207
  46.3 6.1 %copy-start.4 = (bf16[64,64]{1,0:T(8,128)(2,1)S(1)}, bf16[64,64]{1,0:T(8,128)(2,1)}, u32[]{:S(2)}) copy-start(bf16[64,64]{1,0:T(8,128)(2,1)} %wb_ref.1) | copy-start | bytes 24580
  46.3 6.0 %copy-start.8 = (f32[64]{0:T(128)S(1)}, f32[64]{0:T(128)}, u32[]{:S(2)}) copy-start(f32[64]{0:T(128)} %param.18) | copy-start | bytes 772
  46.3 6.0 %copy-start.2 = (bf16[64,64]{1,0:T(8,128)(2,1)S(1)}, bf16[64,64]{1,0:T(8,128)(2,1)}, u32[]{:S(2)}) copy-start(bf16[64,64]{1,0:T(8,128)(2,1)} %wd_ref.1) | copy-start | bytes 24580
  46.3 6.0 %copy-start.3 = (bf16[64,64]{1,0:T(8,128)(2,1)S(1)}, bf16[64,64]{1,0:T(8,128)(2,1)}, u32[]{:S(2)}) copy-start(bf16[64,64]{1,0:T(8,128)(2,1)} %we_ref.1) | copy-start | bytes 24580
  46.4 5.9 %copy-start.5 = (s32[4]{0:T(128)}, s32[4]{0:T(128)S(1)}, u32[]{:S(2)}) copy-start(s32[4]{0:T(128)S(1)} %pad_add_fusion.1.here_ref) | copy-start | bytes 52
  48.5 15.3 %copy-start = (bf16[8,2,208,128]{3,2,1,0:T(8,128)(2,1)}, bf16[8,2,208,128]{3,2,1,0:T(8,128)(2,1)S(1)}, u32[]{:S(2)}) copy-start(bf16[8,2,208,128]{3,2,1,0:T(8,128)(2,1)S(1)} %all-to-all-done) | copy-start | bytes 2555908
  52.3 0.7 copy-start.6

commit v3 on v2

--- a/solution.py
+++ b/solution.py
@@ -11,23 +11,29 @@
 BAND = 16
 
 
-def pack_kernel(rows_ref, x_ref, shard_ref, spread_ref):
+def pack_kernel(rows_ref, x_ref, shard_ref, spread_ref, both_ref):
     width, shard = x_ref.shape
     block_len = spread_ref.shape[3]
     n_tiles = rows_ref.shape[0]
-    for k in range(shard // block_len):
-        block = x_ref[:, k * block_len:(k + 1) * block_len]
-        shard_ref[k * width:(k + 1) * width, :] = block
-        for n in range(spread_ref.shape[0]):
-            spread_ref[n, k] = block
     sub = lax.broadcasted_iota(jnp.int32, (BAND, block_len), 0)
     band = jnp.full((BAND, block_len), -1, jnp.int32)
     for t in range(n_tiles):
         band = jnp.where(sub == t, rows_ref[t], band)
-    shard_ref[shard // block_len * width:, :] = band.astype(jnp.float32).astype(shard_ref.dtype)
-
-
-def pack(rows, x, block_len, copies):
+    band = band.astype(jnp.float32).astype(shard_ref.dtype)
+    for k in range(shard // block_len):
+        block = x_ref[:, k * block_len:(k + 1) * block_len]
+        at = slice(k * width, (k + 1) * width)
+        shard_ref[at, :] = block
+        for n in range(spread_ref.shape[0]):
+            spread_ref[n, k] = block
+        for n in range(both_ref.shape[0]):
+            both_ref[n, 0, at, :] = block
+    shard_ref[shard // block_len * width:, :] = band
+    for n in range(both_ref.shape[0]):
+        both_ref[n, 0, shard // block_len * width:, :] = band
+
+
+def pack(rows, x, block_len, copies, pairs):
     width, shard = x.shape
     n_blocks = shard // block_len
     vmem = pl.BlockSpec(memory_space=pltpu.VMEM)
@@ -36,32 +42,40 @@
         out_shape=(
             jax.ShapeDtypeStruct((n_blocks * width + BAND, block_len), x.dtype),
             jax.ShapeDtypeStruct((copies, n_blocks, width, block_len), x.dtype),
+            jax.ShapeDtypeStruct((pairs, 2, n_blocks * width + BAND, block_len), x.dtype),
         ),
         in_specs=[pl.BlockSpec(memory_space=pltpu.SMEM), vmem],
-        out_specs=(vmem, vmem),
+        out_specs=(vmem, vmem, vmem),
+        compiler_params=pltpu.CompilerParams(vmem_limit_bytes=4 * 1024 * 1024),
         name="pack",
     )(rows, x)
 
 
-def pair_kernel(own_ref, partner_ref, out_ref):
-    for n in range(out_ref.shape[0]):
-        out_ref[n, 0] = own_ref[...]
-        out_ref[n, 1] = partner_ref[...]
-
-
-def pair(own, partner, copies):
-    vmem = pl.BlockSpec(memory_space=pltpu.VMEM)
+def pair_kernel(partner_ref, half_ref, out_ref, sem):
+    del half_ref
+    copies = [pltpu.make_async_copy(partner_ref, out_ref.at[n, 1], sem.at[n]) for n in range(out_ref.shape[0])]
+    for copy in copies:
+        copy.start()
+    for copy in copies:
+        copy.wait()
+
+
+def pair(partner, half):
+    anywhere = pl.BlockSpec(memory_space=pl.ANY)
     return pl.pallas_call(
         pair_kernel,
-        out_shape=jax.ShapeDtypeStruct((copies, 2) + own.shape, own.dtype),
-        in_specs=[vmem, vmem],
-        out_specs=vmem,
+        out_shape=jax.ShapeDtypeStruct(half.shape, half.dtype),
+        in_specs=[anywhere, anywhere],
+        out_specs=anywhere,
+        scratch_shapes=[pltpu.SemaphoreType.DMA((half.shape[0],))],
+        input_output_aliases={1: 0},
+        compiler_params=pltpu.CompilerParams(vmem_limit_bytes=2 * 1024 * 1024),
         name="pair",
-    )(own, partner)
+    )(partner, half)
 
 
 def tiles_kernel(here_ref, tile_rows_ref, tile_cols_ref, gain_ref, rows_ref, own_ref, got_z_ref, got_y_ref, got_zy_ref, w_ref, wd_ref, we_ref, wb_ref,
-                 out_ref, acc, x_scr, d_scr, e_scr, w_scr, m_scr, lhs_scr, rep_scr, gain_scr):
+                 out_ref, acc, x_scr, d_scr, e_scr, w_scr, lhs_scr, rep_scr):
     n_tiles, block_len, _ = w_ref.shape
     width = wd_ref.shape[0]
     n_blocks = rows_ref.shape[1] // width
@@ -77,11 +91,6 @@
     lane = lax.broadcasted_iota(jnp.int32, (GROUP, span), 1)
     sub = lax.broadcasted_iota(jnp.int32, (GROUP, span), 0)
     own = (lane // CHUNK == sub).astype(f32)
-
-    lane = lax.broadcasted_iota(jnp.int32, (width, width), 1)
-    sub = lax.broadcasted_iota(jnp.int32, (width, width), 0)
-    column = jnp.sum(jnp.where(lane == sub, gain_ref[...], 0.0), axis=1, keepdims=True)
-    gain_scr[...] = jnp.broadcast_to(column, gain_scr.shape)
 
     for t in range(n_tiles):
         at = slice(t * block_len, (t + 1) * block_len)
@@ -104,8 +113,8 @@
         d_scr[t] = d_all[:, at]
         e_scr[t] = e_all[at, :]
         wt = w_ref[t].astype(f32).T
-        m_scr[t] = (wt != 0).astype(f32).astype(bf16)
-        w_scr[t] = half * wt
+        w_scr[t, 0] = jnp.where(wt != 0, half * wt, -1e35)
+        w_scr[t, 1] = jnp.where(wt != 0, -half * wt, -1e35)
         for c in range(n_chunks):
             b_rep = jnp.dot(b_all[:, at], rep_scr[:, c * span:(c + 1) * span], preferred_element_type=f32)
             for g in range(n_groups):
@@ -115,14 +124,15 @@
         owner = tile_rows_ref[t] // n_blocks
         for c in range(n_chunks):
             at = slice(c * CHUNK, (c + 1) * CHUNK)
-            w_c, m_c, e_c = w_scr[t, at, :], m_scr[t, at, :], e_scr[t, at, :]
+            e_c = e_scr[t, at, :]
             for g in range(n_groups):
                 gates = []
                 for k in range(GROUP):
                     f = g * GROUP + k
-                    e_f = e_c[:, f:f + 1].astype(f32)
-                    p = gain_scr[f:f + 1, :] * w_c + d_scr[t, f:f + 1, :] + e_f
-                    gates.append((jnp.tanh(p) + 1.0).astype(bf16) * m_c)
+                    gain = gain_ref[f]
+                    w_f = w_scr[t, (gain < 0).astype(jnp.int32), at, :]
+                    p = jnp.maximum(jnp.abs(gain), 1e-30) * w_f + d_scr[t, f:f + 1, :] + e_c[:, f:f + 1].astype(f32)
+                    gates.append((jnp.tanh(p) + 1.0).astype(bf16))
                 sums = jnp.dot(lhs_scr[t, c, g], jnp.concatenate(gates, axis=0), preferred_element_type=f32)
                 acc[owner, g * GROUP:(g + 1) * GROUP, :] += sums[:GROUP]
                 acc[owner, width + g * GROUP:width + (g + 1) * GROUP, :] += sums[GROUP:]
@@ -140,18 +150,16 @@
     return pl.pallas_call(
         tiles_kernel,
         out_shape=jax.ShapeDtypeStruct((n_owners, 2 * width, block_len), jnp.bfloat16),
-        in_specs=[smem] * 3 + [vmem] * 10,
+        in_specs=[smem] * 4 + [vmem] * 9,
         out_specs=vmem,
         scratch_shapes=[
             pltpu.VMEM((n_owners, 2 * width, block_len), jnp.float32),
             pltpu.VMEM((2, width, n_tiles * block_len), jnp.bfloat16),
             pltpu.VMEM((n_tiles, width, block_len), jnp.float32),
             pltpu.VMEM((n_tiles, block_len, width), jnp.bfloat16),
-            pltpu.VMEM((n_tiles, block_len, block_len), jnp.float32),
-            pltpu.VMEM((n_tiles, block_len, block_len), jnp.bfloat16),
+            pltpu.VMEM((n_tiles, 2, block_len, block_len), jnp.float32),
             pltpu.VMEM((n_tiles, n_chunks, n_groups, 2 * GROUP, GROUP * CHUNK), jnp.bfloat16),
             pltpu.VMEM((block_len, n_chunks * GROUP * CHUNK), jnp.bfloat16),
-            pltpu.VMEM((width, block_len), jnp.float32),
         ],
         compiler_params=pltpu.CompilerParams(vmem_limit_bytes=32 * 1024 * 1024),
         name="tile_sums",
@@ -198,6 +206,7 @@
             whole(x), whole(wa), whole(gain),
         ],
         out_specs=whole(x),
+        compiler_params=pltpu.CompilerParams(vmem_limit_bytes=8 * 1024 * 1024),
         name="finish",
     )(here, parts, rows, x, wa, gain)
 
@@ -216,12 +225,13 @@
     tiles = edge_values.reshape(n_tiles, block_len, block_len)
     here = jnp.stack([lax.axis_index(a) for a in ("zb", "yb", "yhi", SRC)]).astype(jnp.int32)
 
-    shard_rows, copies = pack(rows, x, block_len, n_za * 2)
+    shard_rows, copies, both = pack(rows, x, block_len, n_za * 2, n_x * 2)
     partner = flip(shard_rows, ("yhi",))
     held = lax.all_to_all(copies, ("za", "ya"), 0, 0).reshape(-1, width, block_len)
     cols_z = flip(cols, ("zb",))
-    cols_y, cols_zy = flip(jnp.stack([cols, cols_z]), ("yb",))
-    row_panel = lax.all_to_all(pair(shard_rows, partner, n_x * 2), ("x", "core"), 0, 0)
+    cols_y = flip(cols, ("yb",))
+    cols_zy = flip(cols, ("zb", "yb"))
+    row_panel = lax.all_to_all(pair(partner, both), ("x", "core"), 0, 0)
     row_panel = row_panel.reshape(n_x * 4, -1, block_len)
 
     def pick(names):
@@ -234,7 +244,7 @@
     got_zy = flip(pick(cols_zy), ("zb", "yb"))
 
     parts = tile_sums(
-        here, rows, cols, edge_gain[None], row_panel, held, got_z, got_y, got_zy, tiles, wd, we, wb, n_x * 4
+        here, rows, cols, edge_gain, row_panel, held, got_z, got_y, got_zy, tiles, wd, we, wb, n_x * 4
     )
     parts = lax.all_to_all(parts, SRC, 0, 0)
     return finish(here, parts, row_panel, x, wa, ln_gain[None])

time: 95 us -> 98.4 us (1.036)
  the two profiles are of different devices: /device:TPU:8 before, /device:TPU:17 now
where the time goes in v3:
time: 98.4 us; the launch traced here: 97.8 us
  starting transfers between devices  42.1 us (43%)
  blocking collectives  27.4 us (28%)
  Pallas kernels  14.1 us (14%)
  waiting for transfers between devices  8.63 us (9%)
  local copies, waits for them, and re-layouts  5.15 us (5%)
    all_to_all x1, blocking collectives, local(): parts = lax.all_to_all(parts, SRC, 0, 0)  27.4 us
    ppermute x7, starting transfers between devices, flip(): return lax.ppermute(x, axes, [(i, i ^ last) for i in range(last + 1)])  22.8 us
    all_to_all x1, starting transfers between devices, local(): lax.all_to_all(copies, ('za', 'ya'), 0, 0).reshape(-1, width, block_len)  12.1 us
    pallas_call x1, Pallas kernels, tile_sums(): pl.pallas_call(tiles_kernel, out_shape=jax.ShapeDtypeStruct((n_owners, 2...  9.84 us
    all_to_all x1, starting transfers between devices, local(): row_panel = lax.all_to_all(pair(partner, both), ('x', 'core'), 0, 0)  7.23 us
    ppermute x7, waiting for transfers between devices, flip(): return lax.ppermute(x, axes, [(i, i ^ last) for i in range(last + 1)])  6.44 us
    unnamed x22, local copies, waits for them, and re-layouts  3.43 us
    all_to_all x1, waiting for transfers between devices, local(): row_panel = lax.all_to_all(pair(partner, both), ('x', 'core'), 0, 0)  2.19 us
  transfers between devices with their start and end apart: 9, of which 3 were waited for; matrix products, arithmetic and copies ran while one was open for 2% of the time, Pallas kernels for 1%

profile of v3, /device:TPU:17, one launch (start us, length us, event | category | flops | bytes accessed | tf_op | source)
XLA Modules:
  0.0 97.8 jit_solution(7448645762091702240)
XLA Ops:
  0.0 0.0 copy-start.7
  0.0 0.7 copy-done.7
  0.7 0.0 copy-start.1
  0.7 0.8 copy-done.1
  1.5 1.7 %pack.1 = (bf16[208,128]{1,0:T(8,128)(2,1)S(1)}, bf16[8,3,64,128]{3,2,1,0:T(8,128)(2,1)}, bf16[8,2,208,128]{3,2,1,0:T(8,128)(2,1)}) custom-call(s32[8]{0:T(128)S(1)} %bitcast.17, bf16[64,384]{1,0:T(8,128)(2,1)S(1)} %copy-done.1), custom_call_target="tpu_custom_call" | custom-call | tf_op jit(solution)/shard_map/pack/pallas_call | solution.py:40
  3.2 12.1 %all-to-all-start.1 = ((bf16[8,3,64,128]{3,2,1,0:T(8,128)(2,1)}), bf16[8,3,64,128]{3,2,1,0:T(8,128)(2,1)S(1)}, u32[]{:S(2)}, u32[]{:S(2)}) async-start(bf16[8,3,64,128]{3,2,1,0:T(8,128)(2,1)} %get-tuple-element.10), calls=%async_computation.1 | async-start | bytes 786432 | tf_op jit(solution)/shard_map/all_to_all | solution.py:230
  15.3 0.0 copy-start.9
  15.3 0.7 copy-done.9
  16.0 4.1 %collective-permute-start.5 = (s32[8]{0:T(128)S(1)}, s32[8]{0:T(128)S(1)}, u32[]{:S(2)}, u32[]{:S(2)}) collective-permute-start(s32[8]{0:T(128)S(1)} %bitcast.20), channel_id=1, source_target_pairs={{0,80},{16,64},{64,16},{80,0},{1,81},{17,65},{65,17},{81,1},{2,82}... | collective-permute-start | bytes 104 | tf_op jit(solution)/shard_map/ppermute | solution.py:216
  20.1 2.1 %collective-permute-start.3 = (s32[8]{0:T(128)S(1)}, s32[8]{0:T(128)S(1)}, u32[]{:S(2)}, u32[]{:S(2)}) collective-permute-start(s32[8]{0:T(128)S(1)} %bitcast.21), channel_id=1, source_target_pairs={{0,16},{16,0},{1,17},{17,1},{2,18},{18,2},{3,19},{19,3},{4,20},{20... | collective-permute-start | bytes 104 | tf_op jit(solution)/shard_map/ppermute | solution.py:216
  22.1 2.2 %collective-permute-start.1 = (s32[8]{0:T(128)S(1)}, s32[8]{0:T(128)S(1)}, u32[]{:S(2)}, u32[]{:S(2)}) collective-permute-start(s32[8]{0:T(128)S(1)} %bitcast.22), channel_id=1, source_target_pairs={{0,64},{64,0},{1,65},{65,1},{2,66},{66,2},{3,67},{67,3},{4,68},{68... | collective-permute-start | bytes 104 | tf_op jit(solution)/shard_map/ppermute | solution.py:216
  24.3 5.7 %collective-permute-start = (bf16[208,128]{1,0:T(8,128)(2,1)S(1)}, bf16[208,128]{1,0:T(8,128)(2,1)S(1)}, u32[]{:S(2)}, u32[]{:S(2)}) collective-permute-start(bf16[208,128]{1,0:T(8,128)(2,1)S(1)} %get-tuple-element.8), channel_id=1, source_target_pairs={{0,2},{2,0},{1,3},{3,1},{4,6},{6,4},{5,7},{7,5},{8,10},{10,8},{9,1... | collective-permute-start | bytes 159752 | tf_op jit(solution)/shard_map/ppermute | solution.py:216
  30.0 0.0 collective-permute-done.5
  30.0 3.4 %collective-permute-done.partner_ref = bf16[208,128]{1,0:T(8,128)(2,1)S(1)} collective-permute-done((bf16[208,128]{1,0:T(8,128)(2,1)S(1)}, bf16[208,128]{1,0:T(8,128)(2,1)S(1)}, u32[]{:S(2)}, u32[]{:S(2)}) %collective-permute-start) | collective-permute-done | bytes 53280 | tf_op jit(solution)/shard_map/ppermute | solution.py:216
  33.4 0.8 pair.1
  34.3 0.0 all-to-all-done.1
  34.3 7.2 %all-to-all-start = ((bf16[8,2,208,128]{3,2,1,0:T(8,128)(2,1)}), bf16[8,2,208,128]{3,2,1,0:T(8,128)(2,1)S(1)}, u32[]{:S(2)}, u32[]{:S(2)}) async-start(bf16[8,2,208,128]{3,2,1,0:T(8,128)(2,1)} %pair.1), calls=%async_computation | async-start | bytes 1703936 | tf_op jit(solution)/shard_map/all_to_all | solution.py:234
  41.5 0.0 collective-permute-done.3
  41.6 0.0 collective-permute-done.1
  41.7 0.6 gather_fusion.2
  42.2 0.0 copy-start
  42.2 0.6 gather_fusion.1
  42.8 0.6 gather_fusion
  43.4 3.1 %collective-permute-start.2 = (bf16[8,64,128]{2,1,0:T(8,128)(2,1)S(1)}, bf16[8,64,128]{2,1,0:T(8,128)(2,1)S(1)}, u32[]{:S(2)}, u32[]{:S(2)}) collective-permute-start(bf16[8,64,128]{2,1,0:T(8,128)(2,1)S(1)} %gather_fusion), channel_id=1, source_target_pairs={{0,64},{64,0},{1,65},{65,1},{2,66},{66,2},{3,67},{67,3},{4,68},{68... | collective-permute-start | bytes 393224 | tf_op jit(solution)/shard_map/ppermute | solution.py:216
  46.5 3.8 %collective-permute-start.4 = (bf16[8,64,128]{2,1,0:T(8,128)(2,1)S(1)}, bf16[8,64,128]{2,1,0:T(8,128)(2,1)S(1)}, u32[]{:S(2)}, u32[]{:S(2)}) collective-permute-start(bf16[8,64,128]{2,1,0:T(8,128)(2,1)S(1)} %gather_fusion.1), channel_id=1, source_target_pairs={{0,16},{16,0},{1,17},{17,1},{2,18},{18,2},{3,19},{19,3},{4,20},{20... | collective-permute-start | bytes 393224 | tf_op jit(solution)/shard_map/ppermute | solution.py:216
  50.3 1.9 %collective-permute-start.6 = (bf16[8,64,128]{2,1,0:T(8,128)(2,1)S(1)}, bf16[8,64,128]{2,1,0:T(8,128)(2,1)S(1)}, u32[]{:S(2)}, u32[]{:S(2)}) collective-permute-start(bf16[8,64,128]{2,1,0:T(8,128)(2,1)S(1)} %gather_fusion.2), channel_id=1, source_target_pairs={{0,80},{16,64},{64,16},{80,0},{1,81},{17,65},{65,17},{81,1},{2,82}... | collective-permute-start | bytes 393224 | tf_op jit(solution)/shard_map/ppermute | solution.py:216
  52.2 0.0 copy-start.5
  52.2 0.0 copy-start.3
  52.2 0.0 copy-start.4
  52.3 0.1 pad_add_fusion.here_ref
  52.3 2.2 %all-to-all-done = bf16[8,2,208,128]{3,2,1,0:T(8,128)(2,1)S(1)} async-done(((bf16[8,2,208,128]{3,2,1,0:T(8,128)(2,1)}), bf16[8,2,208,128]{3,2,1,0:T(8,128)(2,1)S(1)}, u32[]{:S(2)}, u32[]{:S(2)}) %all-to-all-start) | async-done | bytes 852000 | tf_op jit(solution)/shard_map/all_to_all | solution.py:234
  54.5 0.0 collective-permute-done.2.got_z_ref
  54.5 0.0 collective-permute-done.4.got_y_ref
  54.5 3.0 %collective-permute-done.6.got_zy_ref = bf16[8,64,128]{2,1,0:T(8,128)(2,1)S(1)} collective-permute-done((bf16[8,64,128]{2,1,0:T(8,128)(2,1)S(1)}, bf16[8,64,128]{2,1,0:T(8,128)(2,1)S(1)}, u32[]{:S(2)}, u32[]{:S(2)}) %collective-permute-start.6) | collective-permute-done | bytes 131104 | tf_op jit(solution)/shard_map/ppermute | solution.py:216
  57.6 0.0 copy-start.10
  57.6 0.0 copy-done
  57.6 0.0 copy-done.5
  57.6 0.0 copy-done.3
  57.6 0.0 copy-done.4
  57.6 0.6 copy-done.10
  58.2 9.8 %tile_sums.1 = bf16[16,128,128]{2,1,0:T(8,128)(2,1)S(1)} custom-call(s32[4]{0:T(128)S(1)} %pad_add_fusion.here_ref, s32[8]{0:T(128)S(1)} %bitcast.18, s32[8]{0:T(128)S(1)} %bitcast.23, f32[64]{0:T(128)S(1)} %copy-done.10, bf16[16,208,128]{2,1,0:T(8,128)(2,1)S(1)} %bitcast.10, bf16[24,64,128]{2,1,0:T(8,128)(2,1)S(1)} %bitcast.15, ...), custom_call_target="tpu_custom_call" | custom-call | tf_op jit(solution)/shard_map/tile_sums/pallas_call | solution.py:150
  68.1 0.0 copy-start.2
  68.1 0.0 copy-start.6
  68.1 27.4 %all_to_all.15.parts_ref = bf16[16,128,128]{2,1,0:T(8,128)(2,1)S(1)} all-to-all(bf16[16,128,128]{2,1,0:T(8,128)(2,1)S(1)} %tile_sums.1), channel_id=1, replica_groups=mesh['za'=4,'zb'=2,'ya'=2,'yb'=2,'x'=4,'yhi'=2,'core'=2] {'x','yhi','core'}, dimensions={0} | all-to-all | bytes 1048576 | tf_op jit(solution)/shard_map/all_to_all | solution.py:249
  95.5 0.0 copy-start.8
  95.5 0.0 copy-done.2
  95.5 0.0 copy-done.6
  95.5 0.6 copy-done.8
  96.1 1.6 %finish.1 = bf16[64,384]{1,0:T(8,128)(2,1)} custom-call(s32[4]{0:T(128)S(1)} %pad_add_fusion.here_ref, bf16[16,128,128]{2,1,0:T(8,128)(2,1)S(1)} %all_to_all.15.parts_ref, bf16[16,208,128]{2,1,0:T(8,128)(2,1)S(1)} %bitcast.11, bf16[64,384]{1,0:T(8,128)(2,1)S(1)} %copy-done.2, bf16[64,64]{1,0:T(8,128)(2,1)S(1)} %copy-done.6, f32[1,64]{1,0:T(1,128)S(1)} %bitcast.19), custom_call_target="tpu_custom_call" | custom-call | tf_op jit(solution)/shard_map/finish/pallas_call | solution.py:198
  (6 shorter events, 0.1 us)
Async XLA Ops:
  0.0 0.7 copy-start.7
  0.7 0.8 copy-start.1
  3.2 31.1 %all-to-all-start.1 = ((bf16[8,3,64,128]{3,2,1,0:T(8,128)(2,1)}), bf16[8,3,64,128]{3,2,1,0:T(8,128)(2,1)S(1)}, u32[]{:S(2)}, u32[]{:S(2)}) async-start(bf16[8,3,64,128]{3,2,1,0:T(8,128)(2,1)} %get-tuple-element.10), calls=%async_computation.1 | async-start | bytes 786432 | tf_op jit(solution)/shard_map/all_to_all | solution.py:230
  15.3 0.7 copy-start.9
  16.0 14.1 %collective-permute-start.5 = (s32[8]{0:T(128)S(1)}, s32[8]{0:T(128)S(1)}, u32[]{:S(2)}, u32[]{:S(2)}) collective-permute-start(s32[8]{0:T(128)S(1)} %bitcast.20), channel_id=1, source_target_pairs={{0,80},{16,64},{64,16},{80,0},{1,81},{17,65},{65,17},{81,1},{2,82}... | collective-permute-start | bytes 104 | tf_op jit(solution)/shard_map/ppermute | solution.py:216
  20.1 21.5 %collective-permute-start.3 = (s32[8]{0:T(128)S(1)}, s32[8]{0:T(128)S(1)}, u32[]{:S(2)}, u32[]{:S(2)}) collective-permute-start(s32[8]{0:T(128)S(1)} %bitcast.21), channel_id=1, source_target_pairs={{0,16},{16,0},{1,17},{17,1},{2,18},{18,2},{3,19},{19,3},{4,20},{20... | collective-permute-start | bytes 104 | tf_op jit(solution)/shard_map/ppermute | solution.py:216
  22.1 19.5 %collective-permute-start.1 = (s32[8]{0:T(128)S(1)}, s32[8]{0:T(128)S(1)}, u32[]{:S(2)}, u32[]{:S(2)}) collective-permute-start(s32[8]{0:T(128)S(1)} %bitcast.22), channel_id=1, source_target_pairs={{0,64},{64,0},{1,65},{65,1},{2,66},{66,2},{3,67},{67,3},{4,68},{68... | collective-permute-start | bytes 104 | tf_op jit(solution)/shard_map/ppermute | solution.py:216
  24.3 9.1 %collective-permute-start = (bf16[208,128]{1,0:T(8,128)(2,1)S(1)}, bf16[208,128]{1,0:T(8,128)(2,1)S(1)}, u32[]{:S(2)}, u32[]{:S(2)}) collective-permute-start(bf16[208,128]{1,0:T(8,128)(2,1)S(1)} %get-tuple-element.8), channel_id=1, source_target_pairs={{0,2},{2,0},{1,3},{3,1},{4,6},{6,4},{5,7},{7,5},{8,10},{10,8},{9,1... | collective-permute-start | bytes 159752 | tf_op jit(solution)/shard_map/ppermute | solution.py:216
  34.3 20.2 %all-to-all-start = ((bf16[8,2,208,128]{3,2,1,0:T(8,128)(2,1)}), bf16[8,2,208,128]{3,2,1,0:T(8,128)(2,1)S(1)}, u32[]{:S(2)}, u32[]{:S(2)}) async-start(bf16[8,2,208,128]{3,2,1,0:T(8,128)(2,1)} %pair.1), calls=%async_computation | async-start | bytes 1703936 | tf_op jit(solution)/shard_map/all_to_all | solution.py:234
  42.2 15.3 %copy-start = (bf16[1,1,8,128,128]{4,3,2,1,0:T(8,128)(2,1)S(1)}, bf16[1,1,8,128,128]{4,3,2,1,0:T(8,128)(2,1)}, u32[]{:S(2)}) copy-start(bf16[1,1,8,128,128]{4,3,2,1,0:T(8,128)(2,1)} %param.11) | copy-start | bytes 786436
  43.4 11.1 %collective-permute-start.2 = (bf16[8,64,128]{2,1,0:T(8,128)(2,1)S(1)}, bf16[8,64,128]{2,1,0:T(8,128)(2,1)S(1)}, u32[]{:S(2)}, u32[]{:S(2)}) collective-permute-start(bf16[8,64,128]{2,1,0:T(8,128)(2,1)S(1)} %gather_fusion), channel_id=1, source_target_pairs={{0,64},{64,0},{1,65},{65,1},{2,66},{66,2},{3,67},{67,3},{4,68},{68... | collective-permute-start | bytes 393224 | tf_op jit(solution)/shard_map/ppermute | solution.py:216
  46.5 8.0 %collective-permute-start.4 = (bf16[8,64,128]{2,1,0:T(8,128)(2,1)S(1)}, bf16[8,64,128]{2,1,0:T(8,128)(2,1)S(1)}, u32[]{:S(2)}, u32[]{:S(2)}) collective-permute-start(bf16[8,64,128]{2,1,0:T(8,128)(2,1)S(1)} %gather_fusion.1), channel_id=1, source_target_pairs={{0,16},{16,0},{1,17},{17,1},{2,18},{18,2},{3,19},{19,3},{4,20},{20... | collective-permute-start | bytes 393224 | tf_op jit(solution)/shard_map/ppermute | solution.py:216
  50.3 7.3 %collective-permute-start.6 = (bf16[8,64,128]{2,1,0:T(8,128)(2,1)S(1)}, bf16[8,64,128]{2,1,0:T(8,128)(2,1)S(1)}, u32[]{:S(2)}, u32[]{:S(2)}) collective-permute-start(bf16[8,64,128]{2,1,0:T(8,128)(2,1)S(1)} %gather_fusion.2), channel_id=1, source_target_pairs={{0,80},{16,64},{64,16},{80,0},{1,81},{17,65},{65,17},{81,1},{2,82}... | collective-permute-start | bytes 393224 | tf_op jit(solution)/shard_map/ppermute | solution.py:216
  52.2 5.4 %copy-start.5 = (bf16[64,64]{1,0:T(8,128)(2,1)S(1)}, bf16[64,64]{1,0:T(8,128)(2,1)}, u32[]{:S(2)}) copy-start(bf16[64,64]{1,0:T(8,128)(2,1)} %wb_ref.1) | copy-start | bytes 24580
  52.2 5.3 %copy-start.3 = (bf16[64,64]{1,0:T(8,128)(2,1)S(1)}, bf16[64,64]{1,0:T(8,128)(2,1)}, u32[]{:S(2)}) copy-start(bf16[64,64]{1,0:T(8,128)(2,1)} %wd_ref.1) | copy-start | bytes 24580
  52.2 5.3 %copy-start.4 = (bf16[64,64]{1,0:T(8,128)(2,1)S(1)}, bf16[64,64]{1,0:T(8,128)(2,1)}, u32[]{:S(2)}) copy-start(bf16[64,64]{1,0:T(8,128)(2,1)} %we_ref.1) | copy-start | bytes 24580
  57.6 0.7 copy-start.10
  68.1 27.4 %copy-start.2 = (bf16[64,384]{1,0:T(8,128)(2,1)S(1)}, bf16[64,384]{1,0:T(8,128)(2,1)}, u32[]{:S(2)}) copy-start(bf16[64,384]{1,0:T(8,128)(2,1)} %x_ref.3) | copy-start | bytes 147460
  68.1 27.4 %copy-start.6 = (bf16[64,64]{1,0:T(8,128)(2,1)S(1)}, bf16[64,64]{1,0:T(8,128)(2,1)}, u32[]{:S(2)}) copy-start(bf16[64,64]{1,0:T(8,128)(2,1)} %wa_ref.1) | copy-start | bytes 24580
  95.5 0.7 copy-start.8

commit v4 on v3

--- a/solution.py
+++ b/solution.py
@@ -46,7 +46,6 @@
         ),
         in_specs=[pl.BlockSpec(memory_space=pltpu.SMEM), vmem],
         out_specs=(vmem, vmem, vmem),
-        compiler_params=pltpu.CompilerParams(vmem_limit_bytes=4 * 1024 * 1024),
         name="pack",
     )(rows, x)
 
@@ -65,11 +64,10 @@
     return pl.pallas_call(
         pair_kernel,
         out_shape=jax.ShapeDtypeStruct(half.shape, half.dtype),
-        in_specs=[anywhere, anywhere],
+        in_specs=[pl.BlockSpec(memory_space=pltpu.VMEM), anywhere],
         out_specs=anywhere,
         scratch_shapes=[pltpu.SemaphoreType.DMA((half.shape[0],))],
         input_output_aliases={1: 0},
-        compiler_params=pltpu.CompilerParams(vmem_limit_bytes=2 * 1024 * 1024),
         name="pair",
     )(partner, half)
 
@@ -206,7 +204,6 @@
             whole(x), whole(wa), whole(gain),
         ],
         out_specs=whole(x),
-        compiler_params=pltpu.CompilerParams(vmem_limit_bytes=8 * 1024 * 1024),
         name="finish",
     )(here, parts, rows, x, wa, gain)
 
@@ -228,9 +225,9 @@
     shard_rows, copies, both = pack(rows, x, block_len, n_za * 2, n_x * 2)
     partner = flip(shard_rows, ("yhi",))
     held = lax.all_to_all(copies, ("za", "ya"), 0, 0).reshape(-1, width, block_len)
-    cols_z = flip(cols, ("zb",))
-    cols_y = flip(cols, ("yb",))
-    cols_zy = flip(cols, ("zb", "yb"))
+    asked, _ = lax.optimization_barrier((cols, shard_rows))
+    cols_z = flip(asked, ("zb",))
+    cols_y, cols_zy = flip(jnp.stack([asked, cols_z]), ("yb",))
     row_panel = lax.all_to_all(pair(partner, both), ("x", "core"), 0, 0)
     row_panel = row_panel.reshape(n_x * 4, -1, block_len)
 

time: 98.4 us -> 93.1 us (0.946)
  the two profiles are of different devices: /device:TPU:17 before, /device:TPU:8 now
where the time goes in v4:
time: 93.1 us; the launch traced here: 92.2 us
  starting transfers between devices  38.2 us (41%)
  blocking collectives  27.7 us (30%)
  Pallas kernels  15.7 us (17%)
  waiting for transfers between devices  7.23 us (8%)
  local copies, waits for them, and re-layouts  2.98 us (3%)
    all_to_all x1, blocking collectives, local(): parts = lax.all_to_all(parts, SRC, 0, 0)  27.7 us
    ppermute x6, starting transfers between devices, flip(): return lax.ppermute(x, axes, [(i, i ^ last) for i in range(last + 1)])  21.4 us
    all_to_all x1, starting transfers between devices, local(): lax.all_to_all(copies, ('za', 'ya'), 0, 0).reshape(-1, width, block_len)  12.5 us
    pallas_call x1, Pallas kernels, tile_sums(): pl.pallas_call(tiles_kernel, out_shape=jax.ShapeDtypeStruct((n_owners, 2...  9.87 us
    ppermute x6, waiting for transfers between devices, flip(): return lax.ppermute(x, axes, [(i, i ^ last) for i in range(last + 1)])  5.14 us
    all_to_all x1, starting transfers between devices, local(): row_panel = lax.all_to_all(pair(partner, both), ('x', 'core'), 0, 0)  4.31 us
    pallas_call x1, Pallas kernels, finish(): pl.pallas_call(finish_kernel, grid=(1,), out_shape=jax.ShapeDtypeStruct(x...  2.16 us
    all_to_all x1, waiting for transfers between devices, local(): row_panel = lax.all_to_all(pair(partner, both), ('x', 'core'), 0, 0)  2.09 us
  transfers between devices with their start and end apart: 8, of which 3 were waited for; matrix products, arithmetic and copies ran while one was open for 2% of the time, Pallas kernels for 2%

profile of v4, /device:TPU:8, one launch (start us, length us, event | category | flops | bytes accessed | tf_op | source)
XLA Modules:
  0.0 92.2 jit_solution(15488511709307533915)
XLA Ops:
  0.0 2.0 %pack.1 = (bf16[208,128]{1,0:T(8,128)(2,1)}, bf16[8,3,64,128]{3,2,1,0:T(8,128)(2,1)}, bf16[8,2,208,128]{3,2,1,0:T(8,128)(2,1)}) custom-call(s32[8]{0:T(128)} %bitcast.65, bf16[64,384]{1,0:T(8,128)(2,1)} %x_ref.3), custom_call_target="tpu_custom_call" | custom-call | tf_op jit(solution)/shard_map/pack/pallas_call | solution.py:40
  2.0 0.0 copy-start.10
  2.0 12.5 %all-to-all-start.1 = ((bf16[8,3,64,128]{3,2,1,0:T(8,128)(2,1)}), bf16[8,3,64,128]{3,2,1,0:T(8,128)(2,1)S(1)}, u32[]{:S(2)}, u32[]{:S(2)}) async-start(bf16[8,3,64,128]{3,2,1,0:T(8,128)(2,1)} %get-tuple-element.11), calls=%async_computation.1 | async-start | bytes 786432 | tf_op jit(solution)/shard_map/all_to_all | solution.py:227
  14.5 0.0 copy-done.10
  14.5 0.0 copy-start.7
  14.5 5.0 %collective-permute-start = (bf16[208,128]{1,0:T(8,128)(2,1)S(1)}, bf16[208,128]{1,0:T(8,128)(2,1)S(1)}, u32[]{:S(2)}, u32[]{:S(2)}) collective-permute-start(bf16[208,128]{1,0:T(8,128)(2,1)S(1)} %copy-done.10), channel_id=1, source_target_pairs={{0,2},{2,0},{1,3},{3,1},{4,6},{6,4},{5,7},{7,5},{8,10},{10,8},{9,1... | collective-permute-start | bytes 159752 | tf_op jit(solution)/shard_map/ppermute | solution.py:213
  19.5 0.0 copy-done.7
  19.5 3.4 %collective-permute-start.1 = (s32[8]{0:T(128)S(1)}, s32[8]{0:T(128)S(1)}, u32[]{:S(2)}, u32[]{:S(2)}) collective-permute-start(s32[8]{0:T(128)S(1)} %bitcast.67), channel_id=1, source_target_pairs={{0,64},{64,0},{1,65},{65,1},{2,66},{66,2},{3,67},{67,3},{4,68},{68... | collective-permute-start | bytes 104 | tf_op jit(solution)/shard_map/ppermute | solution.py:213
  22.9 2.0 %collective-permute-done.1 = s32[8]{0:T(128)S(1)} collective-permute-done((s32[8]{0:T(128)S(1)}, s32[8]{0:T(128)S(1)}, u32[]{:S(2)}, u32[]{:S(2)}) %collective-permute-start.1) | collective-permute-done | bytes 64 | tf_op jit(solution)/shard_map/ppermute | solution.py:213
  25.0 3.3 %collective-permute-start.3 = (s32[2,8]{1,0:T(2,128)S(1)}, s32[2,8]{1,0:T(2,128)S(1)}, u32[]{:S(2)}, u32[]{:S(2)}) collective-permute-start(s32[2,8]{1,0:T(2,128)S(1)} %pad_add_fusion), channel_id=1, source_target_pairs={{0,16},{16,0},{1,17},{17,1},{2,18},{18,2},{3,19},{19,3},{4,20},{20... | collective-permute-start | bytes 200 | tf_op jit(solution)/shard_map/ppermute | solution.py:213
  28.2 0.0 collective-permute-done.partner_ref
  28.2 0.0 copy-start.9
  28.3 0.6 copy-done.9
  28.9 1.7 %pair.1 = bf16[8,2,208,128]{3,2,1,0:T(8,128)(2,1)} custom-call(bf16[208,128]{1,0:T(8,128)(2,1)} %copy-done.9, bf16[8,2,208,128]{3,2,1,0:T(8,128)(2,1)} %get-tuple-element.10.half_ref), custom_call_target="tpu_custom_call", output_to_operand_aliasing={{}: (1, {})} | custom-call | tf_op jit(solution)/shard_map/pair/pallas_call | solution.py:64
  30.5 0.0 all-to-all-done.1
  30.5 4.3 %all-to-all-start = ((bf16[8,2,208,128]{3,2,1,0:T(8,128)(2,1)}), bf16[8,2,208,128]{3,2,1,0:T(8,128)(2,1)S(1)}, u32[]{:S(2)}, u32[]{:S(2)}) async-start(bf16[8,2,208,128]{3,2,1,0:T(8,128)(2,1)} %pair.1), calls=%async_computation | async-start | bytes 1703936 | tf_op jit(solution)/shard_map/all_to_all | solution.py:231
  34.9 0.0 collective-permute-done.3
  35.0 0.6 gather_fusion.1
  35.6 0.0 copy-start.1
  35.6 0.6 gather_fusion.2
  36.1 0.0 copy-start.8
  36.2 0.6 gather_fusion
  36.7 3.4 %collective-permute-start.2 = (bf16[8,64,128]{2,1,0:T(8,128)(2,1)S(1)}, bf16[8,64,128]{2,1,0:T(8,128)(2,1)S(1)}, u32[]{:S(2)}, u32[]{:S(2)}) collective-permute-start(bf16[8,64,128]{2,1,0:T(8,128)(2,1)S(1)} %gather_fusion), channel_id=1, source_target_pairs={{0,64},{64,0},{1,65},{65,1},{2,66},{66,2},{3,67},{67,3},{4,68},{68... | collective-permute-start | bytes 393224 | tf_op jit(solution)/shard_map/ppermute | solution.py:213
  40.1 4.4 %collective-permute-start.5 = (bf16[8,64,128]{2,1,0:T(8,128)(2,1)S(1)}, bf16[8,64,128]{2,1,0:T(8,128)(2,1)S(1)}, u32[]{:S(2)}, u32[]{:S(2)}) collective-permute-start(bf16[8,64,128]{2,1,0:T(8,128)(2,1)S(1)} %gather_fusion.2), channel_id=1, source_target_pairs={{0,80},{16,64},{64,16},{80,0},{1,81},{17,65},{65,17},{81,1},{2,82}... | collective-permute-start | bytes 393224 | tf_op jit(solution)/shard_map/ppermute | solution.py:213
  44.6 1.9 %collective-permute-start.4 = (bf16[8,64,128]{2,1,0:T(8,128)(2,1)S(1)}, bf16[8,64,128]{2,1,0:T(8,128)(2,1)S(1)}, u32[]{:S(2)}, u32[]{:S(2)}) collective-permute-start(bf16[8,64,128]{2,1,0:T(8,128)(2,1)S(1)} %gather_fusion.1), channel_id=1, source_target_pairs={{0,16},{16,0},{1,17},{17,1},{2,18},{18,2},{3,19},{19,3},{4,20},{20... | collective-permute-start | bytes 393224 | tf_op jit(solution)/shard_map/ppermute | solution.py:213
  46.5 0.0 copy-start.4
  46.5 0.0 copy-start.2
  46.5 0.0 copy-start.3
  46.5 0.1 pad_add_fusion.1.here_ref
  46.6 0.0 copy-start.5
  46.6 2.1 %all-to-all-done = bf16[8,2,208,128]{3,2,1,0:T(8,128)(2,1)S(1)} async-done(((bf16[8,2,208,128]{3,2,1,0:T(8,128)(2,1)}), bf16[8,2,208,128]{3,2,1,0:T(8,128)(2,1)S(1)}, u32[]{:S(2)}, u32[]{:S(2)}) %all-to-all-start) | async-done | bytes 852000 | tf_op jit(solution)/shard_map/all_to_all | solution.py:231
  48.7 0.0 copy-start
  48.7 0.0 collective-permute-done.2.got_z_ref
  48.7 0.0 collective-permute-done.5.got_zy_ref
  48.7 3.1 %collective-permute-done.4.got_y_ref = bf16[8,64,128]{2,1,0:T(8,128)(2,1)S(1)} collective-permute-done((bf16[8,64,128]{2,1,0:T(8,128)(2,1)S(1)}, bf16[8,64,128]{2,1,0:T(8,128)(2,1)S(1)}, u32[]{:S(2)}, u32[]{:S(2)}) %collective-permute-start.4) | collective-permute-done | bytes 131104 | tf_op jit(solution)/shard_map/ppermute | solution.py:213
  51.8 0.0 copy-start.6
  51.8 0.0 copy-done.5
  51.8 0.0 copy-done.1
  51.8 0.0 copy-done.8
  51.8 0.0 copy-done.4
  51.8 0.0 copy-done.2
  51.8 0.0 copy-done.3
  51.8 0.6 copy-done.6
  52.5 9.9 %tile_sums.1 = bf16[16,128,128]{2,1,0:T(8,128)(2,1)S(1)} custom-call(s32[4]{0:T(128)S(1)} %pad_add_fusion.1.here_ref, s32[8]{0:T(128)S(1)} %bitcast.66, s32[8]{0:T(128)S(1)} %bitcast.69, f32[64]{0:T(128)S(1)} %copy-done.8, bf16[16,208,128]{2,1,0:T(8,128)(2,1)S(1)} %bitcast.58, bf16[24,64,128]{2,1,0:T(8,128)(2,1)S(1)} %bitcast.63, ...), custom_call_target="tpu_custom_call" | custom-call | tf_op jit(solution)/shard_map/tile_sums/pallas_call | solution.py:148
  62.3 0.0 copy-done
  62.3 27.7 %all_to_all.15.parts_ref = bf16[16,128,128]{2,1,0:T(8,128)(2,1)} all-to-all(bf16[16,128,128]{2,1,0:T(8,128)(2,1)S(1)} %tile_sums.1), channel_id=1, replica_groups=mesh['za'=4,'zb'=2,'ya'=2,'yb'=2,'x'=4,'yhi'=2,'core'=2] {'x','yhi','core'}, dimensions={0} | all-to-all | bytes 1048576 | tf_op jit(solution)/shard_map/all_to_all | solution.py:246
  90.1 2.2 %finish.1 = bf16[64,384]{1,0:T(8,128)(2,1)} custom-call(s32[4]{0:T(128)} %copy-done.5, bf16[16,128,128]{2,1,0:T(8,128)(2,1)} %all_to_all.15.parts_ref, bf16[16,208,128]{2,1,0:T(8,128)(2,1)} %bitcast.59, bf16[64,384]{1,0:T(8,128)(2,1)} %x_ref.3, bf16[64,64]{1,0:T(8,128)(2,1)} %wa_ref.1, f32[1,64]{1,0:T(1,128)} %bitcast.70), custom_call_target="tpu_custom_call" | custom-call | tf_op jit(solution)/shard_map/finish/pallas_call | solution.py:196
  (6 shorter events, 0.1 us)
Async XLA Ops:
  2.0 12.5 %copy-start.10 = (bf16[208,128]{1,0:T(8,128)(2,1)S(1)}, bf16[208,128]{1,0:T(8,128)(2,1)}, u32[]{:S(2)}) copy-start(bf16[208,128]{1,0:T(8,128)(2,1)} %get-tuple-element.9) | copy-start | bytes 159748
  2.0 28.5 %all-to-all-start.1 = ((bf16[8,3,64,128]{3,2,1,0:T(8,128)(2,1)}), bf16[8,3,64,128]{3,2,1,0:T(8,128)(2,1)S(1)}, u32[]{:S(2)}, u32[]{:S(2)}) async-start(bf16[8,3,64,128]{3,2,1,0:T(8,128)(2,1)} %get-tuple-element.11), calls=%async_computation.1 | async-start | bytes 786432 | tf_op jit(solution)/shard_map/all_to_all | solution.py:227
  14.5 5.1 %copy-start.7 = (s32[1,1,8]{2,1,0:T(1,128)S(1)}, s32[1,1,8]{2,1,0:T(1,128)}, u32[]{:S(2)}) copy-start(s32[1,1,8]{2,1,0:T(1,128)} %param.13) | copy-start | bytes 100
  14.5 13.8 %collective-permute-start = (bf16[208,128]{1,0:T(8,128)(2,1)S(1)}, bf16[208,128]{1,0:T(8,128)(2,1)S(1)}, u32[]{:S(2)}, u32[]{:S(2)}) collective-permute-start(bf16[208,128]{1,0:T(8,128)(2,1)S(1)} %copy-done.10), channel_id=1, source_target_pairs={{0,2},{2,0},{1,3},{3,1},{4,6},{6,4},{5,7},{7,5},{8,10},{10,8},{9,1... | collective-permute-start | bytes 159752 | tf_op jit(solution)/shard_map/ppermute | solution.py:213
  19.5 5.4 %collective-permute-start.1 = (s32[8]{0:T(128)S(1)}, s32[8]{0:T(128)S(1)}, u32[]{:S(2)}, u32[]{:S(2)}) collective-permute-start(s32[8]{0:T(128)S(1)} %bitcast.67), channel_id=1, source_target_pairs={{0,64},{64,0},{1,65},{65,1},{2,66},{66,2},{3,67},{67,3},{4,68},{68... | collective-permute-start | bytes 104 | tf_op jit(solution)/shard_map/ppermute | solution.py:213
  25.0 9.9 %collective-permute-start.3 = (s32[2,8]{1,0:T(2,128)S(1)}, s32[2,8]{1,0:T(2,128)S(1)}, u32[]{:S(2)}, u32[]{:S(2)}) collective-permute-start(s32[2,8]{1,0:T(2,128)S(1)} %pad_add_fusion), channel_id=1, source_target_pairs={{0,16},{16,0},{1,17},{17,1},{2,18},{18,2},{3,19},{19,3},{4,20},{20... | collective-permute-start | bytes 200 | tf_op jit(solution)/shard_map/ppermute | solution.py:213
  28.2 0.6 copy-start.9
  30.5 18.2 %all-to-all-start = ((bf16[8,2,208,128]{3,2,1,0:T(8,128)(2,1)}), bf16[8,2,208,128]{3,2,1,0:T(8,128)(2,1)S(1)}, u32[]{:S(2)}, u32[]{:S(2)}) async-start(bf16[8,2,208,128]{3,2,1,0:T(8,128)(2,1)} %pair.1), calls=%async_computation | async-start | bytes 1703936 | tf_op jit(solution)/shard_map/all_to_all | solution.py:231
  35.6 16.3 %copy-start.1 = (bf16[1,1,8,128,128]{4,3,2,1,0:T(8,128)(2,1)S(1)}, bf16[1,1,8,128,128]{4,3,2,1,0:T(8,128)(2,1)}, u32[]{:S(2)}) copy-start(bf16[1,1,8,128,128]{4,3,2,1,0:T(8,128)(2,1)} %param.11) | copy-start | bytes 786436
  36.1 15.7 %copy-start.8 = (f32[64]{0:T(128)S(1)}, f32[64]{0:T(128)}, u32[]{:S(2)}) copy-start(f32[64]{0:T(128)} %gain_ref.1) | copy-start | bytes 772
  36.7 12.0 %collective-permute-start.2 = (bf16[8,64,128]{2,1,0:T(8,128)(2,1)S(1)}, bf16[8,64,128]{2,1,0:T(8,128)(2,1)S(1)}, u32[]{:S(2)}, u32[]{:S(2)}) collective-permute-start(bf16[8,64,128]{2,1,0:T(8,128)(2,1)S(1)} %gather_fusion), channel_id=1, source_target_pairs={{0,64},{64,0},{1,65},{65,1},{2,66},{66,2},{3,67},{67,3},{4,68},{68... | collective-permute-start | bytes 393224 | tf_op jit(solution)/shard_map/ppermute | solution.py:213
  40.1 8.6 %collective-permute-start.5 = (bf16[8,64,128]{2,1,0:T(8,128)(2,1)S(1)}, bf16[8,64,128]{2,1,0:T(8,128)(2,1)S(1)}, u32[]{:S(2)}, u32[]{:S(2)}) collective-permute-start(bf16[8,64,128]{2,1,0:T(8,128)(2,1)S(1)} %gather_fusion.2), channel_id=1, source_target_pairs={{0,80},{16,64},{64,16},{80,0},{1,81},{17,65},{65,17},{81,1},{2,82}... | collective-permute-start | bytes 393224 | tf_op jit(solution)/shard_map/ppermute | solution.py:213
  44.6 7.2 %collective-permute-start.4 = (bf16[8,64,128]{2,1,0:T(8,128)(2,1)S(1)}, bf16[8,64,128]{2,1,0:T(8,128)(2,1)S(1)}, u32[]{:S(2)}, u32[]{:S(2)}) collective-permute-start(bf16[8,64,128]{2,1,0:T(8,128)(2,1)S(1)} %gather_fusion.1), channel_id=1, source_target_pairs={{0,16},{16,0},{1,17},{17,1},{2,18},{18,2},{3,19},{19,3},{4,20},{20... | collective-permute-start | bytes 393224 | tf_op jit(solution)/shard_map/ppermute | solution.py:213
  46.5 5.3 %copy-start.4 = (bf16[64,64]{1,0:T(8,128)(2,1)S(1)}, bf16[64,64]{1,0:T(8,128)(2,1)}, u32[]{:S(2)}) copy-start(bf16[64,64]{1,0:T(8,128)(2,1)} %wb_ref.1) | copy-start | bytes 24580
  46.5 5.3 %copy-start.2 = (bf16[64,64]{1,0:T(8,128)(2,1)S(1)}, bf16[64,64]{1,0:T(8,128)(2,1)}, u32[]{:S(2)}) copy-start(bf16[64,64]{1,0:T(8,128)(2,1)} %wd_ref.1) | copy-start | bytes 24580
  46.5 5.3 %copy-start.3 = (bf16[64,64]{1,0:T(8,128)(2,1)S(1)}, bf16[64,64]{1,0:T(8,128)(2,1)}, u32[]{:S(2)}) copy-start(bf16[64,64]{1,0:T(8,128)(2,1)} %we_ref.1) | copy-start | bytes 24580
  46.6 5.2 %copy-start.5 = (s32[4]{0:T(128)}, s32[4]{0:T(128)S(1)}, u32[]{:S(2)}) copy-start(s32[4]{0:T(128)S(1)} %pad_add_fusion.1.here_ref) | copy-start | bytes 52
  48.7 13.6 %copy-start = (bf16[8,2,208,128]{3,2,1,0:T(8,128)(2,1)}, bf16[8,2,208,128]{3,2,1,0:T(8,128)(2,1)S(1)}, u32[]{:S(2)}) copy-start(bf16[8,2,208,128]{3,2,1,0:T(8,128)(2,1)S(1)} %all-to-all-done) | copy-start | bytes 2555908
  51.8 0.7 copy-start.6

commit v5 on v4

--- a/solution.py
+++ b/solution.py
@@ -1,3 +1,5 @@
+import functools
+
 import jax, jax.numpy as jnp
 from jax import lax
 from jax.sharding import Mesh, PartitionSpec as P
@@ -120,6 +122,7 @@
 
     def tile(t, _):
         owner = tile_rows_ref[t] // n_blocks
+        slot = (owner // 4 * 2 + owner % 2) * 2 + ((owner // 2 % 2) ^ here_ref[2])
         for c in range(n_chunks):
             at = slice(c * CHUNK, (c + 1) * CHUNK)
             e_c = e_scr[t, at, :]
@@ -132,8 +135,8 @@
                     p = jnp.maximum(jnp.abs(gain), 1e-30) * w_f + d_scr[t, f:f + 1, :] + e_c[:, f:f + 1].astype(f32)
                     gates.append((jnp.tanh(p) + 1.0).astype(bf16))
                 sums = jnp.dot(lhs_scr[t, c, g], jnp.concatenate(gates, axis=0), preferred_element_type=f32)
-                acc[owner, g * GROUP:(g + 1) * GROUP, :] += sums[:GROUP]
-                acc[owner, width + g * GROUP:width + (g + 1) * GROUP, :] += sums[GROUP:]
+                acc[slot, g * GROUP:(g + 1) * GROUP, :] += sums[:GROUP]
+                acc[slot, width + g * GROUP:width + (g + 1) * GROUP, :] += sums[GROUP:]
         return 0
     lax.fori_loop(0, n_tiles, tile, 0)
     out_ref[...] = (half * acc[...]).astype(out_ref.dtype)
@@ -164,48 +167,99 @@
     )(here, tile_rows, tile_cols, gain, rows, own, got_z, got_y, got_zy, w, wd, we, wb)
 
 
-def finish_kernel(here_ref, parts_ref, band_ref, x_ref, wa_ref, gain_ref, out_ref):
+def sums_kernel(flipped, here_ref, parts_ref, band_ref, out_ref):
+    n_senders = parts_ref.shape[0]
+    n_blocks = out_ref.shape[0]
+    f32 = jnp.float32
+    first = ((here_ref[3] ^ flipped) * n_blocks).astype(f32)
+    named = [band_ref[s, 0].astype(f32) for s in range(n_senders)]
+    for k in range(n_blocks):
+        total = jnp.zeros(out_ref.shape[1:], f32)
+        for s in range(n_senders):
+            hit = jnp.max((named[s] == first + float(k)).astype(f32), axis=0, keepdims=True)
+            total += parts_ref[s, 0].astype(f32) * hit
+        out_ref[k] = total.astype(out_ref.dtype)
+
+
+def own_kernel(here_ref, parts_ref, band_ref, x_ref, wa_ref, gain_ref, out_ref, proj_ref, gains_ref):
     width = wa_ref.shape[0]
-    n_src, _, block_len = parts_ref.shape
-    n_blocks = x_ref.shape[1] // block_len
-    f32 = jnp.float32
     lane = lax.broadcasted_iota(jnp.int32, (width, width), 1)
     sub = lax.broadcasted_iota(jnp.int32, (width, width), 0)
     gain = jnp.sum(jnp.where(lane == sub, gain_ref[...], 0.0), axis=1, keepdims=True)
-    first = (here_ref[3] * n_blocks).astype(f32)
-    named = [band_ref[(s // 4 * 2 + s % 2) * 2 + ((s // 2 % 2) ^ here_ref[2])].astype(f32) for s in range(n_src)]
+    gains_ref[...] = jnp.broadcast_to(gain, gains_ref.shape)
+    proj_ref[...] = jnp.dot(wa_ref[...], x_ref[...], preferred_element_type=jnp.float32)
+    sums_kernel(0, here_ref, parts_ref, band_ref, out_ref)
+
+
+def whole(shape):
+    return pl.BlockSpec(shape, lambda i: (0,) * len(shape))
+
+
+def sums_specs(parts, panel, side):
+    n, _, depth, block_len = parts.shape
+    return [
+        pl.BlockSpec(memory_space=pltpu.SMEM),
+        pl.BlockSpec((n, 1, depth, block_len), lambda i: (0, side, 0, 0)),
+        pl.BlockSpec((n, 1, BAND, block_len), lambda i: (0, 0, panel.shape[2] // BAND - 1, 0)),
+    ]
+
+
+GRANT = pltpu.CompilerParams(vmem_limit_bytes=4 * 1024 * 1024)
+
+
+def far_sums(here, parts, panel, n_blocks):
+    shape = (n_blocks,) + parts.shape[2:]
+    return pl.pallas_call(
+        functools.partial(sums_kernel, 2),
+        grid=(1,),
+        out_shape=jax.ShapeDtypeStruct(shape, jnp.bfloat16),
+        in_specs=sums_specs(parts, panel, 1),
+        out_specs=whole(shape),
+        compiler_params=GRANT,
+        name="far_sums",
+    )(here, parts, panel)
+
+
+def own_sums(here, parts, panel, x, wa, gain):
+    width, shard = x.shape
+    shape = (shard // parts.shape[3],) + parts.shape[2:]
+    shapes = (shape, x.shape, (width, parts.shape[3]))
+    return pl.pallas_call(
+        own_kernel,
+        grid=(1,),
+        out_shape=tuple(jax.ShapeDtypeStruct(a, jnp.float32) for a in shapes),
+        in_specs=sums_specs(parts, panel, 0) + [whole(x.shape), whole(wa.shape), whole(gain.shape)],
+        out_specs=tuple(whole(a) for a in shapes),
+        compiler_params=GRANT,
+        name="own_sums",
+    )(here, parts, panel, x, wa, gain)
+
+
+def finish_kernel(got_ref, own_ref, proj_ref, gains_ref, x_ref, out_ref):
+    width = x_ref.shape[0]
+    n_blocks, _, block_len = own_ref.shape
+    f32 = jnp.float32
     for k in range(n_blocks):
-        num = jnp.zeros((width, block_len), f32)
-        den = jnp.zeros((width, block_len), f32)
-        for s in range(n_src):
-            hit = jnp.max((named[s] == first + float(k)).astype(f32), axis=0, keepdims=True)
-            num += parts_ref[s, :width, :].astype(f32) * hit
-            den += parts_ref[s, width:, :].astype(f32) * hit
-        x = x_ref[:, k * block_len:(k + 1) * block_len]
-        a = jnp.dot(wa_ref[...], x, preferred_element_type=f32)
-        mixed = a + num / (den + 1e-6)
+        at = slice(k * block_len, (k + 1) * block_len)
+        num = own_ref[k, :width, :] + got_ref[k, :width, :].astype(f32)
+        den = own_ref[k, width:, :] + got_ref[k, width:, :].astype(f32)
+        mixed = proj_ref[:, at] + num / (den + 1e-6)
         center = mixed - jnp.mean(mixed, axis=0, keepdims=True)
         spread = jnp.mean(center * center, axis=0, keepdims=True)
-        normed = center * lax.rsqrt(spread + 1e-5) * gain
-        out_ref[:, k * block_len:(k + 1) * block_len] = (x.astype(f32) + jnp.maximum(normed, 0.0)).astype(jnp.bfloat16)
-
-
-def finish(here, parts, rows, x, wa, gain):
-    whole = lambda a: pl.BlockSpec(a.shape, lambda i: (0,) * a.ndim)
-    n, depth, block_len = rows.shape
+        normed = center * lax.rsqrt(spread + 1e-5) * gains_ref[...]
+        out_ref[:, at] = (x_ref[:, at].astype(f32) + jnp.maximum(normed, 0.0)).astype(jnp.bfloat16)
+
+
+def finish(got, own, proj, gains, x):
+    vmem = pl.BlockSpec(memory_space=pltpu.VMEM)
     return pl.pallas_call(
         finish_kernel,
-        grid=(1,),
         out_shape=jax.ShapeDtypeStruct(x.shape, jnp.bfloat16),
-        in_specs=[
-            pl.BlockSpec(memory_space=pltpu.SMEM),
-            whole(parts),
-            pl.BlockSpec((n, BAND, block_len), lambda i: (0, depth // BAND - 1, 0)),
-            whole(x), whole(wa), whole(gain),
-        ],
-        out_specs=whole(x),
+        in_specs=[vmem] * 5,
+        out_specs=vmem,
+        compiler_params=GRANT,
         name="finish",
-    )(here, parts, rows, x, wa, gain)
+    )(got, own, proj, gains, x)
 
 
 def flip(x, axes):
@@ -243,8 +297,10 @@
     parts = tile_sums(
         here, rows, cols, edge_gain, row_panel, held, got_z, got_y, got_zy, tiles, wd, we, wb, n_x * 4
     )
-    parts = lax.all_to_all(parts, SRC, 0, 0)
-    return finish(here, parts, row_panel, x, wa, ln_gain[None])
+    parts = lax.all_to_all(parts.reshape((n_x * 2, 2) + parts.shape[1:]), ("x", "core"), 0, 0)
+    panel = row_panel.reshape((n_x * 2, 2) + row_panel.shape[1:])
+    got = flip(far_sums(here, parts, panel, n_blocks), ("yhi",))
+    return finish(got, *own_sums(here, parts, panel, x, wa, ln_gain[None]), x)
 
 
 def solution(mesh):

time: 93.1 us -> 91.2 us (0.980)
  blocking collectives: 27.7 us -> 14.6 us
  starting transfers between devices: 38.2 us -> 44.2 us
  waiting for transfers between devices: 7.23 us -> 12.6 us
    all_to_all x1, blocking collectives: 27.7 us -> 14.6 us  [local(): lax.all_to_all(parts.reshape((n_x * 2, 2) + parts.shape[1:]), ('x', 'core...]
    ppermute x6 -> x7, starting transfers between devices: 21.4 us -> 27.4 us  [flip(): return lax.ppermute(x, axes, [(i, i ^ last) for i in range(last + 1)])]
    ppermute x6 -> x7, waiting for transfers between devices: 5.14 us -> 10.5 us  [flip(): return lax.ppermute(x, axes, [(i, i ^ last) for i in range(last + 1)])]
    pallas_call x1 -> x3, Pallas kernels: 2.16 us -> 2.23 us  [the longest x1 0.78 us: own_sums(): pl.pallas_call(own_kernel, grid=(1,), out_shape=tuple((jax.ShapeDtypeStru...]
  transfers between devices with their start and end apart: 8 -> 9, of which waited for: 3 -> 4; matrix products, arithmetic and copies ran while one was open for 2% -> 2% of each run, Pallas kernels for 2% -> 3%
where the time goes in v5:
time: 91.2 us; the launch traced here: 90.6 us
  starting transfers between devices  44.2 us (48%)
  Pallas kernels  15.8 us (17%)
  blocking collectives  14.6 us (16%)
  waiting for transfers between devices  12.6 us (14%)
  local copies, waits for them, and re-layouts  3 us (3%)
    ppermute x7, starting transfers between devices, flip(): return lax.ppermute(x, axes, [(i, i ^ last) for i in range(last + 1)])  27.4 us
    all_to_all x1, blocking collectives, local(): lax.all_to_all(parts.reshape((n_x * 2, 2) + parts.shape[1:]), ('x', 'core...  14.6 us
    all_to_all x1, starting transfers between devices, local(): lax.all_to_all(copies, ('za', 'ya'), 0, 0).reshape(-1, width, block_len)  12.5 us
    ppermute x7, waiting for transfers between devices, flip(): return lax.ppermute(x, axes, [(i, i ^ last) for i in range(last + 1)])  10.5 us
    pallas_call x1, Pallas kernels, tile_sums(): pl.pallas_call(tiles_kernel, out_shape=jax.ShapeDtypeStruct((n_owners, 2...  9.87 us
    all_to_all x1, starting transfers between devices, local(): row_panel = lax.all_to_all(pair(partner, both), ('x', 'core'), 0, 0)  4.31 us
    all_to_all x1, waiting for transfers between devices, local(): row_panel = lax.all_to_all(pair(partner, both), ('x', 'core'), 0, 0)  2.11 us
    pallas_call x1, Pallas kernels, pack(): pl.pallas_call(pack_kernel, out_shape=(jax.ShapeDtypeStruct((n_blocks * w...  1.99 us
  transfers between devices with their start and end apart: 9, of which 4 were waited for; matrix products, arithmetic and copies ran while one was open for 2% of the time, Pallas kernels for 3%

profile of v5, /device:TPU:8, one launch (start us, length us, event | category | flops | bytes accessed | tf_op | source)
XLA Modules:
  0.0 90.6 jit_solution(13792884375856241554)
XLA Ops:
  0.0 2.0 %pack.1 = (bf16[208,128]{1,0:T(8,128)(2,1)}, bf16[8,3,64,128]{3,2,1,0:T(8,128)(2,1)}, bf16[8,2,208,128]{3,2,1,0:T(8,128)(2,1)}) custom-call(s32[8]{0:T(128)} %bitcast.66, bf16[64,384]{1,0:T(8,128)(2,1)} %x_ref.5), custom_call_target="tpu_custom_call" | custom-call | tf_op jit(solution)/shard_map/pack/pallas_call | solution.py:42
  2.0 0.0 copy-start.11
  2.0 12.5 %all-to-all-start.1 = ((bf16[8,3,64,128]{3,2,1,0:T(8,128)(2,1)}), bf16[8,3,64,128]{3,2,1,0:T(8,128)(2,1)S(1)}, u32[]{:S(2)}, u32[]{:S(2)}) async-start(bf16[8,3,64,128]{3,2,1,0:T(8,128)(2,1)} %get-tuple-element.14), calls=%async_computation.1 | async-start | bytes 786432 | tf_op jit(solution)/shard_map/all_to_all | solution.py:281
  14.5 0.0 copy-done.11
  14.5 0.0 copy-start.7
  14.5 5.0 %collective-permute-start = (bf16[208,128]{1,0:T(8,128)(2,1)S(1)}, bf16[208,128]{1,0:T(8,128)(2,1)S(1)}, u32[]{:S(2)}, u32[]{:S(2)}) collective-permute-start(bf16[208,128]{1,0:T(8,128)(2,1)S(1)} %copy-done.11), channel_id=1, source_target_pairs={{0,2},{2,0},{1,3},{3,1},{4,6},{6,4},{5,7},{7,5},{8,10},{10,8},{9,1... | collective-permute-start | bytes 159752 | tf_op jit(solution)/shard_map/ppermute | solution.py:267
  19.5 0.0 copy-done.7
  19.5 3.4 %collective-permute-start.1 = (s32[8]{0:T(128)S(1)}, s32[8]{0:T(128)S(1)}, u32[]{:S(2)}, u32[]{:S(2)}) collective-permute-start(s32[8]{0:T(128)S(1)} %bitcast.68), channel_id=1, source_target_pairs={{0,64},{64,0},{1,65},{65,1},{2,66},{66,2},{3,67},{67,3},{4,68},{68... | collective-permute-start | bytes 104 | tf_op jit(solution)/shard_map/ppermute | solution.py:267
  22.9 2.0 %collective-permute-done.1 = s32[8]{0:T(128)S(1)} collective-permute-done((s32[8]{0:T(128)S(1)}, s32[8]{0:T(128)S(1)}, u32[]{:S(2)}, u32[]{:S(2)}) %collective-permute-start.1) | collective-permute-done | bytes 64 | tf_op jit(solution)/shard_map/ppermute | solution.py:267
  25.0 3.3 %collective-permute-start.3 = (s32[2,8]{1,0:T(2,128)S(1)}, s32[2,8]{1,0:T(2,128)S(1)}, u32[]{:S(2)}, u32[]{:S(2)}) collective-permute-start(s32[2,8]{1,0:T(2,128)S(1)} %pad_add_fusion), channel_id=1, source_target_pairs={{0,16},{16,0},{1,17},{17,1},{2,18},{18,2},{3,19},{19,3},{4,20},{20... | collective-permute-start | bytes 200 | tf_op jit(solution)/shard_map/ppermute | solution.py:267
  28.2 0.0 collective-permute-done.partner_ref
  28.2 0.0 copy-start.10
  28.2 0.6 copy-done.10
  28.9 1.7 %pair.1 = bf16[8,2,208,128]{3,2,1,0:T(8,128)(2,1)} custom-call(bf16[208,128]{1,0:T(8,128)(2,1)} %copy-done.10, bf16[8,2,208,128]{3,2,1,0:T(8,128)(2,1)} %get-tuple-element.13.half_ref), custom_call_target="tpu_custom_call", output_to_operand_aliasing={{}: (1, {})} | custom-call | tf_op jit(solution)/shard_map/pair/pallas_call | solution.py:66
  30.5 0.0 all-to-all-done.1
  30.5 4.3 %all-to-all-start = ((bf16[8,2,208,128]{3,2,1,0:T(8,128)(2,1)}), bf16[8,2,208,128]{3,2,1,0:T(8,128)(2,1)S(1)}, u32[]{:S(2)}, u32[]{:S(2)}) async-start(bf16[8,2,208,128]{3,2,1,0:T(8,128)(2,1)} %pair.1), calls=%async_computation | async-start | bytes 1703936 | tf_op jit(solution)/shard_map/all_to_all | solution.py:285
  34.9 0.0 collective-permute-done.3
  35.0 0.6 gather_fusion.1
  35.6 0.0 copy-start.1
  35.6 0.6 gather_fusion.2
  36.1 0.0 copy-start.9
  36.2 0.6 gather_fusion
  36.7 3.4 %collective-permute-start.2 = (bf16[8,64,128]{2,1,0:T(8,128)(2,1)S(1)}, bf16[8,64,128]{2,1,0:T(8,128)(2,1)S(1)}, u32[]{:S(2)}, u32[]{:S(2)}) collective-permute-start(bf16[8,64,128]{2,1,0:T(8,128)(2,1)S(1)} %gather_fusion), channel_id=1, source_target_pairs={{0,64},{64,0},{1,65},{65,1},{2,66},{66,2},{3,67},{67,3},{4,68},{68... | collective-permute-start | bytes 393224 | tf_op jit(solution)/shard_map/ppermute | solution.py:267
  40.1 4.4 %collective-permute-start.5 = (bf16[8,64,128]{2,1,0:T(8,128)(2,1)S(1)}, bf16[8,64,128]{2,1,0:T(8,128)(2,1)S(1)}, u32[]{:S(2)}, u32[]{:S(2)}) collective-permute-start(bf16[8,64,128]{2,1,0:T(8,128)(2,1)S(1)} %gather_fusion.2), channel_id=1, source_target_pairs={{0,80},{16,64},{64,16},{80,0},{1,81},{17,65},{65,17},{81,1},{2,82}... | collective-permute-start | bytes 393224 | tf_op jit(solution)/shard_map/ppermute | solution.py:267
  44.6 1.9 %collective-permute-start.4 = (bf16[8,64,128]{2,1,0:T(8,128)(2,1)S(1)}, bf16[8,64,128]{2,1,0:T(8,128)(2,1)S(1)}, u32[]{:S(2)}, u32[]{:S(2)}) collective-permute-start(bf16[8,64,128]{2,1,0:T(8,128)(2,1)S(1)} %gather_fusion.1), channel_id=1, source_target_pairs={{0,16},{16,0},{1,17},{17,1},{2,18},{18,2},{3,19},{19,3},{4,20},{20... | collective-permute-start | bytes 393224 | tf_op jit(solution)/shard_map/ppermute | solution.py:267
  46.5 0.0 copy-start.4
  46.5 0.0 copy-start.2
  46.5 0.0 copy-start.3
  46.5 0.1 pad_add_fusion.1.here_ref
  46.6 2.1 %all-to-all-done.band_ref = bf16[8,2,208,128]{3,2,1,0:T(8,128)(2,1)S(1)} async-done(((bf16[8,2,208,128]{3,2,1,0:T(8,128)(2,1)}), bf16[8,2,208,128]{3,2,1,0:T(8,128)(2,1)S(1)}, u32[]{:S(2)}, u32[]{:S(2)}) %all-to-all-start) | async-done | bytes 852000 | tf_op jit(solution)/shard_map/all_to_all | solution.py:285
  48.7 0.0 collective-permute-done.2.got_z_ref
  48.7 0.0 collective-permute-done.5.got_zy_ref
  48.7 3.1 %collective-permute-done.4.got_y_ref = bf16[8,64,128]{2,1,0:T(8,128)(2,1)S(1)} collective-permute-done((bf16[8,64,128]{2,1,0:T(8,128)(2,1)S(1)}, bf16[8,64,128]{2,1,0:T(8,128)(2,1)S(1)}, u32[]{:S(2)}, u32[]{:S(2)}) %collective-permute-start.4) | collective-permute-done | bytes 131104 | tf_op jit(solution)/shard_map/ppermute | solution.py:267
  51.8 0.0 copy-start.6
  51.8 0.0 copy-done.1
  51.8 0.0 copy-done.9
  51.8 0.0 copy-done.4
  51.8 0.0 copy-done.2
  51.8 0.0 copy-done.3
  51.8 0.6 copy-done.6
  52.5 9.9 %tile_sums.1 = bf16[16,128,128]{2,1,0:T(8,128)(2,1)S(1)} custom-call(s32[4]{0:T(128)S(1)} %pad_add_fusion.1.here_ref, s32[8]{0:T(128)S(1)} %bitcast.67, s32[8]{0:T(128)S(1)} %bitcast.70, f32[64]{0:T(128)S(1)} %copy-done.9, bf16[16,208,128]{2,1,0:T(8,128)(2,1)S(1)} %bitcast.59, bf16[24,64,128]{2,1,0:T(8,128)(2,1)S(1)} %bitcast.63, ...), custom_call_target="tpu_custom_call" | custom-call | tf_op jit(solution)/shard_map/tile_sums/pallas_call | solution.py:151
  62.3 14.6 %all_to_all.15.parts_ref = bf16[8,2,128,128]{3,2,1,0:T(8,128)(2,1)S(1)} all-to-all(bf16[8,2,128,128]{3,2,1,0:T(8,128)(2,1)S(1)} %bitcast.64), channel_id=1, replica_groups=mesh['za'=4,'zb'=2,'ya'=2,'yb'=2,'x'=4,'yhi'=2,'core'=2] {'x','core'}, dimensions={0} | all-to-all | bytes 1048576 | tf_op jit(solution)/shard_map/all_to_all | solution.py:300
  77.0 0.0 copy-start
  77.0 0.0 copy-start.5
  77.0 0.7 far_sums.1
  77.7 0.0 copy-start.8
  77.7 6.0 %collective-permute-start.6 = (bf16[3,128,128]{2,1,0:T(8,128)(2,1)S(1)}, bf16[3,128,128]{2,1,0:T(8,128)(2,1)S(1)}, u32[]{:S(2)}, u32[]{:S(2)}) collective-permute-start(bf16[3,128,128]{2,1,0:T(8,128)(2,1)S(1)} %far_sums.1), channel_id=1, source_target_pairs={{0,2},{2,0},{1,3},{3,1},{4,6},{6,4},{5,7},{7,5},{8,10},{10,8},{9,1... | collective-permute-start | bytes 294920 | tf_op jit(solution)/shard_map/ppermute | solution.py:267
  83.7 0.0 copy-done
  83.7 0.0 copy-done.5
  83.7 0.0 copy-done.8
  83.7 0.8 own_sums.1
  84.5 5.3 %collective-permute-done.6.got_ref = bf16[3,128,128]{2,1,0:T(8,128)(2,1)S(1)} collective-permute-done((bf16[3,128,128]{2,1,0:T(8,128)(2,1)S(1)}, bf16[3,128,128]{2,1,0:T(8,128)(2,1)S(1)}, u32[]{:S(2)}, u32[]{:S(2)}) %collective-permute-start.6) | collective-permute-done | bytes 98336 | tf_op jit(solution)/shard_map/ppermute | solution.py:267
  89.9 0.7 finish.1
  (6 shorter events, 0.1 us)
Async XLA Ops:
  2.0 12.5 %copy-start.11 = (bf16[208,128]{1,0:T(8,128)(2,1)S(1)}, bf16[208,128]{1,0:T(8,128)(2,1)}, u32[]{:S(2)}) copy-start(bf16[208,128]{1,0:T(8,128)(2,1)} %get-tuple-element.12) | copy-start | bytes 159748
  2.0 28.5 %all-to-all-start.1 = ((bf16[8,3,64,128]{3,2,1,0:T(8,128)(2,1)}), bf16[8,3,64,128]{3,2,1,0:T(8,128)(2,1)S(1)}, u32[]{:S(2)}, u32[]{:S(2)}) async-start(bf16[8,3,64,128]{3,2,1,0:T(8,128)(2,1)} %get-tuple-element.14), calls=%async_computation.1 | async-start | bytes 786432 | tf_op jit(solution)/shard_map/all_to_all | solution.py:281
  14.5 5.1 %copy-start.7 = (s32[1,1,8]{2,1,0:T(1,128)S(1)}, s32[1,1,8]{2,1,0:T(1,128)}, u32[]{:S(2)}) copy-start(s32[1,1,8]{2,1,0:T(1,128)} %param.13) | copy-start | bytes 100
  14.5 13.8 %collective-permute-start = (bf16[208,128]{1,0:T(8,128)(2,1)S(1)}, bf16[208,128]{1,0:T(8,128)(2,1)S(1)}, u32[]{:S(2)}, u32[]{:S(2)}) collective-permute-start(bf16[208,128]{1,0:T(8,128)(2,1)S(1)} %copy-done.11), channel_id=1, source_target_pairs={{0,2},{2,0},{1,3},{3,1},{4,6},{6,4},{5,7},{7,5},{8,10},{10,8},{9,1... | collective-permute-start | bytes 159752 | tf_op jit(solution)/shard_map/ppermute | solution.py:267
  19.5 5.4 %collective-permute-start.1 = (s32[8]{0:T(128)S(1)}, s32[8]{0:T(128)S(1)}, u32[]{:S(2)}, u32[]{:S(2)}) collective-permute-start(s32[8]{0:T(128)S(1)} %bitcast.68), channel_id=1, source_target_pairs={{0,64},{64,0},{1,65},{65,1},{2,66},{66,2},{3,67},{67,3},{4,68},{68... | collective-permute-start | bytes 104 | tf_op jit(solution)/shard_map/ppermute | solution.py:267
  25.0 9.9 %collective-permute-start.3 = (s32[2,8]{1,0:T(2,128)S(1)}, s32[2,8]{1,0:T(2,128)S(1)}, u32[]{:S(2)}, u32[]{:S(2)}) collective-permute-start(s32[2,8]{1,0:T(2,128)S(1)} %pad_add_fusion), channel_id=1, source_target_pairs={{0,16},{16,0},{1,17},{17,1},{2,18},{18,2},{3,19},{19,3},{4,20},{20... | collective-permute-start | bytes 200 | tf_op jit(solution)/shard_map/ppermute | solution.py:267
  28.2 0.6 copy-start.10
  30.5 18.2 %all-to-all-start = ((bf16[8,2,208,128]{3,2,1,0:T(8,128)(2,1)}), bf16[8,2,208,128]{3,2,1,0:T(8,128)(2,1)S(1)}, u32[]{:S(2)}, u32[]{:S(2)}) async-start(bf16[8,2,208,128]{3,2,1,0:T(8,128)(2,1)} %pair.1), calls=%async_computation | async-start | bytes 1703936 | tf_op jit(solution)/shard_map/all_to_all | solution.py:285
  35.6 16.2 %copy-start.1 = (bf16[1,1,8,128,128]{4,3,2,1,0:T(8,128)(2,1)S(1)}, bf16[1,1,8,128,128]{4,3,2,1,0:T(8,128)(2,1)}, u32[]{:S(2)}) copy-start(bf16[1,1,8,128,128]{4,3,2,1,0:T(8,128)(2,1)} %param.11) | copy-start | bytes 786436
  36.1 15.7 %copy-start.9 = (f32[64]{0:T(128)S(1)}, f32[64]{0:T(128)}, u32[]{:S(2)}) copy-start(f32[64]{0:T(128)} %gain_ref.1) | copy-start | bytes 772
  36.7 12.0 %collective-permute-start.2 = (bf16[8,64,128]{2,1,0:T(8,128)(2,1)S(1)}, bf16[8,64,128]{2,1,0:T(8,128)(2,1)S(1)}, u32[]{:S(2)}, u32[]{:S(2)}) collective-permute-start(bf16[8,64,128]{2,1,0:T(8,128)(2,1)S(1)} %gather_fusion), channel_id=1, source_target_pairs={{0,64},{64,0},{1,65},{65,1},{2,66},{66,2},{3,67},{67,3},{4,68},{68... | collective-permute-start | bytes 393224 | tf_op jit(solution)/shard_map/ppermute | solution.py:267
  40.1 8.6 %collective-permute-start.5 = (bf16[8,64,128]{2,1,0:T(8,128)(2,1)S(1)}, bf16[8,64,128]{2,1,0:T(8,128)(2,1)S(1)}, u32[]{:S(2)}, u32[]{:S(2)}) collective-permute-start(bf16[8,64,128]{2,1,0:T(8,128)(2,1)S(1)} %gather_fusion.2), channel_id=1, source_target_pairs={{0,80},{16,64},{64,16},{80,0},{1,81},{17,65},{65,17},{81,1},{2,82}... | collective-permute-start | bytes 393224 | tf_op jit(solution)/shard_map/ppermute | solution.py:267
  44.6 7.2 %collective-permute-start.4 = (bf16[8,64,128]{2,1,0:T(8,128)(2,1)S(1)}, bf16[8,64,128]{2,1,0:T(8,128)(2,1)S(1)}, u32[]{:S(2)}, u32[]{:S(2)}) collective-permute-start(bf16[8,64,128]{2,1,0:T(8,128)(2,1)S(1)} %gather_fusion.1), channel_id=1, source_target_pairs={{0,16},{16,0},{1,17},{17,1},{2,18},{18,2},{3,19},{19,3},{4,20},{20... | collective-permute-start | bytes 393224 | tf_op jit(solution)/shard_map/ppermute | solution.py:267
  46.5 5.3 %copy-start.4 = (bf16[64,64]{1,0:T(8,128)(2,1)S(1)}, bf16[64,64]{1,0:T(8,128)(2,1)}, u32[]{:S(2)}) copy-start(bf16[64,64]{1,0:T(8,128)(2,1)} %wb_ref.1) | copy-start | bytes 24580
  46.5 5.3 %copy-start.2 = (bf16[64,64]{1,0:T(8,128)(2,1)S(1)}, bf16[64,64]{1,0:T(8,128)(2,1)}, u32[]{:S(2)}) copy-start(bf16[64,64]{1,0:T(8,128)(2,1)} %wd_ref.1) | copy-start | bytes 24580
  46.5 5.3 %copy-start.3 = (bf16[64,64]{1,0:T(8,128)(2,1)S(1)}, bf16[64,64]{1,0:T(8,128)(2,1)}, u32[]{:S(2)}) copy-start(bf16[64,64]{1,0:T(8,128)(2,1)} %we_ref.1) | copy-start | bytes 24580
  51.8 0.7 copy-start.6
  77.0 6.8 %copy-start = (bf16[64,384]{1,0:T(8,128)(2,1)S(1)}, bf16[64,384]{1,0:T(8,128)(2,1)}, u32[]{:S(2)}) copy-start(bf16[64,384]{1,0:T(8,128)(2,1)} %x_ref.5) | copy-start | bytes 147460
  77.0 6.8 %copy-start.5 = (bf16[64,64]{1,0:T(8,128)(2,1)S(1)}, bf16[64,64]{1,0:T(8,128)(2,1)}, u32[]{:S(2)}) copy-start(bf16[64,64]{1,0:T(8,128)(2,1)} %wa_ref.1) | copy-start | bytes 24580
  77.7 6.0 %copy-start.8 = (f32[64]{0:T(128)S(1)}, f32[64]{0:T(128)}, u32[]{:S(2)}) copy-start(f32[64]{0:T(128)} %param.19) | copy-start | bytes 772
  77.7 12.2 %collective-permute-start.6 = (bf16[3,128,128]{2,1,0:T(8,128)(2,1)S(1)}, bf16[3,128,128]{2,1,0:T(8,128)(2,1)S(1)}, u32[]{:S(2)}, u32[]{:S(2)}) collective-permute-start(bf16[3,128,128]{2,1,0:T(8,128)(2,1)S(1)} %far_sums.1), channel_id=1, source_target_pairs={{0,2},{2,0},{1,3},{3,1},{4,6},{6,4},{5,7},{7,5},{8,10},{10,8},{9,1... | collective-permute-start | bytes 294920 | tf_op jit(solution)/shard_map/ppermute | solution.py:267

commit v6 on v5

--- a/solution.py
+++ b/solution.py
@@ -11,31 +11,26 @@
 GROUP = 8
 CHUNK = 128
 BAND = 16
-
-
-def pack_kernel(rows_ref, x_ref, shard_ref, spread_ref, both_ref):
+HERE = 4
+
+
+def pack_kernel(rows_ref, x_ref, shard_ref, spread_ref):
     width, shard = x_ref.shape
     block_len = spread_ref.shape[3]
     n_tiles = rows_ref.shape[0]
+    for k in range(shard // block_len):
+        block = x_ref[:, k * block_len:(k + 1) * block_len]
+        shard_ref[k * width:(k + 1) * width, :] = block
+        for n in range(spread_ref.shape[0]):
+            spread_ref[n, k] = block
     sub = lax.broadcasted_iota(jnp.int32, (BAND, block_len), 0)
     band = jnp.full((BAND, block_len), -1, jnp.int32)
     for t in range(n_tiles):
         band = jnp.where(sub == t, rows_ref[t], band)
-    band = band.astype(jnp.float32).astype(shard_ref.dtype)
-    for k in range(shard // block_len):
-        block = x_ref[:, k * block_len:(k + 1) * block_len]
-        at = slice(k * width, (k + 1) * width)
-        shard_ref[at, :] = block
-        for n in range(spread_ref.shape[0]):
-            spread_ref[n, k] = block
-        for n in range(both_ref.shape[0]):
-            both_ref[n, 0, at, :] = block
-    shard_ref[shard // block_len * width:, :] = band
-    for n in range(both_ref.shape[0]):
-        both_ref[n, 0, shard // block_len * width:, :] = band
-
-
-def pack(rows, x, block_len, copies, pairs):
+    shard_ref[shard // block_len * width:, :] = band.astype(jnp.float32).astype(shard_ref.dtype)
+
+
+def pack(rows, x, block_len, copies):
     width, shard = x.shape
     n_blocks = shard // block_len
     vmem = pl.BlockSpec(memory_space=pltpu.VMEM)
@@ -44,37 +39,39 @@
         out_shape=(
             jax.ShapeDtypeStruct((n_blocks * width + BAND, block_len), x.dtype),
             jax.ShapeDtypeStruct((copies, n_blocks, width, block_len), x.dtype),
-            jax.ShapeDtypeStruct((pairs, 2, n_blocks * width + BAND, block_len), x.dtype),
         ),
         in_specs=[pl.BlockSpec(memory_space=pltpu.SMEM), vmem],
-        out_specs=(vmem, vmem, vmem),
+        out_specs=(vmem, vmem),
         name="pack",
     )(rows, x)
 
 
-def pair_kernel(partner_ref, half_ref, out_ref, sem):
-    del half_ref
-    copies = [pltpu.make_async_copy(partner_ref, out_ref.at[n, 1], sem.at[n]) for n in range(out_ref.shape[0])]
+def pair_kernel(own_ref, partner_ref, out_ref, sem):
+    copies = [
+        pltpu.make_async_copy(ref, out_ref.at[n, k], sem.at[n, k])
+        for n in range(out_ref.shape[0])
+        for k, ref in enumerate((own_ref, partner_ref))
+    ]
     for copy in copies:
         copy.start()
     for copy in copies:
         copy.wait()
 
 
-def pair(partner, half):
-    anywhere = pl.BlockSpec(memory_space=pl.ANY)
+def pair(own, partner, copies):
+    vmem = pl.BlockSpec(memory_space=pltpu.VMEM)
     return pl.pallas_call(
         pair_kernel,
-        out_shape=jax.ShapeDtypeStruct(half.shape, half.dtype),
-        in_specs=[pl.BlockSpec(memory_space=pltpu.VMEM), anywhere],
-        out_specs=anywhere,
-        scratch_shapes=[pltpu.SemaphoreType.DMA((half.shape[0],))],
-        input_output_aliases={1: 0},
+        out_shape=jax.ShapeDtypeStruct((copies, 2) + own.shape, own.dtype),
+        in_specs=[vmem, vmem],
+        out_specs=pl.BlockSpec(memory_space=pl.ANY),
+        scratch_shapes=[pltpu.SemaphoreType.DMA((copies, 2))],
+        compiler_params=pltpu.CompilerParams(vmem_limit_bytes=32 * 1024 * 1024),
         name="pair",
-    )(partner, half)
-
-
-def tiles_kernel(here_ref, tile_rows_ref, tile_cols_ref, gain_ref, rows_ref, own_ref, got_z_ref, got_y_ref, got_zy_ref, w_ref, wd_ref, we_ref, wb_ref,
+    )(own, partner)
+
+
+def tiles_kernel(here_ref, gain_ref, rows_ref, own_ref, got_z_ref, got_y_ref, got_zy_ref, w_ref, wd_ref, we_ref, wb_ref,
                  out_ref, acc, x_scr, d_scr, e_scr, w_scr, lhs_scr, rep_scr):
     n_tiles, block_len, _ = w_ref.shape
     width = wd_ref.shape[0]
@@ -94,12 +91,12 @@
 
     for t in range(n_tiles):
         at = slice(t * block_len, (t + 1) * block_len)
-        owner, block = tile_rows_ref[t] // n_blocks, tile_rows_ref[t] % n_blocks
+        owner, block = here_ref[HERE + t] // n_blocks, here_ref[HERE + t] % n_blocks
         panel = (owner // 4 * 2 + owner % 2) * 2 + ((owner // 2 % 2) ^ here_ref[2])
         x_scr[0, :, at] = rows_ref[panel, pl.ds(pl.multiple_of(block * width, width), width), :]
-        owner = tile_cols_ref[t] // n_blocks
-        source = ((owner // 4 % 2) ^ here_ref[0]) * 2 + ((owner % 2) ^ here_ref[1])
-        place = (owner // 8 * 2 + owner // 2 % 2) * n_blocks + tile_cols_ref[t] % n_blocks
+        owner = here_ref[HERE + n_tiles + t] // n_blocks
+        source = ((owner // 2 % 2) ^ here_ref[0]) * 2 + ((owner % 2) ^ here_ref[1])
+        place = (owner // 4) * n_blocks + here_ref[HERE + n_tiles + t] % n_blocks
         for k, ref in enumerate((own_ref, got_y_ref, got_z_ref, got_zy_ref)):
             @pl.when(source == k)
             def _(ref=ref, at=at, t=t, k=k):
@@ -121,7 +118,7 @@
                 lhs_scr[t, c, g] = jnp.concatenate([b_rep[g * GROUP:(g + 1) * GROUP] * own, own], axis=0).astype(bf16)
 
     def tile(t, _):
-        owner = tile_rows_ref[t] // n_blocks
+        owner = here_ref[HERE + t] // n_blocks
         slot = (owner // 4 * 2 + owner % 2) * 2 + ((owner // 2 % 2) ^ here_ref[2])
         for c in range(n_chunks):
             at = slice(c * CHUNK, (c + 1) * CHUNK)
@@ -142,7 +139,7 @@
     out_ref[...] = (half * acc[...]).astype(out_ref.dtype)
 
 
-def tile_sums(here, tile_rows, tile_cols, gain, rows, own, got_z, got_y, got_zy, w, wd, we, wb, n_owners):
+def tile_sums(here, gain, rows, own, got_z, got_y, got_zy, w, wd, we, wb, n_owners):
     n_tiles, block_len, _ = w.shape
     width = wd.shape[0]
     smem = pl.BlockSpec(memory_space=pltpu.SMEM)
@@ -151,7 +148,7 @@
     return pl.pallas_call(
         tiles_kernel,
         out_shape=jax.ShapeDtypeStruct((n_owners, 2 * width, block_len), jnp.bfloat16),
-        in_specs=[smem] * 4 + [vmem] * 9,
+        in_specs=[smem] * 2 + [vmem] * 9,
         out_specs=vmem,
         scratch_shapes=[
             pltpu.VMEM((n_owners, 2 * width, block_len), jnp.float32),
@@ -164,7 +161,7 @@
         ],
         compiler_params=pltpu.CompilerParams(vmem_limit_bytes=32 * 1024 * 1024),
         name="tile_sums",
-    )(here, tile_rows, tile_cols, gain, rows, own, got_z, got_y, got_zy, w, wd, we, wb)
+    )(here, gain, rows, own, got_z, got_y, got_zy, w, wd, we, wb)
 
 
 def sums_kernel(flipped, here_ref, parts_ref, band_ref, out_ref):
@@ -274,28 +271,29 @@
     n_za, n_x = lax.axis_size("za"), lax.axis_size("x")
     rows, cols = tile_rows.reshape(-1), tile_cols.reshape(-1)
     tiles = edge_values.reshape(n_tiles, block_len, block_len)
-    here = jnp.stack([lax.axis_index(a) for a in ("zb", "yb", "yhi", SRC)]).astype(jnp.int32)
-
-    shard_rows, copies, both = pack(rows, x, block_len, n_za * 2, n_x * 2)
+    here = jnp.stack([lax.axis_index(a) for a in ("ya", "yb", "yhi", SRC)]).astype(jnp.int32)
+    here = jnp.concatenate([here, rows, cols])
+
+    shard_rows, copies = pack(rows, x, block_len, n_za * 2)
     partner = flip(shard_rows, ("yhi",))
-    held = lax.all_to_all(copies, ("za", "ya"), 0, 0).reshape(-1, width, block_len)
+    held = lax.all_to_all(copies, ("za", "zb"), 0, 0).reshape(-1, width, block_len)
     asked, _ = lax.optimization_barrier((cols, shard_rows))
-    cols_z = flip(asked, ("zb",))
+    cols_z = flip(asked, ("ya",))
     cols_y, cols_zy = flip(jnp.stack([asked, cols_z]), ("yb",))
-    row_panel = lax.all_to_all(pair(partner, both), ("x", "core"), 0, 0)
+    row_panel = lax.all_to_all(pair(shard_rows, partner, n_x * 2), ("x", "core"), 0, 0)
     row_panel = row_panel.reshape(n_x * 4, -1, block_len)
 
     def pick(names):
         owner = names // n_blocks
-        place = (owner // 8 * 2 + owner // 2 % 2) * n_blocks + names % n_blocks
+        place = (owner // 4) * n_blocks + names % n_blocks
         return held.at[place].get(mode="promise_in_bounds")
 
-    got_z = flip(pick(cols_z), ("zb",))
+    got_z = flip(pick(cols_z), ("ya",))
     got_y = flip(pick(cols_y), ("yb",))
-    got_zy = flip(pick(cols_zy), ("zb", "yb"))
+    got_zy = flip(pick(cols_zy), ("ya", "yb"))
 
     parts = tile_sums(
-        here, rows, cols, edge_gain, row_panel, held, got_z, got_y, got_zy, tiles, wd, we, wb, n_x * 4
+        here, edge_gain, row_panel, held, got_z, got_y, got_zy, tiles, wd, we, wb, n_x * 4
     )
     parts = lax.all_to_all(parts.reshape((n_x * 2, 2) + parts.shape[1:]), ("x", "core"), 0, 0)
     panel = row_panel.reshape((n_x * 2, 2) + row_panel.shape[1:])

time: 91.2 us -> 90.8 us (level)
  waiting for transfers between devices: 12.6 us -> 16.7 us
  starting transfers between devices: 44.2 us -> 41.4 us
  Pallas kernels: 15.8 us -> 14.7 us
    ppermute x7, waiting for transfers between devices: 10.5 us -> 14.2 us  [flip(): return lax.ppermute(x, axes, [(i, i ^ last) for i in range(last + 1)])]
    all_to_all x2, starting transfers between devices: 16.8 us -> 14.8 us  [the longest x1 10.4 us: local(): lax.all_to_all(copies, ('za', 'zb'), 0, 0).reshape(-1, width, block_len)]
  transfers between devices with their start and end apart: 9 -> 9, of which waited for: 4 -> 4; matrix products, arithmetic and copies ran while one was open for 2% -> 2% of each run, Pallas kernels for 3% -> 2%
where the time goes in v6:
time: 90.8 us; the launch traced here: 90.3 us
  starting transfers between devices  41.4 us (46%)
  waiting for transfers between devices  16.7 us (18%)
  Pallas kernels  14.7 us (16%)
  blocking collectives  14.6 us (16%)
  local copies, waits for them, and re-layouts  2.49 us (3%)
    ppermute x7, starting transfers between devices, flip(): return lax.ppermute(x, axes, [(i, i ^ last) for i in range(last + 1)])  26.6 us
    all_to_all x1, blocking collectives, local(): lax.all_to_all(parts.reshape((n_x * 2, 2) + parts.shape[1:]), ('x', 'core...  14.6 us
    ppermute x7, waiting for transfers between devices, flip(): return lax.ppermute(x, axes, [(i, i ^ last) for i in range(last + 1)])  14.2 us
    all_to_all x1, starting transfers between devices, local(): lax.all_to_all(copies, ('za', 'zb'), 0, 0).reshape(-1, width, block_len)  10.4 us
    pallas_call x1, Pallas kernels, tile_sums(): pl.pallas_call(tiles_kernel, out_shape=jax.ShapeDtypeStruct((n_owners, 2...  9.79 us
    all_to_all x1, starting transfers between devices, local(): lax.all_to_all(pair(shard_rows, partner, n_x * 2), ('x', 'core'), 0, 0)  4.31 us
    all_to_all x1, waiting for transfers between devices, local(): lax.all_to_all(pair(shard_rows, partner, n_x * 2), ('x', 'core'), 0, 0)  2.48 us
  transfers between devices with their start and end apart: 9, of which 4 were waited for; matrix products, arithmetic and copies ran while one was open for 2% of the time, Pallas kernels for 2%

profile of v6, /device:TPU:8, one launch (start us, length us, event | category | flops | bytes accessed | tf_op | source)
XLA Modules:
  0.0 90.3 jit_solution(4926532980068654115)
XLA Ops:
  0.0 1.6 %pack.1 = (bf16[208,128]{1,0:T(8,128)(2,1)}, bf16[8,3,64,128]{3,2,1,0:T(8,128)(2,1)}) custom-call(s32[8]{0:T(128)} %bitcast.67, bf16[64,384]{1,0:T(8,128)(2,1)} %x_ref.5), custom_call_target="tpu_custom_call" | custom-call | tf_op jit(solution)/shard_map/pack/pallas_call | solution.py:37
  1.6 0.0 copy-start.2
  1.7 10.4 %all-to-all-start.1 = ((bf16[8,3,64,128]{3,2,1,0:T(8,128)(2,1)}), bf16[8,3,64,128]{3,2,1,0:T(8,128)(2,1)S(1)}, u32[]{:S(2)}, u32[]{:S(2)}) async-start(bf16[8,3,64,128]{3,2,1,0:T(8,128)(2,1)} %get-tuple-element.12), calls=%async_computation.1 | async-start | bytes 786432 | tf_op jit(solution)/shard_map/all_to_all | solution.py:279
  12.1 0.0 copy-done.2
  12.1 0.0 copy-start.10
  12.1 6.8 %collective-permute-start = (bf16[208,128]{1,0:T(8,128)(2,1)S(1)}, bf16[208,128]{1,0:T(8,128)(2,1)S(1)}, u32[]{:S(2)}, u32[]{:S(2)}) collective-permute-start(bf16[208,128]{1,0:T(8,128)(2,1)S(1)} %copy-done.2), channel_id=1, source_target_pairs={{0,2},{2,0},{1,3},{3,1},{4,6},{6,4},{5,7},{7,5},{8,10},{10,8},{9,1... | collective-permute-start | bytes 159752 | tf_op jit(solution)/shard_map/ppermute | solution.py:264
  19.0 0.0 copy-done.10
  19.0 2.7 %collective-permute-start.1 = (s32[8]{0:T(128)S(1)}, s32[8]{0:T(128)S(1)}, u32[]{:S(2)}, u32[]{:S(2)}) collective-permute-start(s32[8]{0:T(128)S(1)} %bitcast.69), channel_id=1, source_target_pairs={{0,32},{32,0},{1,33},{33,1},{2,34},{34,2},{3,35},{35,3},{4,36},{36... | collective-permute-start | bytes 104 | tf_op jit(solution)/shard_map/ppermute | solution.py:264
  21.7 3.6 %collective-permute-done.1 = s32[8]{0:T(128)S(1)} collective-permute-done((s32[8]{0:T(128)S(1)}, s32[8]{0:T(128)S(1)}, u32[]{:S(2)}, u32[]{:S(2)}) %collective-permute-start.1) | collective-permute-done | bytes 64 | tf_op jit(solution)/shard_map/ppermute | solution.py:264
  25.3 3.3 %collective-permute-start.3 = (s32[2,8]{1,0:T(2,128)S(1)}, s32[2,8]{1,0:T(2,128)S(1)}, u32[]{:S(2)}, u32[]{:S(2)}) collective-permute-start(s32[2,8]{1,0:T(2,128)S(1)} %pad_add_fusion), channel_id=1, source_target_pairs={{0,16},{16,0},{1,17},{17,1},{2,18},{18,2},{3,19},{19,3},{4,20},{20... | collective-permute-start | bytes 200 | tf_op jit(solution)/shard_map/ppermute | solution.py:264
  28.6 0.0 collective-permute-done.partner_ref
  28.6 1.1 %pair.1 = bf16[8,2,208,128]{3,2,1,0:T(8,128)(2,1)} custom-call(bf16[208,128]{1,0:T(8,128)(2,1)S(1)} %copy-done.2, bf16[208,128]{1,0:T(8,128)(2,1)S(1)} %collective-permute-done.partner_ref), custom_call_target="tpu_custom_call" | custom-call | tf_op jit(solution)/shard_map/pair/pallas_call | solution.py:63
  29.6 0.0 all-to-all-done.1
  29.7 4.3 %all-to-all-start = ((bf16[8,2,208,128]{3,2,1,0:T(8,128)(2,1)}), bf16[8,2,208,128]{3,2,1,0:T(8,128)(2,1)S(1)}, u32[]{:S(2)}, u32[]{:S(2)}) async-start(bf16[8,2,208,128]{3,2,1,0:T(8,128)(2,1)} %pair.1), calls=%async_computation | async-start | bytes 1703936 | tf_op jit(solution)/shard_map/all_to_all | solution.py:283
  34.0 0.0 collective-permute-done.3
  34.1 0.6 gather_fusion
  34.7 0.0 copy-start.1
  34.7 2.8 %collective-permute-start.2 = (bf16[8,64,128]{2,1,0:T(8,128)(2,1)S(1)}, bf16[8,64,128]{2,1,0:T(8,128)(2,1)S(1)}, u32[]{:S(2)}, u32[]{:S(2)}) collective-permute-start(bf16[8,64,128]{2,1,0:T(8,128)(2,1)S(1)} %gather_fusion), channel_id=1, source_target_pairs={{0,32},{32,0},{1,33},{33,1},{2,34},{34,2},{3,35},{35,3},{4,36},{36... | collective-permute-start | bytes 393224 | tf_op jit(solution)/shard_map/ppermute | solution.py:264
  37.5 0.6 gather_fusion.1
  38.1 2.6 %collective-permute-start.4 = (bf16[8,64,128]{2,1,0:T(8,128)(2,1)S(1)}, bf16[8,64,128]{2,1,0:T(8,128)(2,1)S(1)}, u32[]{:S(2)}, u32[]{:S(2)}) collective-permute-start(bf16[8,64,128]{2,1,0:T(8,128)(2,1)S(1)} %gather_fusion.1), channel_id=1, source_target_pairs={{0,16},{16,0},{1,17},{17,1},{2,18},{18,2},{3,19},{19,3},{4,20},{20... | collective-permute-start | bytes 393224 | tf_op jit(solution)/shard_map/ppermute | solution.py:264
  40.7 0.0 copy-start.9
  40.7 0.6 gather_fusion.2
  41.3 3.9 %collective-permute-start.5 = (bf16[8,64,128]{2,1,0:T(8,128)(2,1)S(1)}, bf16[8,64,128]{2,1,0:T(8,128)(2,1)S(1)}, u32[]{:S(2)}, u32[]{:S(2)}) collective-permute-start(bf16[8,64,128]{2,1,0:T(8,128)(2,1)S(1)} %gather_fusion.2), channel_id=1, source_target_pairs={{0,48},{16,32},{32,16},{48,0},{1,49},{17,33},{33,17},{49,1},{2,50}... | collective-permute-start | bytes 393224 | tf_op jit(solution)/shard_map/ppermute | solution.py:264
  45.2 0.0 copy-start.5
  45.2 0.0 copy-start.4
  45.2 0.0 copy-start.3
  45.3 0.0 copy-done.9
  45.3 0.1 concatenate.3.here_ref
  45.4 2.5 %all-to-all-done.band_ref = bf16[8,2,208,128]{3,2,1,0:T(8,128)(2,1)S(1)} async-done(((bf16[8,2,208,128]{3,2,1,0:T(8,128)(2,1)}), bf16[8,2,208,128]{3,2,1,0:T(8,128)(2,1)S(1)}, u32[]{:S(2)}, u32[]{:S(2)}) %all-to-all-start) | async-done | bytes 852000 | tf_op jit(solution)/shard_map/all_to_all | solution.py:283
  47.8 0.0 collective-permute-done.2.got_z_ref
  47.8 0.0 collective-permute-done.4.got_y_ref
  47.8 3.8 %collective-permute-done.5.got_zy_ref = bf16[8,64,128]{2,1,0:T(8,128)(2,1)S(1)} collective-permute-done((bf16[8,64,128]{2,1,0:T(8,128)(2,1)S(1)}, bf16[8,64,128]{2,1,0:T(8,128)(2,1)S(1)}, u32[]{:S(2)}, u32[]{:S(2)}) %collective-permute-start.5) | collective-permute-done | bytes 131104 | tf_op jit(solution)/shard_map/ppermute | solution.py:264
  51.6 0.0 copy-start.8
  51.6 0.0 copy-done.1
  51.6 0.0 copy-done.5
  51.6 0.0 copy-done.4
  51.6 0.0 copy-done.3
  51.6 0.6 copy-done.8
  52.3 9.8 %tile_sums.1 = bf16[16,128,128]{2,1,0:T(8,128)(2,1)S(1)} custom-call(s32[20]{0:T(128)S(1)} %concatenate.3.here_ref, f32[64]{0:T(128)S(1)} %copy-done.8, bf16[16,208,128]{2,1,0:T(8,128)(2,1)S(1)} %bitcast.59, bf16[24,64,128]{2,1,0:T(8,128)(2,1)S(1)} %bitcast.63, bf16[8,64,128]{2,1,0:T(8,128)(2,1)S(1)} %collective-permute-done.2.got_z_ref, ...), custom_call_target="tpu_custom_call" | custom-call | tf_op jit(solution)/shard_map/tile_sums/pallas_call | solution.py:148
  62.1 14.6 %all_to_all.15.parts_ref = bf16[8,2,128,128]{3,2,1,0:T(8,128)(2,1)S(1)} all-to-all(bf16[8,2,128,128]{3,2,1,0:T(8,128)(2,1)S(1)} %bitcast.64), channel_id=1, replica_groups=mesh['za'=4,'zb'=2,'ya'=2,'yb'=2,'x'=4,'yhi'=2,'core'=2] {'x','core'}, dimensions={0} | all-to-all | bytes 1048576 | tf_op jit(solution)/shard_map/all_to_all | solution.py:298
  76.7 0.0 copy-start
  76.7 0.0 copy-start.6
  76.7 0.7 far_sums.1
  77.5 0.0 copy-start.7
  77.5 4.5 %collective-permute-start.6 = (bf16[3,128,128]{2,1,0:T(8,128)(2,1)S(1)}, bf16[3,128,128]{2,1,0:T(8,128)(2,1)S(1)}, u32[]{:S(2)}, u32[]{:S(2)}) collective-permute-start(bf16[3,128,128]{2,1,0:T(8,128)(2,1)S(1)} %far_sums.1), channel_id=1, source_target_pairs={{0,2},{2,0},{1,3},{3,1},{4,6},{6,4},{5,7},{7,5},{8,10},{10,8},{9,1... | collective-permute-start | bytes 294920 | tf_op jit(solution)/shard_map/ppermute | solution.py:264
  81.9 0.0 copy-done
  82.0 0.0 copy-done.6
  82.0 0.0 copy-done.7
  82.0 0.8 own_sums.1
  82.8 6.8 %collective-permute-done.6.got_ref = bf16[3,128,128]{2,1,0:T(8,128)(2,1)S(1)} collective-permute-done((bf16[3,128,128]{2,1,0:T(8,128)(2,1)S(1)}, bf16[3,128,128]{2,1,0:T(8,128)(2,1)S(1)}, u32[]{:S(2)}, u32[]{:S(2)}) %collective-permute-start.6) | collective-permute-done | bytes 98336 | tf_op jit(solution)/shard_map/ppermute | solution.py:264
  89.6 0.7 finish.1
  (6 shorter events, 0.1 us)
Async XLA Ops:
  1.6 10.5 %copy-start.2 = (bf16[208,128]{1,0:T(8,128)(2,1)S(1)}, bf16[208,128]{1,0:T(8,128)(2,1)}, u32[]{:S(2)}) copy-start(bf16[208,128]{1,0:T(8,128)(2,1)} %get-tuple-element.11.own_ref) | copy-start | bytes 159748
  1.7 28.0 %all-to-all-start.1 = ((bf16[8,3,64,128]{3,2,1,0:T(8,128)(2,1)}), bf16[8,3,64,128]{3,2,1,0:T(8,128)(2,1)S(1)}, u32[]{:S(2)}, u32[]{:S(2)}) async-start(bf16[8,3,64,128]{3,2,1,0:T(8,128)(2,1)} %get-tuple-element.12), calls=%async_computation.1 | async-start | bytes 786432 | tf_op jit(solution)/shard_map/all_to_all | solution.py:279
  12.1 6.9 %copy-start.10 = (s32[1,1,8]{2,1,0:T(1,128)S(1)}, s32[1,1,8]{2,1,0:T(1,128)}, u32[]{:S(2)}) copy-start(s32[1,1,8]{2,1,0:T(1,128)} %param.13) | copy-start | bytes 100
  12.1 16.5 %collective-permute-start = (bf16[208,128]{1,0:T(8,128)(2,1)S(1)}, bf16[208,128]{1,0:T(8,128)(2,1)S(1)}, u32[]{:S(2)}, u32[]{:S(2)}) collective-permute-start(bf16[208,128]{1,0:T(8,128)(2,1)S(1)} %copy-done.2), channel_id=1, source_target_pairs={{0,2},{2,0},{1,3},{3,1},{4,6},{6,4},{5,7},{7,5},{8,10},{10,8},{9,1... | collective-permute-start | bytes 159752 | tf_op jit(solution)/shard_map/ppermute | solution.py:264
  19.0 6.3 %collective-permute-start.1 = (s32[8]{0:T(128)S(1)}, s32[8]{0:T(128)S(1)}, u32[]{:S(2)}, u32[]{:S(2)}) collective-permute-start(s32[8]{0:T(128)S(1)} %bitcast.69), channel_id=1, source_target_pairs={{0,32},{32,0},{1,33},{33,1},{2,34},{34,2},{3,35},{35,3},{4,36},{36... | collective-permute-start | bytes 104 | tf_op jit(solution)/shard_map/ppermute | solution.py:264
  25.3 8.7 %collective-permute-start.3 = (s32[2,8]{1,0:T(2,128)S(1)}, s32[2,8]{1,0:T(2,128)S(1)}, u32[]{:S(2)}, u32[]{:S(2)}) collective-permute-start(s32[2,8]{1,0:T(2,128)S(1)} %pad_add_fusion), channel_id=1, source_target_pairs={{0,16},{16,0},{1,17},{17,1},{2,18},{18,2},{3,19},{19,3},{4,20},{20... | collective-permute-start | bytes 200 | tf_op jit(solution)/shard_map/ppermute | solution.py:264
  29.7 18.2 %all-to-all-start = ((bf16[8,2,208,128]{3,2,1,0:T(8,128)(2,1)}), bf16[8,2,208,128]{3,2,1,0:T(8,128)(2,1)S(1)}, u32[]{:S(2)}, u32[]{:S(2)}) async-start(bf16[8,2,208,128]{3,2,1,0:T(8,128)(2,1)} %pair.1), calls=%async_computation | async-start | bytes 1703936 | tf_op jit(solution)/shard_map/all_to_all | solution.py:283
  34.7 17.0 %copy-start.1 = (bf16[1,1,8,128,128]{4,3,2,1,0:T(8,128)(2,1)S(1)}, bf16[1,1,8,128,128]{4,3,2,1,0:T(8,128)(2,1)}, u32[]{:S(2)}) copy-start(bf16[1,1,8,128,128]{4,3,2,1,0:T(8,128)(2,1)} %param.11) | copy-start | bytes 786436
  34.7 13.2 %collective-permute-start.2 = (bf16[8,64,128]{2,1,0:T(8,128)(2,1)S(1)}, bf16[8,64,128]{2,1,0:T(8,128)(2,1)S(1)}, u32[]{:S(2)}, u32[]{:S(2)}) collective-permute-start(bf16[8,64,128]{2,1,0:T(8,128)(2,1)S(1)} %gather_fusion), channel_id=1, source_target_pairs={{0,32},{32,0},{1,33},{33,1},{2,34},{34,2},{3,35},{35,3},{4,36},{36... | collective-permute-start | bytes 393224 | tf_op jit(solution)/shard_map/ppermute | solution.py:264
  38.1 9.7 %collective-permute-start.4 = (bf16[8,64,128]{2,1,0:T(8,128)(2,1)S(1)}, bf16[8,64,128]{2,1,0:T(8,128)(2,1)S(1)}, u32[]{:S(2)}, u32[]{:S(2)}) collective-permute-start(bf16[8,64,128]{2,1,0:T(8,128)(2,1)S(1)} %gather_fusion.1), channel_id=1, source_target_pairs={{0,16},{16,0},{1,17},{17,1},{2,18},{18,2},{3,19},{19,3},{4,20},{20... | collective-permute-start | bytes 393224 | tf_op jit(solution)/shard_map/ppermute | solution.py:264
  40.7 4.6 %copy-start.9 = (s32[1,1,8]{2,1,0:T(1,128)S(1)}, s32[1,1,8]{2,1,0:T(1,128)}, u32[]{:S(2)}) copy-start(s32[1,1,8]{2,1,0:T(1,128)} %param.12) | copy-start | bytes 100
  41.3 10.3 %collective-permute-start.5 = (bf16[8,64,128]{2,1,0:T(8,128)(2,1)S(1)}, bf16[8,64,128]{2,1,0:T(8,128)(2,1)S(1)}, u32[]{:S(2)}, u32[]{:S(2)}) collective-permute-start(bf16[8,64,128]{2,1,0:T(8,128)(2,1)S(1)} %gather_fusion.2), channel_id=1, source_target_pairs={{0,48},{16,32},{32,16},{48,0},{1,49},{17,33},{33,17},{49,1},{2,50}... | collective-permute-start | bytes 393224 | tf_op jit(solution)/shard_map/ppermute | solution.py:264
  45.2 6.4 %copy-start.5 = (bf16[64,64]{1,0:T(8,128)(2,1)S(1)}, bf16[64,64]{1,0:T(8,128)(2,1)}, u32[]{:S(2)}) copy-start(bf16[64,64]{1,0:T(8,128)(2,1)} %wb_ref.1) | copy-start | bytes 24580
  45.2 6.4 %copy-start.4 = (bf16[64,64]{1,0:T(8,128)(2,1)S(1)}, bf16[64,64]{1,0:T(8,128)(2,1)}, u32[]{:S(2)}) copy-start(bf16[64,64]{1,0:T(8,128)(2,1)} %we_ref.1) | copy-start | bytes 24580
  45.2 6.4 %copy-start.3 = (bf16[64,64]{1,0:T(8,128)(2,1)S(1)}, bf16[64,64]{1,0:T(8,128)(2,1)}, u32[]{:S(2)}) copy-start(bf16[64,64]{1,0:T(8,128)(2,1)} %wd_ref.1) | copy-start | bytes 24580
  51.6 0.7 copy-start.8
  76.7 5.2 %copy-start = (bf16[64,384]{1,0:T(8,128)(2,1)S(1)}, bf16[64,384]{1,0:T(8,128)(2,1)}, u32[]{:S(2)}) copy-start(bf16[64,384]{1,0:T(8,128)(2,1)} %x_ref.5) | copy-start | bytes 147460
  76.7 5.2 %copy-start.6 = (bf16[64,64]{1,0:T(8,128)(2,1)S(1)}, bf16[64,64]{1,0:T(8,128)(2,1)}, u32[]{:S(2)}) copy-start(bf16[64,64]{1,0:T(8,128)(2,1)} %wa_ref.1) | copy-start | bytes 24580
  77.5 4.5 %copy-start.7 = (f32[64]{0:T(128)S(1)}, f32[64]{0:T(128)}, u32[]{:S(2)}) copy-start(f32[64]{0:T(128)} %param.19) | copy-start | bytes 772
  77.5 12.1 %collective-permute-start.6 = (bf16[3,128,128]{2,1,0:T(8,128)(2,1)S(1)}, bf16[3,128,128]{2,1,0:T(8,128)(2,1)S(1)}, u32[]{:S(2)}, u32[]{:S(2)}) collective-permute-start(bf16[3,128,128]{2,1,0:T(8,128)(2,1)S(1)} %far_sums.1), channel_id=1, source_target_pairs={{0,2},{2,0},{1,3},{3,1},{4,6},{6,4},{5,7},{7,5},{8,10},{10,8},{9,1... | collective-permute-start | bytes 294920 | tf_op jit(solution)/shard_map/ppermute | solution.py:264

commit v7 on v6

--- a/solution.py
+++ b/solution.py
@@ -129,7 +129,7 @@
                     f = g * GROUP + k
                     gain = gain_ref[f]
                     w_f = w_scr[t, (gain < 0).astype(jnp.int32), at, :]
-                    p = jnp.maximum(jnp.abs(gain), 1e-30) * w_f + d_scr[t, f:f + 1, :] + e_c[:, f:f + 1].astype(f32)
+                    p = jnp.abs(gain) * w_f + d_scr[t, f:f + 1, :] + e_c[:, f:f + 1].astype(f32)
                     gates.append((jnp.tanh(p) + 1.0).astype(bf16))
                 sums = jnp.dot(lhs_scr[t, c, g], jnp.concatenate(gates, axis=0), preferred_element_type=f32)
                 acc[slot, g * GROUP:(g + 1) * GROUP, :] += sums[:GROUP]
@@ -273,13 +273,14 @@
     tiles = edge_values.reshape(n_tiles, block_len, block_len)
     here = jnp.stack([lax.axis_index(a) for a in ("ya", "yb", "yhi", SRC)]).astype(jnp.int32)
     here = jnp.concatenate([here, rows, cols])
+    gain = jnp.where(edge_gain < 0, jnp.minimum(edge_gain, -1e-30), jnp.maximum(edge_gain, 1e-30))
 
     shard_rows, copies = pack(rows, x, block_len, n_za * 2)
     partner = flip(shard_rows, ("yhi",))
     held = lax.all_to_all(copies, ("za", "zb"), 0, 0).reshape(-1, width, block_len)
     asked, _ = lax.optimization_barrier((cols, shard_rows))
-    cols_z = flip(asked, ("ya",))
-    cols_y, cols_zy = flip(jnp.stack([asked, cols_z]), ("yb",))
+    cols_y = flip(asked, ("yb",))
+    cols_z, cols_zy = flip(jnp.stack([asked, cols_y]), ("ya",))
     row_panel = lax.all_to_all(pair(shard_rows, partner, n_x * 2), ("x", "core"), 0, 0)
     row_panel = row_panel.reshape(n_x * 4, -1, block_len)
 
@@ -293,7 +294,7 @@
     got_zy = flip(pick(cols_zy), ("ya", "yb"))
 
     parts = tile_sums(
-        here, edge_gain, row_panel, held, got_z, got_y, got_zy, tiles, wd, we, wb, n_x * 4
+        here, gain, row_panel, held, got_z, got_y, got_zy, tiles, wd, we, wb, n_x * 4
     )
     parts = lax.all_to_all(parts.reshape((n_x * 2, 2) + parts.shape[1:]), ("x", "core"), 0, 0)
     panel = row_panel.reshape((n_x * 2, 2) + row_panel.shape[1:])

time: 90.8 us -> 89.8 us (0.989)
  transfers between devices with their start and end apart: 9 -> 9, of which waited for: 4 -> 5; matrix products, arithmetic and copies ran while one was open for 2% -> 2% of each run, Pallas kernels for 2% -> 2%
where the time goes in v7:
time: 89.8 us; the launch traced here: 89.3 us
  starting transfers between devices  41 us (46%)
  waiting for transfers between devices  16 us (18%)
  Pallas kernels  14.7 us (16%)
  blocking collectives  14.6 us (16%)
  local copies, waits for them, and re-layouts  2.5 us (3%)
    ppermute x7, starting transfers between devices, flip(): return lax.ppermute(x, axes, [(i, i ^ last) for i in range(last + 1)])  26.2 us
    all_to_all x1, blocking collectives, local(): lax.all_to_all(parts.reshape((n_x * 2, 2) + parts.shape[1:]), ('x', 'core...  14.6 us
    ppermute x7, waiting for transfers between devices, flip(): return lax.ppermute(x, axes, [(i, i ^ last) for i in range(last + 1)])  13.4 us
    all_to_all x1, starting transfers between devices, local(): lax.all_to_all(copies, ('za', 'zb'), 0, 0).reshape(-1, width, block_len)  10.4 us
    pallas_call x1, Pallas kernels, tile_sums(): pl.pallas_call(tiles_kernel, out_shape=jax.ShapeDtypeStruct((n_owners, 2...  9.8 us
    all_to_all x1, starting transfers between devices, local(): lax.all_to_all(pair(shard_rows, partner, n_x * 2), ('x', 'core'), 0, 0)  4.31 us
    all_to_all x1, waiting for transfers between devices, local(): lax.all_to_all(pair(shard_rows, partner, n_x * 2), ('x', 'core'), 0, 0)  2.59 us
  transfers between devices with their start and end apart: 9, of which 5 were waited for; matrix products, arithmetic and copies ran while one was open for 2% of the time, Pallas kernels for 2%

profile of v7, /device:TPU:8, one launch (start us, length us, event | category | flops | bytes accessed | tf_op | source)
XLA Modules:
  0.0 89.3 jit_solution(9311598820412927568)
XLA Ops:
  0.0 1.6 %pack.1 = (bf16[208,128]{1,0:T(8,128)(2,1)}, bf16[8,3,64,128]{3,2,1,0:T(8,128)(2,1)}) custom-call(s32[8]{0:T(128)} %bitcast.67, bf16[64,384]{1,0:T(8,128)(2,1)} %x_ref.5), custom_call_target="tpu_custom_call" | custom-call | tf_op jit(solution)/shard_map/pack/pallas_call | solution.py:37
  1.6 0.0 copy-start.2
  1.7 10.4 %all-to-all-start.1 = ((bf16[8,3,64,128]{3,2,1,0:T(8,128)(2,1)}), bf16[8,3,64,128]{3,2,1,0:T(8,128)(2,1)S(1)}, u32[]{:S(2)}, u32[]{:S(2)}) async-start(bf16[8,3,64,128]{3,2,1,0:T(8,128)(2,1)} %get-tuple-element.12), calls=%async_computation.1 | async-start | bytes 786432 | tf_op jit(solution)/shard_map/all_to_all | solution.py:280
  12.1 0.0 copy-done.2
  12.1 0.0 copy-start.9
  12.1 6.8 %collective-permute-start = (bf16[208,128]{1,0:T(8,128)(2,1)S(1)}, bf16[208,128]{1,0:T(8,128)(2,1)S(1)}, u32[]{:S(2)}, u32[]{:S(2)}) collective-permute-start(bf16[208,128]{1,0:T(8,128)(2,1)S(1)} %copy-done.2), channel_id=1, source_target_pairs={{0,2},{2,0},{1,3},{3,1},{4,6},{6,4},{5,7},{7,5},{8,10},{10,8},{9,1... | collective-permute-start | bytes 159752 | tf_op jit(solution)/shard_map/ppermute | solution.py:264
  19.0 0.0 copy-done.9
  19.0 3.3 %collective-permute-start.1 = (s32[8]{0:T(128)S(1)}, s32[8]{0:T(128)S(1)}, u32[]{:S(2)}, u32[]{:S(2)}) collective-permute-start(s32[8]{0:T(128)S(1)} %bitcast.69), channel_id=1, source_target_pairs={{0,16},{16,0},{1,17},{17,1},{2,18},{18,2},{3,19},{19,3},{4,20},{20... | collective-permute-start | bytes 104 | tf_op jit(solution)/shard_map/ppermute | solution.py:264
  22.2 0.0 copy-start.8
  22.3 0.6 copy-done.8
  22.9 0.1 concatenate.3.here_ref
  23.0 1.4 %collective-permute-done.1 = s32[8]{0:T(128)S(1)} collective-permute-done((s32[8]{0:T(128)S(1)}, s32[8]{0:T(128)S(1)}, u32[]{:S(2)}, u32[]{:S(2)}) %collective-permute-start.1) | collective-permute-done | bytes 64 | tf_op jit(solution)/shard_map/ppermute | solution.py:264
  24.4 2.8 %collective-permute-start.2 = (s32[2,8]{1,0:T(2,128)S(1)}, s32[2,8]{1,0:T(2,128)S(1)}, u32[]{:S(2)}, u32[]{:S(2)}) collective-permute-start(s32[2,8]{1,0:T(2,128)S(1)} %pad_add_fusion), channel_id=1, source_target_pairs={{0,32},{32,0},{1,33},{33,1},{2,34},{34,2},{3,35},{35,3},{4,36},{36... | collective-permute-start | bytes 200 | tf_op jit(solution)/shard_map/ppermute | solution.py:264
  27.2 0.0 collective-permute-done.partner_ref
  27.2 1.1 %pair.1 = bf16[8,2,208,128]{3,2,1,0:T(8,128)(2,1)} custom-call(bf16[208,128]{1,0:T(8,128)(2,1)S(1)} %copy-done.2, bf16[208,128]{1,0:T(8,128)(2,1)S(1)} %collective-permute-done.partner_ref), custom_call_target="tpu_custom_call" | custom-call | tf_op jit(solution)/shard_map/pair/pallas_call | solution.py:63
  28.3 0.0 all-to-all-done.1
  28.3 4.3 %all-to-all-start = ((bf16[8,2,208,128]{3,2,1,0:T(8,128)(2,1)}), bf16[8,2,208,128]{3,2,1,0:T(8,128)(2,1)S(1)}, u32[]{:S(2)}, u32[]{:S(2)}) async-start(bf16[8,2,208,128]{3,2,1,0:T(8,128)(2,1)} %pair.1), calls=%async_computation | async-start | bytes 1703936 | tf_op jit(solution)/shard_map/all_to_all | solution.py:284
  32.6 0.0 collective-permute-done.2
  32.7 0.6 gather_fusion
  33.3 0.0 copy-start.1
  33.3 4.1 %collective-permute-start.3 = (bf16[8,64,128]{2,1,0:T(8,128)(2,1)S(1)}, bf16[8,64,128]{2,1,0:T(8,128)(2,1)S(1)}, u32[]{:S(2)}, u32[]{:S(2)}) collective-permute-start(bf16[8,64,128]{2,1,0:T(8,128)(2,1)S(1)} %gather_fusion), channel_id=1, source_target_pairs={{0,32},{32,0},{1,33},{33,1},{2,34},{34,2},{3,35},{35,3},{4,36},{36... | collective-permute-start | bytes 393224 | tf_op jit(solution)/shard_map/ppermute | solution.py:264
  37.4 0.6 gather_fusion.1
  38.0 0.0 copy-start.10
  38.0 3.3 %collective-permute-start.4 = (bf16[8,64,128]{2,1,0:T(8,128)(2,1)S(1)}, bf16[8,64,128]{2,1,0:T(8,128)(2,1)S(1)}, u32[]{:S(2)}, u32[]{:S(2)}) collective-permute-start(bf16[8,64,128]{2,1,0:T(8,128)(2,1)S(1)} %gather_fusion.1), channel_id=1, source_target_pairs={{0,16},{16,0},{1,17},{17,1},{2,18},{18,2},{3,19},{19,3},{4,20},{20... | collective-permute-start | bytes 393224 | tf_op jit(solution)/shard_map/ppermute | solution.py:264
  41.3 0.0 copy-start.3
  41.3 0.0 copy-start.4
  41.3 0.0 copy-start.5
  41.3 0.6 gather_fusion.2
  41.9 2.0 %collective-permute-start.5 = (bf16[8,64,128]{2,1,0:T(8,128)(2,1)S(1)}, bf16[8,64,128]{2,1,0:T(8,128)(2,1)S(1)}, u32[]{:S(2)}, u32[]{:S(2)}) collective-permute-start(bf16[8,64,128]{2,1,0:T(8,128)(2,1)S(1)} %gather_fusion.2), channel_id=1, source_target_pairs={{0,48},{16,32},{32,16},{48,0},{1,49},{17,33},{33,17},{49,1},{2,50}... | collective-permute-start | bytes 393224 | tf_op jit(solution)/shard_map/ppermute | solution.py:264
  43.9 0.0 copy-done.10
  43.9 2.6 %all-to-all-done.band_ref = bf16[8,2,208,128]{3,2,1,0:T(8,128)(2,1)S(1)} async-done(((bf16[8,2,208,128]{3,2,1,0:T(8,128)(2,1)}), bf16[8,2,208,128]{3,2,1,0:T(8,128)(2,1)S(1)}, u32[]{:S(2)}, u32[]{:S(2)}) %all-to-all-start) | async-done | bytes 852000 | tf_op jit(solution)/shard_map/all_to_all | solution.py:284
  46.5 0.0 collective-permute-done.3.got_z_ref
  46.5 0.1 collective-permute-done.4.got_y_ref
  46.6 5.3 %collective-permute-done.5.got_zy_ref = bf16[8,64,128]{2,1,0:T(8,128)(2,1)S(1)} collective-permute-done((bf16[8,64,128]{2,1,0:T(8,128)(2,1)S(1)}, bf16[8,64,128]{2,1,0:T(8,128)(2,1)S(1)}, u32[]{:S(2)}, u32[]{:S(2)}) %collective-permute-start.5) | collective-permute-done | bytes 131104 | tf_op jit(solution)/shard_map/ppermute | solution.py:264
  51.9 0.0 copy-done.1
  51.9 0.0 copy-done.3
  51.9 0.0 copy-done.4
  51.9 0.0 copy-done.5
  51.9 9.8 %tile_sums.1 = bf16[16,128,128]{2,1,0:T(8,128)(2,1)S(1)} custom-call(s32[20]{0:T(128)S(1)} %concatenate.3.here_ref, f32[64]{0:T(128)S(1)} %compare_select_fusion.3.gain_ref, bf16[16,208,128]{2,1,0:T(8,128)(2,1)S(1)} %bitcast.59, bf16[24,64,128]{2,1,0:T(8,128)(2,1)S(1)} %bitcast.63, bf16[8,64,128]{2,1,0:T(8,128)(2,1)S(1)} %collective-permute-done.3.got_z_ref, ...), custom_call_target="tpu_custom_call" | custom-call | tf_op jit(solution)/shard_map/tile_sums/pallas_call | solution.py:148
  61.7 14.6 %all_to_all.15.parts_ref = bf16[8,2,128,128]{3,2,1,0:T(8,128)(2,1)S(1)} all-to-all(bf16[8,2,128,128]{3,2,1,0:T(8,128)(2,1)S(1)} %bitcast.64), channel_id=1, replica_groups=mesh['za'=4,'zb'=2,'ya'=2,'yb'=2,'x'=4,'yhi'=2,'core'=2] {'x','core'}, dimensions={0} | all-to-all | bytes 1048576 | tf_op jit(solution)/shard_map/all_to_all | solution.py:299
  76.4 0.0 copy-start
  76.4 0.0 copy-start.6
  76.4 0.7 far_sums.1
  77.1 0.0 copy-start.7
  77.1 4.0 %collective-permute-start.6 = (bf16[3,128,128]{2,1,0:T(8,128)(2,1)S(1)}, bf16[3,128,128]{2,1,0:T(8,128)(2,1)S(1)}, u32[]{:S(2)}, u32[]{:S(2)}) collective-permute-start(bf16[3,128,128]{2,1,0:T(8,128)(2,1)S(1)} %far_sums.1), channel_id=1, source_target_pairs={{0,2},{2,0},{1,3},{3,1},{4,6},{6,4},{5,7},{7,5},{8,10},{10,8},{9,1... | collective-permute-start | bytes 294920 | tf_op jit(solution)/shard_map/ppermute | solution.py:264
  81.2 0.0 copy-done
  81.2 0.0 copy-done.6
  81.2 0.0 copy-done.7
  81.2 0.8 own_sums.1
  82.0 6.5 %collective-permute-done.6.got_ref = bf16[3,128,128]{2,1,0:T(8,128)(2,1)S(1)} collective-permute-done((bf16[3,128,128]{2,1,0:T(8,128)(2,1)S(1)}, bf16[3,128,128]{2,1,0:T(8,128)(2,1)S(1)}, u32[]{:S(2)}, u32[]{:S(2)}) %collective-permute-start.6) | collective-permute-done | bytes 98336 | tf_op jit(solution)/shard_map/ppermute | solution.py:264
  88.5 0.7 finish.1
  (7 shorter events, 0.1 us)
Async XLA Ops:
  1.6 10.5 %copy-start.2 = (bf16[208,128]{1,0:T(8,128)(2,1)S(1)}, bf16[208,128]{1,0:T(8,128)(2,1)}, u32[]{:S(2)}) copy-start(bf16[208,128]{1,0:T(8,128)(2,1)} %get-tuple-element.11.own_ref) | copy-start | bytes 159748
  1.7 26.6 %all-to-all-start.1 = ((bf16[8,3,64,128]{3,2,1,0:T(8,128)(2,1)}), bf16[8,3,64,128]{3,2,1,0:T(8,128)(2,1)S(1)}, u32[]{:S(2)}, u32[]{:S(2)}) async-start(bf16[8,3,64,128]{3,2,1,0:T(8,128)(2,1)} %get-tuple-element.12), calls=%async_computation.1 | async-start | bytes 786432 | tf_op jit(solution)/shard_map/all_to_all | solution.py:280
  12.1 6.9 %copy-start.9 = (s32[1,1,8]{2,1,0:T(1,128)S(1)}, s32[1,1,8]{2,1,0:T(1,128)}, u32[]{:S(2)}) copy-start(s32[1,1,8]{2,1,0:T(1,128)} %param.13) | copy-start | bytes 100
  12.1 15.1 %collective-permute-start = (bf16[208,128]{1,0:T(8,128)(2,1)S(1)}, bf16[208,128]{1,0:T(8,128)(2,1)S(1)}, u32[]{:S(2)}, u32[]{:S(2)}) collective-permute-start(bf16[208,128]{1,0:T(8,128)(2,1)S(1)} %copy-done.2), channel_id=1, source_target_pairs={{0,2},{2,0},{1,3},{3,1},{4,6},{6,4},{5,7},{7,5},{8,10},{10,8},{9,1... | collective-permute-start | bytes 159752 | tf_op jit(solution)/shard_map/ppermute | solution.py:264
  19.0 5.4 %collective-permute-start.1 = (s32[8]{0:T(128)S(1)}, s32[8]{0:T(128)S(1)}, u32[]{:S(2)}, u32[]{:S(2)}) collective-permute-start(s32[8]{0:T(128)S(1)} %bitcast.69), channel_id=1, source_target_pairs={{0,16},{16,0},{1,17},{17,1},{2,18},{18,2},{3,19},{19,3},{4,20},{20... | collective-permute-start | bytes 104 | tf_op jit(solution)/shard_map/ppermute | solution.py:264
  22.2 0.7 copy-start.8
  24.4 8.2 %collective-permute-start.2 = (s32[2,8]{1,0:T(2,128)S(1)}, s32[2,8]{1,0:T(2,128)S(1)}, u32[]{:S(2)}, u32[]{:S(2)}) collective-permute-start(s32[2,8]{1,0:T(2,128)S(1)} %pad_add_fusion), channel_id=1, source_target_pairs={{0,32},{32,0},{1,33},{33,1},{2,34},{34,2},{3,35},{35,3},{4,36},{36... | collective-permute-start | bytes 200 | tf_op jit(solution)/shard_map/ppermute | solution.py:264
  28.3 18.2 %all-to-all-start = ((bf16[8,2,208,128]{3,2,1,0:T(8,128)(2,1)}), bf16[8,2,208,128]{3,2,1,0:T(8,128)(2,1)S(1)}, u32[]{:S(2)}, u32[]{:S(2)}) async-start(bf16[8,2,208,128]{3,2,1,0:T(8,128)(2,1)} %pair.1), calls=%async_computation | async-start | bytes 1703936 | tf_op jit(solution)/shard_map/all_to_all | solution.py:284
  33.3 18.7 %copy-start.1 = (bf16[1,1,8,128,128]{4,3,2,1,0:T(8,128)(2,1)S(1)}, bf16[1,1,8,128,128]{4,3,2,1,0:T(8,128)(2,1)}, u32[]{:S(2)}) copy-start(bf16[1,1,8,128,128]{4,3,2,1,0:T(8,128)(2,1)} %param.11) | copy-start | bytes 786436
  33.3 13.2 %collective-permute-start.3 = (bf16[8,64,128]{2,1,0:T(8,128)(2,1)S(1)}, bf16[8,64,128]{2,1,0:T(8,128)(2,1)S(1)}, u32[]{:S(2)}, u32[]{:S(2)}) collective-permute-start(bf16[8,64,128]{2,1,0:T(8,128)(2,1)S(1)} %gather_fusion), channel_id=1, source_target_pairs={{0,32},{32,0},{1,33},{33,1},{2,34},{34,2},{3,35},{35,3},{4,36},{36... | collective-permute-start | bytes 393224 | tf_op jit(solution)/shard_map/ppermute | solution.py:264
  38.0 5.9 %copy-start.10 = (f32[64]{0:T(128)S(1)}, f32[64]{0:T(128)}, u32[]{:S(2)}) copy-start(f32[64]{0:T(128)} %param.18) | copy-start | bytes 772
  38.0 8.6 %collective-permute-start.4 = (bf16[8,64,128]{2,1,0:T(8,128)(2,1)S(1)}, bf16[8,64,128]{2,1,0:T(8,128)(2,1)S(1)}, u32[]{:S(2)}, u32[]{:S(2)}) collective-permute-start(bf16[8,64,128]{2,1,0:T(8,128)(2,1)S(1)} %gather_fusion.1), channel_id=1, source_target_pairs={{0,16},{16,0},{1,17},{17,1},{2,18},{18,2},{3,19},{19,3},{4,20},{20... | collective-permute-start | bytes 393224 | tf_op jit(solution)/shard_map/ppermute | solution.py:264
  41.3 10.7 %copy-start.3 = (bf16[64,64]{1,0:T(8,128)(2,1)S(1)}, bf16[64,64]{1,0:T(8,128)(2,1)}, u32[]{:S(2)}) copy-start(bf16[64,64]{1,0:T(8,128)(2,1)} %wd_ref.1) | copy-start | bytes 24580
  41.3 10.7 %copy-start.4 = (bf16[64,64]{1,0:T(8,128)(2,1)S(1)}, bf16[64,64]{1,0:T(8,128)(2,1)}, u32[]{:S(2)}) copy-start(bf16[64,64]{1,0:T(8,128)(2,1)} %we_ref.1) | copy-start | bytes 24580
  41.3 10.7 %copy-start.5 = (bf16[64,64]{1,0:T(8,128)(2,1)S(1)}, bf16[64,64]{1,0:T(8,128)(2,1)}, u32[]{:S(2)}) copy-start(bf16[64,64]{1,0:T(8,128)(2,1)} %wb_ref.1) | copy-start | bytes 24580
  41.9 10.1 %collective-permute-start.5 = (bf16[8,64,128]{2,1,0:T(8,128)(2,1)S(1)}, bf16[8,64,128]{2,1,0:T(8,128)(2,1)S(1)}, u32[]{:S(2)}, u32[]{:S(2)}) collective-permute-start(bf16[8,64,128]{2,1,0:T(8,128)(2,1)S(1)} %gather_fusion.2), channel_id=1, source_target_pairs={{0,48},{16,32},{32,16},{48,0},{1,49},{17,33},{33,17},{49,1},{2,50}... | collective-permute-start | bytes 393224 | tf_op jit(solution)/shard_map/ppermute | solution.py:264
  76.4 4.8 %copy-start = (bf16[64,384]{1,0:T(8,128)(2,1)S(1)}, bf16[64,384]{1,0:T(8,128)(2,1)}, u32[]{:S(2)}) copy-start(bf16[64,384]{1,0:T(8,128)(2,1)} %x_ref.5) | copy-start | bytes 147460
  76.4 4.8 %copy-start.6 = (bf16[64,64]{1,0:T(8,128)(2,1)S(1)}, bf16[64,64]{1,0:T(8,128)(2,1)}, u32[]{:S(2)}) copy-start(bf16[64,64]{1,0:T(8,128)(2,1)} %wa_ref.1) | copy-start | bytes 24580
  77.1 4.1 %copy-start.7 = (f32[64]{0:T(128)S(1)}, f32[64]{0:T(128)}, u32[]{:S(2)}) copy-start(f32[64]{0:T(128)} %param.19) | copy-start | bytes 772
  77.1 11.4 %collective-permute-start.6 = (bf16[3,128,128]{2,1,0:T(8,128)(2,1)S(1)}, bf16[3,128,128]{2,1,0:T(8,128)(2,1)S(1)}, u32[]{:S(2)}, u32[]{:S(2)}) collective-permute-start(bf16[3,128,128]{2,1,0:T(8,128)(2,1)S(1)} %far_sums.1), channel_id=1, source_target_pairs={{0,2},{2,0},{1,3},{3,1},{4,6},{6,4},{5,7},{7,5},{8,10},{10,8},{9,1... | collective-permute-start | bytes 294920 | tf_op jit(solution)/shard_map/ppermute | solution.py:264
